TPU v7x, 32 devices: a whole 2x2x4 slice. The times are simulated.
32 devices in a mesh: groups: 2 (over x), expert: 16 (over z, y, core).
Axes of the slice: x: 2, y: 2, z: 4, core: 2. Of those that a mesh axis runs over, the one named last changes fastest.
Arguments:
- hidden_in: bfloat16 [256, 6400], P(('groups', 'expert')), parts along dimension 0, may hold values from -6 to 6
- norm_gain: float32 [6400], replicated, may hold values from 0.1 to 1.9
- router: bfloat16 [6400, 2], replicated, may hold values from -0.078125 to 0.078125
- routes: int32 [256, 1], P(('groups', 'expert')), parts along dimension 0, may hold values from 0 to 1; in each aligned block of 8 rows (0 to 7, 8 to 15, ...) at most 6 rows name the same one
- routed_gate_up: bfloat16 [16, 6400, 576], P('expert'), may hold values from -0.078125 to 0.078125
- routed_down: bfloat16 [16, 288, 6400], P('expert'), may hold values from -0.125 to 0.125
Outputs:
- mixed: bfloat16 [256, 6400], P(('groups', 'expert')), parts along dimension 0
There are 2 independent parts, one for each index of `groups`. A program takes and returns all parts, laid end to end along the dimension named above; an argument that names none is the same for every part. Nothing has to cross between parts.
Inputs may be any that keep to these rules, and one draw needn't show every extreme that they name: `routes`: among the rows of one device no expert is named by more than 6 rows, and in every draw some device names one expert exactly 6 times.
All inputs are finite; a program needn't handle non-finite values.
Results may differ from a plain program's by a relative error of at most 0.0049.
Values may be sent and summed in bfloat16 or wider, within the bound.
No kernel may reach another device: no remote copies, remote signals or barrier semaphores. Data moves between devices by JAX's collectives and lax.ppermute only.
A program may use at most 128 MiB of HBM per device.

v0:
```python
import jax
import jax.numpy as jnp
from jax import lax
from jax.sharding import PartitionSpec as P


def rms_norm(hidden_in, norm_gain):
    values = hidden_in.astype(jnp.float32)
    mean_square = jnp.mean(values * values, axis=-1, keepdims=True)
    return (values * lax.rsqrt(mean_square + 1e-06) * norm_gain).astype(jnp.bfloat16)


def expert_rows(sel_rows, gate_up, down_w, column):
    hidden_units = down_w.shape[0]
    lifted = jnp.dot(sel_rows, gate_up, preferred_element_type=jnp.float32)
    act = (jax.nn.silu(lifted[:, :hidden_units]) * lifted[:, hidden_units:]).astype(jnp.bfloat16)
    output = jnp.dot(act, down_w, preferred_element_type=jnp.float32)
    scores = jax.nn.sigmoid(jnp.dot(sel_rows, column, preferred_element_type=jnp.float32))
    return output * scores


def body(hidden_in, norm_gain, router, routes, routed_gate_up, routed_down):
    tok_rows = hidden_in.shape[0]
    width_d = hidden_in.shape[1]
    axis_len = lax.axis_size("expert")
    experts = router.shape[1]
    copies = axis_len // experts
    capacity = max(2, 3 * tok_rows // 4)
    own_expert = lax.axis_index("expert") // copies
    column = lax.dynamic_slice_in_dim(router, own_expert, 1, 1)
    gate_up = routed_gate_up[0]
    down_w = routed_down[0]
    normed = rms_norm(hidden_in, norm_gain)
    one_hot = (routes == jnp.arange(experts, dtype=jnp.int32)[None, :]).astype(jnp.int32)
    slot_rank = jnp.sum(one_hot * (jnp.cumsum(one_hot, axis=0) - 1), axis=1)
    target = routes[:, 0] * capacity + slot_rank
    dispatch = (jnp.arange(experts * capacity, dtype=jnp.int32)[:, None] == target[None, :]).astype(
        jnp.bfloat16
    )
    packed = jnp.dot(dispatch, normed, preferred_element_type=jnp.float32).astype(jnp.bfloat16)
    send_rows = jnp.repeat(packed.reshape(experts, capacity, width_d), copies, axis=0)
    arrived = lax.all_to_all(send_rows, "expert", split_axis=0, concat_axis=0, tiled=True)
    item_count = arrived.shape[1]
    result = expert_rows(arrived.reshape(-1, width_d), gate_up, down_w, column)
    result = result.reshape(axis_len, item_count, width_d)
    returned = lax.all_to_all(
        result.astype(jnp.bfloat16), "expert", split_axis=0, concat_axis=0, tiled=True
    ).astype(result.dtype)
    summed = jnp.sum(returned.reshape(experts, copies, capacity, width_d), axis=1).reshape(
        experts * capacity, width_d
    )
    total = jnp.dot(
        dispatch.astype(jnp.float32).T,
        summed,
        precision=lax.Precision.HIGHEST,
        preferred_element_type=jnp.float32,
    )
    return (hidden_in.astype(jnp.float32) + total).astype(jnp.bfloat16)


def solution(mesh):
    placed = (
        P(("groups", "expert"), None),
        P(),
        P(),
        P(("groups", "expert"), None),
        P("expert", None, None),
        P("expert", None, None),
    )
    return jax.shard_map(
        body, mesh=mesh, in_specs=placed, out_specs=P(("groups", "expert"), None), check_vma=False
    )
```

profile of v0, /device:TPU:0, one launch (start us, length us, event | category | flops | bytes accessed | tf_op | source)
XLA Modules:
  0.0 105.1 jit_solution(1566724386976389454)
XLA Ops:
  0.0 0.0 copy-start
  0.0 1.1 %fusion.9 = f32[8]{0:T(128)S(1)} fusion(bf16[8,6400]{1,0:T(8,128)(2,1)} %param.6), kind=kLoop, calls=%fused_computation.16 | loop fusion | flops 153592 | bytes 102432 | tf_op jit(solution)/shard_map/reduce_sum | solution.py:9
  1.1 0.7 fusion.21
  1.8 0.2 reduce_window_sum.11
  1.9 0.7 select_reduce_fusion
  2.6 0.7 multiply_add_fusion
  3.3 1.1 %convolution_convert_fusion = bf16[12,6400]{1,0:T(8,128)(2,1)S(1)} fusion(bf16[8,6400]{1,0:T(8,128)(2,1)} %param.6, f32[6400]{0:T(1024)} %param.7, f32[8]{0:T(128)S(1)} %add_rsqrt_fusion, s32[8]{0:T(128)S(1)} %multiply_add_fusion), kind=kOutput, calls=%fused_computation.2 | convolution fusion | flops 1510496 | bytes 281664 | tf_op jit(solution)/shard_map/dot_general | solution.py:40
  4.4 0.1 reshape.46
  4.5 1.3 %broadcast_in_dim.2 = bf16[2,8,6,6400]{3,2,1,0:T(8,128)(2,1)} broadcast(bf16[2,6,6400]{2,1,0:T(8,128)(2,1)S(1)} %reshape.46), dimensions={0,2,3} | broadcast | bytes 1382400 | tf_op jit(solution)/shard_map/broadcast_in_dim | solution.py:41
  5.8 7.4 %all-to-all-start = ((bf16[16,6,6400]{2,1,0:T(8,128)(2,1)}), bf16[16,6,6400]{2,1,0:T(8,128)(2,1)S(1)}, u32[]{:S(2)}, u32[]{:S(2)}) async-start(bf16[16,6,6400]{2,1,0:T(8,128)(2,1)} %bitcast.1), calls=%async_computation | async-start | bytes 3276800 | tf_op jit(solution)/shard_map/all_to_all | solution.py:42
  13.2 33.1 %all-to-all-done = bf16[16,6,6400]{2,1,0:T(8,128)(2,1)S(1)} async-done(((bf16[16,6,6400]{2,1,0:T(8,128)(2,1)}), bf16[16,6,6400]{2,1,0:T(8,128)(2,1)S(1)}, u32[]{:S(2)}, u32[]{:S(2)}) %all-to-all-start) | async-done | bytes 1228832 | tf_op jit(solution)/shard_map/all_to_all | solution.py:42
  46.3 0.5 reshape.48
  46.8 0.0 copy-start.1
  46.8 5.6 %fusion.2 = f32[96,576]{1,0:T(8,128)S(1)} fusion(bf16[96,6400]{1,0:T(8,128)(2,1)S(1)} %reshape.48, bf16[1,6400,576]{1,2,0:T(8,128)(2,1)} %param.10), kind=kOutput, calls=%fused_computation.5 | convolution fusion | flops 707788800 | bytes 8822784 | tf_op jit(solution)/shard_map/dot_general | solution.py:15
  52.4 0.0 copy-done
  52.4 0.4 fusion.8
  52.8 0.0 copy-done.1
  52.8 1.0 fusion
  53.8 0.5 convert_element_type.34
  54.3 48.9 %all_to_all.10 = bf16[16,6,6400]{2,1,0:T(8,128)(2,1)S(1)} all-to-all(bf16[16,6,6400]{2,1,0:T(8,128)(2,1)S(1)} %convert_element_type.34), channel_id=1, replica_groups=mesh['groups'=2,'expert'=16] {'expert'}, dimensions={0} | all-to-all | bytes 2457600 | tf_op jit(solution)/shard_map/all_to_all | solution.py:46
  103.3 0.0 copy-start.2
  103.3 0.3 convert_reduce_fusion
  103.6 0.5 copy-done.2
  104.2 0.9 fusion.1
  (2 shorter events, 0.1 us)
Async XLA Ops:
  0.0 52.4 %copy-start = (bf16[6400,2]{0,1:T(2,128)(2,1)S(1)}, bf16[6400,2]{0,1:T(2,128)(2,1)}, u32[]{:S(2)}) copy-start(bf16[6400,2]{0,1:T(2,128)(2,1)} %param.8) | copy-start | bytes 76804
  5.8 40.5 %all-to-all-start = ((bf16[16,6,6400]{2,1,0:T(8,128)(2,1)}), bf16[16,6,6400]{2,1,0:T(8,128)(2,1)S(1)}, u32[]{:S(2)}, u32[]{:S(2)}) async-start(bf16[16,6,6400]{2,1,0:T(8,128)(2,1)} %bitcast.1), calls=%async_computation | async-start | bytes 3276800 | tf_op jit(solution)/shard_map/all_to_all | solution.py:42
  46.8 6.1 %copy-start.1 = (bf16[1,288,6400]{2,1,0:T(8,128)(2,1)S(1)}, bf16[1,288,6400]{2,1,0:T(8,128)(2,1)}, u32[]{:S(2)}) copy-start(bf16[1,288,6400]{2,1,0:T(8,128)(2,1)} %param.11) | copy-start | bytes 11059204
  103.3 0.9 copy-start.2
where the time goes:
time: 105 us
  blocking collectives  48.9 us (47%)
  waiting for transfers between devices  33.1 us (32%)
  matrix products  9.15 us (9%)
  starting transfers between devices  7.39 us (7%)
  other arithmetic  3.57 us (3%)
  local copies, waits for them, and re-layouts  2.87 us (3%)
    all_to_all x1, blocking collectives, body(): lax.all_to_all(result.astype(jnp.bfloat16), 'expert', split_axis=0, conca...  48.9 us
    all_to_all x1, waiting for transfers between devices, body(): lax.all_to_all(send_rows, 'expert', split_axis=0, concat_axis=0, tiled=True)  33.1 us
    all_to_all x1, starting transfers between devices, body(): lax.all_to_all(send_rows, 'expert', split_axis=0, concat_axis=0, tiled=True)  7.39 us
    dot_general x1, matrix products, expert_rows(): lifted = jnp.dot(sel_rows, gate_up, preferred_element_type=jnp.float32)  5.64 us
  transfers between devices with their start and end apart: 1, of which 1 were waited for; matrix products, arithmetic and copies ran while one was open for 0% of the time, Pallas kernels for 0%

commit v1 on v0

v1 whole, which is shorter than its diff:
```python
import jax
import jax.numpy as jnp
from jax import lax
from jax.sharding import PartitionSpec as P


def rms_norm(hidden_in, norm_gain):
    values = hidden_in.astype(jnp.float32)
    mean_square = jnp.mean(values * values, axis=-1, keepdims=True)
    return (values * lax.rsqrt(mean_square + 1e-06) * norm_gain).astype(jnp.bfloat16)


def expert_rows(rows, norm_gain, gate_up, down_w, column):
    normed = rms_norm(rows, norm_gain)
    hidden_units = down_w.shape[0]
    lifted = jnp.dot(normed, gate_up, preferred_element_type=jnp.float32)
    act = (jax.nn.silu(lifted[:, :hidden_units]) * lifted[:, hidden_units:]).astype(jnp.bfloat16)
    output = jnp.dot(act, down_w, preferred_element_type=jnp.float32)
    scores = jax.nn.sigmoid(jnp.dot(normed, column, preferred_element_type=jnp.float32))
    return output * scores


def steps_of(axis_len, copies):
    masks = []
    mask = 2
    while mask < copies:
        masks.append(mask)
        mask *= 2
    steps = []
    for first, second in zip(masks, masks[::-1]):
        steps.append([(i, i ^ (second if i % 2 else first)) for i in range(axis_len)])
    return steps


def flip(axis_len, mask):
    return [(i, i ^ mask) for i in range(axis_len)]


def body(hidden_in, norm_gain, router, routes, routed_gate_up, routed_down):
    axis_len = lax.axis_size("expert")
    experts = router.shape[1]
    copies = axis_len // experts
    own_expert = lax.axis_index("expert") // copies
    column = lax.dynamic_slice_in_dim(router, own_expert, 1, 1)
    steps = steps_of(axis_len, copies)

    def swap(block, pairs):
        return lax.ppermute(block, "expert", pairs)

    blocks = hidden_in[None]
    mask = copies
    while mask < axis_len:
        blocks = jnp.concatenate([blocks, swap(blocks, flip(axis_len, mask))], axis=0)
        mask *= 2
    for pairs in steps:
        blocks = jnp.concatenate([blocks, swap(blocks, pairs)], axis=0)
    blocks = jnp.concatenate([blocks, swap(blocks, flip(axis_len, 1))], axis=0)
    rows = blocks.reshape(-1, blocks.shape[-1])
    result = expert_rows(rows, norm_gain, routed_gate_up[0], routed_down[0], column)
    part = result.reshape(blocks.shape)

    def fold(part, pairs):
        half = part.shape[0] // 2
        arrived = swap(part[half:].astype(jnp.bfloat16), pairs)
        return part[:half] + arrived.astype(jnp.float32)

    part = fold(part, flip(axis_len, 1))
    for pairs in steps[::-1]:
        part = fold(part, pairs)
    chosen = part[0]
    for k in range(1, experts):
        arrived = swap(part[k].astype(jnp.bfloat16), flip(axis_len, copies * k))
        other = jnp.bitwise_xor(own_expert, k)
        chosen = jnp.where(routes == other, arrived.astype(jnp.float32), chosen)
    return (hidden_in.astype(jnp.float32) + chosen).astype(jnp.bfloat16)


def solution(mesh):
    placed = (
        P(("groups", "expert"), None),
        P(),
        P(),
        P(("groups", "expert"), None),
        P("expert", None, None),
        P("expert", None, None),
    )
    return jax.shard_map(
        body, mesh=mesh, in_specs=placed, out_specs=P(("groups", "expert"), None), check_vma=False
    )
```

time: 105 us -> 59.5 us (0.57)
  blocking collectives: 48.9 us -> 0 us
  starting transfers between devices: 7.39 us -> 11.4 us
  waiting for transfers between devices: 33.1 us -> 36.1 us
  matrix products: 9.15 us -> 7.1 us
  local copies, waits for them, and re-layouts: 2.87 us -> 1.2 us
    all_to_all x1 -> x0, blocking collectives: 48.9 us -> none  [body(): lax.all_to_all(result.astype(jnp.bfloat16), 'expert', split_axis=0, conca...]
    ppermute x0 -> x8, waiting for transfers between devices: none -> 36.1 us  [swap(): return lax.ppermute(block, 'expert', pairs)]
    all_to_all x1 -> x0, waiting for transfers between devices: 33.1 us -> none  [body(): lax.all_to_all(send_rows, 'expert', split_axis=0, concat_axis=0, tiled=True)]
    ppermute x0 -> x8, starting transfers between devices: none -> 11.4 us  [swap(): return lax.ppermute(block, 'expert', pairs)]
    all_to_all x1 -> x0, starting transfers between devices: 7.39 us -> none  [body(): lax.all_to_all(send_rows, 'expert', split_axis=0, concat_axis=0, tiled=True)]
    dot_general x4 -> x2, matrix products: 8.13 us -> 5.95 us  [the longest x1 5.37 us: expert_rows(): lifted = jnp.dot(normed, gate_up, preferred_element_type=jnp.float32)]
    concatenate x0 -> x3, other arithmetic: none -> 1.93 us  [the longest x2 1.02 us: body(): blocks = jnp.concatenate([blocks, swap(blocks, pairs)], axis=0)]
    broadcast_in_dim x1 -> x0, local copies, waits for them, and re-layouts: 1.3 us -> none  [body(): jnp.repeat(packed.reshape(experts, capacity, width_d), copies, axis=0)]
  transfers between devices with their start and end apart: 1 -> 8, of which waited for: 1 -> 8; matrix products, arithmetic and copies ran while one was open for 0% -> 2% of each run, Pallas kernels for 0% -> 0%
where the time goes in v1:
time: 59.5 us; the launch traced here: 59.3 us
  waiting for transfers between devices  36.1 us (61%)
  starting transfers between devices  11.4 us (19%)
  matrix products  7.1 us (12%)
  other arithmetic  3.36 us (6%)
  local copies, waits for them, and re-layouts  1.2 us (2%)
    ppermute x8, waiting for transfers between devices, swap(): return lax.ppermute(block, 'expert', pairs)  36.1 us
    ppermute x8, starting transfers between devices, swap(): return lax.ppermute(block, 'expert', pairs)  11.4 us
    dot_general x1, matrix products, expert_rows(): lifted = jnp.dot(normed, gate_up, preferred_element_type=jnp.float32)  5.37 us
  transfers between devices with their start and end apart: 8, of which 8 were waited for; matrix products, arithmetic and copies ran while one was open for 2% of the time, Pallas kernels for 0%

profile of v1, /device:TPU:0, one launch (start us, length us, event | category | flops | bytes accessed | tf_op | source)
XLA Modules:
  0.0 59.3 jit_solution(14174825371844167492)
XLA Ops:
  0.0 0.0 copy-start
  0.0 4.0 %collective-permute-start = (bf16[1,8,6400]{2,1,0:T(8,128)(2,1)}, bf16[1,8,6400]{2,1,0:T(8,128)(2,1)S(1)}, u32[]{:S(2)}, u32[]{:S(2)}) collective-permute-start(bf16[1,8,6400]{2,1,0:T(8,128)(2,1)} %bitcast.50), channel_id=1, source_target_pairs={{0,8},{1,9},{2,10},{3,11},{4,12},{5,13},{6,14},{7,15},{8,0},{9,1},... | collective-permute-start | bytes 307208 | tf_op jit(solution)/shard_map/ppermute | solution.py:48
  4.0 5.3 %collective-permute-done = bf16[1,8,6400]{2,1,0:T(8,128)(2,1)S(1)} collective-permute-done((bf16[1,8,6400]{2,1,0:T(8,128)(2,1)}, bf16[1,8,6400]{2,1,0:T(8,128)(2,1)S(1)}, u32[]{:S(2)}, u32[]{:S(2)}) %collective-permute-start) | collective-permute-done | bytes 102432 | tf_op jit(solution)/shard_map/ppermute | solution.py:48
  9.4 0.9 %pad_maximum_fusion.2 = bf16[2,8,6400]{2,1,0:T(8,128)(2,1)S(1)} fusion(bf16[1,8,6400]{2,1,0:T(8,128)(2,1)S(1)} %collective-permute-done, bf16[1,8,6400]{2,1,0:T(8,128)(2,1)} %bitcast.51), kind=kLoop, calls=%fused_computation.31 | loop fusion | flops 102400 | bytes 409600 | tf_op jit(solution)/shard_map/concatenate | solution.py:53
  10.3 1.6 %collective-permute-start.1 = (bf16[2,8,6400]{2,1,0:T(8,128)(2,1)S(1)}, bf16[2,8,6400]{2,1,0:T(8,128)(2,1)S(1)}, u32[]{:S(2)}, u32[]{:S(2)}) collective-permute-start(bf16[2,8,6400]{2,1,0:T(8,128)(2,1)S(1)} %pad_maximum_fusion.2), channel_id=1, source_target_pairs={{0,2},{1,5},{2,0},{3,7},{4,6},{5,1},{6,4},{7,3},{8,10},{9,13},{10,... | collective-permute-start | bytes 614408 | tf_op jit(solution)/shard_map/ppermute | solution.py:48
  11.9 0.9 %constant_dynamic-update-slice_fusion.4 = bf16[16,8,6400]{2,1,0:T(8,128)(2,1)S(1)} fusion(bf16[8,6400]{1,0:T(8,128)(2,1)} %param.6), kind=kLoop, calls=%fused_computation.41 | loop fusion | bytes 204800
  12.8 3.3 %collective-permute-done.1 = bf16[2,8,6400]{2,1,0:T(8,128)(2,1)S(1)} collective-permute-done((bf16[2,8,6400]{2,1,0:T(8,128)(2,1)S(1)}, bf16[2,8,6400]{2,1,0:T(8,128)(2,1)S(1)}, u32[]{:S(2)}, u32[]{:S(2)}) %collective-permute-start.1) | collective-permute-done | bytes 204832 | tf_op jit(solution)/shard_map/ppermute | solution.py:48
  16.1 0.9 %pad_maximum_fusion.1 = bf16[4,8,6400]{2,1,0:T(8,128)(2,1)S(1)} fusion(bf16[2,8,6400]{2,1,0:T(8,128)(2,1)S(1)} %collective-permute-done.1, bf16[1,8,6400]{2,1,0:T(8,128)(2,1)S(1)} %collective-permute-done, bf16[1,8,6400]{2,1,0:T(8,128)(2,1)} %bitcast.52), kind=kLoop, calls=%fused_computation.25 | loop fusion | flops 409600 | bytes 819200 | tf_op jit(solution)/shard_map/concatenate | solution.py:56
  17.0 0.9 %collective-permute-start.2 = (bf16[4,8,6400]{2,1,0:T(8,128)(2,1)S(1)}, bf16[4,8,6400]{2,1,0:T(8,128)(2,1)S(1)}, u32[]{:S(2)}, u32[]{:S(2)}) collective-permute-start(bf16[4,8,6400]{2,1,0:T(8,128)(2,1)S(1)} %pad_maximum_fusion.1), channel_id=1, source_target_pairs={{0,4},{1,3},{2,6},{3,1},{4,0},{5,7},{6,2},{7,5},{8,12},{9,11},{10,... | collective-permute-start | bytes 1228808 | tf_op jit(solution)/shard_map/ppermute | solution.py:48
  17.9 7.1 %collective-permute-done.2 = bf16[4,8,6400]{2,1,0:T(8,128)(2,1)S(1)} collective-permute-done((bf16[4,8,6400]{2,1,0:T(8,128)(2,1)S(1)}, bf16[4,8,6400]{2,1,0:T(8,128)(2,1)S(1)}, u32[]{:S(2)}, u32[]{:S(2)}) %collective-permute-start.2) | collective-permute-done | bytes 409632 | tf_op jit(solution)/shard_map/ppermute | solution.py:48
  25.1 0.1 pad_maximum_fusion
  25.1 0.1 collective-permute-start.3
  25.3 0.0 copy-start.3
  25.3 2.2 %collective-permute-done.3 = bf16[8,8,6400]{2,1,0:T(8,128)(2,1)S(1)} collective-permute-done((bf16[8,8,6400]{2,1,0:T(8,128)(2,1)S(1)}, bf16[8,8,6400]{2,1,0:T(8,128)(2,1)S(1)}, u32[]{:S(2)}, u32[]{:S(2)}) %collective-permute-start.3) | collective-permute-done | bytes 819232 | tf_op jit(solution)/shard_map/ppermute | solution.py:48
  27.5 0.1 constant_dynamic-update-slice_fusion
  27.6 0.4 fusion.3
  28.0 5.4 %fusion = f32[128,576]{0,1:T(8,128)S(1)} fusion(bf16[1,6400,576]{1,2,0:T(8,128)(2,1)} %param.10, bf16[16,8,6400]{2,1,0:T(8,128)(2,1)S(1)} %constant_dynamic-update-slice_fusion, f32[6400]{0:T(1024)S(1)} %copy-done.3, f32[16,8]{1,0:T(8,128)S(1)} %add_rsqrt_fusion), kind=kOutput, calls=%fused_computation.1 | convolution fusion | flops 946995200 | bytes 9332224 | tf_op jit(solution)/shard_map/dot_general | solution.py:16
  33.4 0.6 fusion.23
  34.0 1.2 %convolution_multiply_fusion = f32[128,6400]{1,0:T(8,128)S(1)} fusion(bf16[1,288,6400]{2,1,0:T(8,128)(2,1)S(1)} %copy-done.1, f32[128]{0:T(128)S(1)} %fusion.23, f32[128,576]{0,1:T(8,128)S(1)} %fusion), kind=kOutput, calls=%fused_computation | convolution fusion | flops 472899584 | bytes 7258624 | tf_op jit(solution)/shard_map/dot_general | solution.py:18
  35.2 0.1 fusion.26
  35.3 0.2 collective-permute-start.4
  35.5 2.2 %collective-permute-done.4 = bf16[8,8,6400]{2,1,0:T(8,128)(2,1)S(1)} collective-permute-done((bf16[8,8,6400]{2,1,0:T(8,128)(2,1)S(1)}, bf16[8,8,6400]{2,1,0:T(8,128)(2,1)S(1)}, u32[]{:S(2)}, u32[]{:S(2)}) %collective-permute-start.4) | collective-permute-done | bytes 819232 | tf_op jit(solution)/shard_map/ppermute | solution.py:48
  37.7 0.1 fusion.7
  37.8 0.0 copy-start.4
  37.9 0.9 %collective-permute-start.5 = (bf16[4,8,6400]{2,1,0:T(8,128)(2,1)S(1)}, bf16[4,8,6400]{2,1,0:T(8,128)(2,1)S(1)}, u32[]{:S(2)}, u32[]{:S(2)}) collective-permute-start(bf16[4,8,6400]{2,1,0:T(8,128)(2,1)S(1)} %slice.85), channel_id=1, source_target_pairs={{0,4},{1,3},{2,6},{3,1},{4,0},{5,7},{6,2},{7,5},{8,12},{9,11},{10,... | collective-permute-start | bytes 1228808 | tf_op jit(solution)/shard_map/ppermute | solution.py:48
  38.7 7.2 %collective-permute-done.5 = bf16[4,8,6400]{2,1,0:T(8,128)(2,1)S(1)} collective-permute-done((bf16[4,8,6400]{2,1,0:T(8,128)(2,1)S(1)}, bf16[4,8,6400]{2,1,0:T(8,128)(2,1)S(1)}, u32[]{:S(2)}, u32[]{:S(2)}) %collective-permute-start.5) | collective-permute-done | bytes 409632 | tf_op jit(solution)/shard_map/ppermute | solution.py:48
  45.9 0.1 slice_add_fusion
  46.0 1.6 %collective-permute-start.6 = (bf16[2,8,6400]{2,1,0:T(8,128)(2,1)S(1)}, bf16[2,8,6400]{2,1,0:T(8,128)(2,1)S(1)}, u32[]{:S(2)}, u32[]{:S(2)}) collective-permute-start(bf16[2,8,6400]{2,1,0:T(8,128)(2,1)S(1)} %slice.86), channel_id=1, source_target_pairs={{0,2},{1,5},{2,0},{3,7},{4,6},{5,1},{6,4},{7,3},{8,10},{9,13},{10,... | collective-permute-start | bytes 614408 | tf_op jit(solution)/shard_map/ppermute | solution.py:48
  47.6 4.2 %collective-permute-done.6 = bf16[2,8,6400]{2,1,0:T(8,128)(2,1)S(1)} collective-permute-done((bf16[2,8,6400]{2,1,0:T(8,128)(2,1)S(1)}, bf16[2,8,6400]{2,1,0:T(8,128)(2,1)S(1)}, u32[]{:S(2)}, u32[]{:S(2)}) %collective-permute-start.6) | collective-permute-done | bytes 204832 | tf_op jit(solution)/shard_map/ppermute | solution.py:48
  51.9 2.1 %collective-permute-start.7 = (bf16[8,6400]{1,0:T(8,128)(2,1)S(1)}, bf16[8,6400]{1,0:T(8,128)(2,1)S(1)}, u32[]{:S(2)}, u32[]{:S(2)}) collective-permute-start(bf16[8,6400]{1,0:T(8,128)(2,1)S(1)} %fusion.31), channel_id=1, source_target_pairs={{0,8},{1,9},{2,10},{3,11},{4,12},{5,13},{6,14},{7,15},{8,0},{9,1},... | collective-permute-start | bytes 307208 | tf_op jit(solution)/shard_map/ppermute | solution.py:48
  54.0 4.6 %collective-permute-done.7 = bf16[8,6400]{1,0:T(8,128)(2,1)S(1)} collective-permute-done((bf16[8,6400]{1,0:T(8,128)(2,1)S(1)}, bf16[8,6400]{1,0:T(8,128)(2,1)S(1)}, u32[]{:S(2)}, u32[]{:S(2)}) %collective-permute-start.7) | collective-permute-done | bytes 102432 | tf_op jit(solution)/shard_map/ppermute | solution.py:48
  58.6 0.7 %fusion.29 = bf16[8,6400]{1,0:T(8,128)(2,1)} fusion(f32[2,8,6400]{2,1,0:T(8,128)S(1)} %slice_add_fusion.1, bf16[8,6400]{1,0:T(8,128)(2,1)S(1)} %collective-permute-done.7, bf16[8,6400]{1,0:T(8,128)(2,1)S(1)} %copy-done.2, pred[8]{0:T(512)(128)(4,1)S(1)} %compare_bitcast_fusion), kind=kLoop, calls=%fused_computation.29 | loop fusion | flops 256000 | bytes 512008 | tf_op jit(solution)/shard_map/convert_element_type | solution.py:75
  (16 shorter events, 0.2 us)
Async XLA Ops:
  0.0 33.4 %copy-start = (bf16[6400,2]{0,1:T(2,128)(2,1)S(1)}, bf16[6400,2]{0,1:T(2,128)(2,1)}, u32[]{:S(2)}) copy-start(bf16[6400,2]{0,1:T(2,128)(2,1)} %param.8) | copy-start | bytes 76804
  0.0 25.1 %copy-start.2 = (bf16[8,6400]{1,0:T(8,128)(2,1)S(1)}, bf16[8,6400]{1,0:T(8,128)(2,1)}, u32[]{:S(2)}) copy-start(bf16[8,6400]{1,0:T(8,128)(2,1)} %param.6) | copy-start | bytes 307204
  0.0 9.4 %collective-permute-start = (bf16[1,8,6400]{2,1,0:T(8,128)(2,1)}, bf16[1,8,6400]{2,1,0:T(8,128)(2,1)S(1)}, u32[]{:S(2)}, u32[]{:S(2)}) collective-permute-start(bf16[1,8,6400]{2,1,0:T(8,128)(2,1)} %bitcast.50), channel_id=1, source_target_pairs={{0,8},{1,9},{2,10},{3,11},{4,12},{5,13},{6,14},{7,15},{8,0},{9,1},... | collective-permute-start | bytes 307208 | tf_op jit(solution)/shard_map/ppermute | solution.py:48
  10.3 5.8 %collective-permute-start.1 = (bf16[2,8,6400]{2,1,0:T(8,128)(2,1)S(1)}, bf16[2,8,6400]{2,1,0:T(8,128)(2,1)S(1)}, u32[]{:S(2)}, u32[]{:S(2)}) collective-permute-start(bf16[2,8,6400]{2,1,0:T(8,128)(2,1)S(1)} %pad_maximum_fusion.2), channel_id=1, source_target_pairs={{0,2},{1,5},{2,0},{3,7},{4,6},{5,1},{6,4},{7,3},{8,10},{9,13},{10,... | collective-permute-start | bytes 614408 | tf_op jit(solution)/shard_map/ppermute | solution.py:48
  17.0 8.0 %collective-permute-start.2 = (bf16[4,8,6400]{2,1,0:T(8,128)(2,1)S(1)}, bf16[4,8,6400]{2,1,0:T(8,128)(2,1)S(1)}, u32[]{:S(2)}, u32[]{:S(2)}) collective-permute-start(bf16[4,8,6400]{2,1,0:T(8,128)(2,1)S(1)} %pad_maximum_fusion.1), channel_id=1, source_target_pairs={{0,4},{1,3},{2,6},{3,1},{4,0},{5,7},{6,2},{7,5},{8,12},{9,11},{10,... | collective-permute-start | bytes 1228808 | tf_op jit(solution)/shard_map/ppermute | solution.py:48
  25.1 2.4 %collective-permute-start.3 = (bf16[8,8,6400]{2,1,0:T(8,128)(2,1)S(1)}, bf16[8,8,6400]{2,1,0:T(8,128)(2,1)S(1)}, u32[]{:S(2)}, u32[]{:S(2)}) collective-permute-start(bf16[8,8,6400]{2,1,0:T(8,128)(2,1)S(1)} %pad_maximum_fusion), channel_id=1, source_target_pairs={{0,1},{1,0},{2,3},{3,2},{4,5},{5,4},{6,7},{7,6},{8,9},{9,8},{10,11... | collective-permute-start | bytes 2457608 | tf_op jit(solution)/shard_map/ppermute | solution.py:48
  25.3 2.7 %copy-start.3 = (f32[6400]{0:T(1024)S(1)}, f32[6400]{0:T(1024)}, u32[]{:S(2)}) copy-start(f32[6400]{0:T(1024)} %param.7) | copy-start | bytes 76804
  28.0 6.0 %copy-start.1 = (bf16[1,288,6400]{2,1,0:T(8,128)(2,1)S(1)}, bf16[1,288,6400]{2,1,0:T(8,128)(2,1)}, u32[]{:S(2)}) copy-start(bf16[1,288,6400]{2,1,0:T(8,128)(2,1)} %param.11) | copy-start | bytes 11059204
  35.3 2.4 %collective-permute-start.4 = (bf16[8,8,6400]{2,1,0:T(8,128)(2,1)S(1)}, bf16[8,8,6400]{2,1,0:T(8,128)(2,1)S(1)}, u32[]{:S(2)}, u32[]{:S(2)}) collective-permute-start(bf16[8,8,6400]{2,1,0:T(8,128)(2,1)S(1)} %fusion.26), channel_id=1, source_target_pairs={{0,1},{1,0},{2,3},{3,2},{4,5},{5,4},{6,7},{7,6},{8,9},{9,8},{10,11... | collective-permute-start | bytes 2457608 | tf_op jit(solution)/shard_map/ppermute | solution.py:48
  37.8 16.2 %copy-start.4 = (s32[8,1]{0,1:T(1,128)S(1)}, s32[8,1]{0,1:T(1,128)}, u32[]{:S(2)}) copy-start(s32[8,1]{0,1:T(1,128)} %param.9) | copy-start | bytes 100
  37.9 8.0 %collective-permute-start.5 = (bf16[4,8,6400]{2,1,0:T(8,128)(2,1)S(1)}, bf16[4,8,6400]{2,1,0:T(8,128)(2,1)S(1)}, u32[]{:S(2)}, u32[]{:S(2)}) collective-permute-start(bf16[4,8,6400]{2,1,0:T(8,128)(2,1)S(1)} %slice.85), channel_id=1, source_target_pairs={{0,4},{1,3},{2,6},{3,1},{4,0},{5,7},{6,2},{7,5},{8,12},{9,11},{10,... | collective-permute-start | bytes 1228808 | tf_op jit(solution)/shard_map/ppermute | solution.py:48
  46.0 5.8 %collective-permute-start.6 = (bf16[2,8,6400]{2,1,0:T(8,128)(2,1)S(1)}, bf16[2,8,6400]{2,1,0:T(8,128)(2,1)S(1)}, u32[]{:S(2)}, u32[]{:S(2)}) collective-permute-start(bf16[2,8,6400]{2,1,0:T(8,128)(2,1)S(1)} %slice.86), channel_id=1, source_target_pairs={{0,2},{1,5},{2,0},{3,7},{4,6},{5,1},{6,4},{7,3},{8,10},{9,13},{10,... | collective-permute-start | bytes 614408 | tf_op jit(solution)/shard_map/ppermute | solution.py:48
  51.9 6.7 %collective-permute-start.7 = (bf16[8,6400]{1,0:T(8,128)(2,1)S(1)}, bf16[8,6400]{1,0:T(8,128)(2,1)S(1)}, u32[]{:S(2)}, u32[]{:S(2)}) collective-permute-start(bf16[8,6400]{1,0:T(8,128)(2,1)S(1)} %fusion.31), channel_id=1, source_target_pairs={{0,8},{1,9},{2,10},{3,11},{4,12},{5,13},{6,14},{7,15},{8,0},{9,1},... | collective-permute-start | bytes 307208 | tf_op jit(solution)/shard_map/ppermute | solution.py:48

commit v2 on v0

v2 whole, which is shorter than its diff:
```python
import functools

import jax
import jax.numpy as jnp
from jax import lax
from jax.experimental import pallas as pl
from jax.experimental.pallas import tpu as pltpu
from jax.sharding import PartitionSpec as P


def pick_chunk(width, most):
    chunk = most
    while width % chunk:
        chunk -= 128
    return chunk


def expert_kernel(copies, count, *refs):
    block_refs, refs = refs[:count], refs[count:]
    gain_ref, router_ref, up_ref, down_ref = refs[:4]
    out_refs, normed_ref = refs[4 : 4 + count], refs[4 + count]
    tok_rows, width = block_refs[0].shape
    units = down_ref.shape[0]
    chunk = pick_chunk(width, 1280)
    for first in range(0, count, 2):
        pair = block_refs[first : first + 2]

        def load(at):
            return jnp.concatenate([ref[:, at : at + chunk].astype(jnp.float32) for ref in pair], axis=0)

        total = jnp.zeros((2 * tok_rows, chunk), jnp.float32)
        for at in range(0, width, chunk):
            values = load(at)
            total = total + values * values
        mean_square = jnp.sum(total, axis=1, keepdims=True) * (1.0 / width)
        factor = lax.rsqrt(mean_square + 1e-06)
        for at in range(0, width, chunk):
            normed = load(at) * factor * gain_ref[:, at : at + chunk]
            normed_ref[first * tok_rows : (first + 2) * tok_rows, at : at + chunk] = normed.astype(jnp.bfloat16)
    nt = (((1,), (1,)), ((), ()))
    normed = normed_ref[...]
    lifted = lax.dot_general(normed, up_ref[...], nt, preferred_element_type=jnp.float32)
    gate, up = lifted[:, :units], lifted[:, units:]
    act = (gate / (1.0 + jnp.exp(-gate)) * up).astype(jnp.bfloat16)
    logits = lax.dot_general(normed, router_ref[...], nt, preferred_element_type=jnp.float32)
    own = lax.axis_index("expert") // copies
    columns = lax.broadcasted_iota(jnp.int32, logits.shape, 1)
    logit = jnp.sum(jnp.where(columns == own, logits, 0.0), axis=1, keepdims=True)
    scores = 1.0 / (1.0 + jnp.exp(-logit))
    for at in range(0, width, chunk):
        output = jnp.dot(act, down_ref[:, at : at + chunk], preferred_element_type=jnp.float32) * scores
        for k in range(count):
            out_refs[k][:, at : at + chunk] = output[k * tok_rows : (k + 1) * tok_rows].astype(jnp.bfloat16)


def expert_rows(blocks, norm_gain, router, gate_up, down_w, copies):
    count = len(blocks)
    tok_rows, width = blocks[0].shape
    units = down_w.shape[0]
    rows = count * tok_rows
    vmem = pl.BlockSpec(memory_space=pltpu.VMEM)
    gate_up = pltpu.with_memory_space_constraint(gate_up, pltpu.VMEM)
    down_w = pltpu.with_memory_space_constraint(down_w, pltpu.VMEM)
    return pl.pallas_call(
        functools.partial(expert_kernel, copies, count),
        out_shape=[jax.ShapeDtypeStruct((tok_rows, width), jnp.bfloat16)] * count,
        in_specs=[vmem] * (count + 4),
        out_specs=[vmem] * count,
        scratch_shapes=[pltpu.VMEM((rows, width), jnp.bfloat16)],
        compiler_params=pltpu.CompilerParams(vmem_limit_bytes=40 * 1024 * 1024),
        cost_estimate=pl.CostEstimate(
            flops=6 * rows * width * units,
            bytes_accessed=6 * units * width,
            transcendentals=rows * units,
        ),
    )(*blocks, norm_gain[None, :], router.T, gate_up, down_w)


def body(hidden_in, norm_gain, router, routes, routed_gate_up, routed_down):
    axis_len = lax.axis_size("expert")
    experts = router.shape[1]
    copies = axis_len // experts
    own_expert = lax.axis_index("expert") // copies
    chips = list(range(2, copies, 2))[::-1]

    def swap(block, mask):
        return lax.ppermute(block, "expert", [(i, i ^ mask) for i in range(axis_len)])

    far = [swap(hidden_in, copies * k) for k in range(1, experts)]
    sources = [hidden_in] + far
    mine = [[block] + [swap(block, mask) for mask in chips] for block in sources]
    theirs = [[swap(block, 1) for block in group] for group in mine]
    flat = sum(mine, []) + sum(theirs, [])
    outs = expert_rows(flat, norm_gain, router, routed_gate_up[0].T, routed_down[0], copies)
    size = len(chips) + 1
    kept = [outs[k * size : (k + 1) * size] for k in range(experts)]
    given = [outs[(experts + k) * size : (experts + k + 1) * size] for k in range(experts)]

    def fold(own_parts, given_parts):
        back = [swap(part, 1) for part in given_parts]
        both = [a.astype(jnp.float32) + b.astype(jnp.float32) for a, b in zip(own_parts, back)]
        total = both[0]
        for part, mask in zip(both[1:], chips):
            total = total + swap(part.astype(jnp.bfloat16), mask).astype(jnp.float32)
        return total

    chosen = None
    for k in list(range(1, experts)) + [0]:
        total = fold(kept[k], given[k])
        if k:
            total = swap(total.astype(jnp.bfloat16), copies * k).astype(jnp.float32)
        other = jnp.bitwise_xor(own_expert, k)
        chosen = total if chosen is None else jnp.where(routes == other, total, chosen)
    return (hidden_in.astype(jnp.float32) + chosen).astype(jnp.bfloat16)


def solution(mesh):
    placed = (
        P(("groups", "expert"), None),
        P(),
        P(),
        P(("groups", "expert"), None),
        P("expert", None, None),
        P("expert", None, None),
    )
    return jax.shard_map(
        body, mesh=mesh, in_specs=placed, out_specs=P(("groups", "expert"), None), check_vma=False
    )
```

time: 105 us -> 50.8 us (0.48)
  blocking collectives: 48.9 us -> 0 us
  waiting for transfers between devices: 33.1 us -> 13.5 us
  starting transfers between devices: 7.39 us -> 24 us
  matrix products: 9.15 us -> 0 us
  local copies, waits for them, and re-layouts: 2.87 us -> 7.54 us
  Pallas kernels: 0 us -> 4.35 us
  other arithmetic: 3.57 us -> 0.99 us
    all_to_all x1 -> x0, blocking collectives: 48.9 us -> none  [body(): lax.all_to_all(result.astype(jnp.bfloat16), 'expert', split_axis=0, conca...]
    all_to_all x1 -> x0, waiting for transfers between devices: 33.1 us -> none  [body(): lax.all_to_all(send_rows, 'expert', split_axis=0, concat_axis=0, tiled=True)]
    ppermute x0 -> x30, starting transfers between devices: none -> 24 us  [swap(): lax.ppermute(block, 'expert', [(i, i ^ mask) for i in range(axis_len)])]
    ppermute x0 -> x30, waiting for transfers between devices: none -> 13.5 us  [swap(): lax.ppermute(block, 'expert', [(i, i ^ mask) for i in range(axis_len)])]
    dot_general x5 -> x0, matrix products: 9.15 us -> none  [the longest x1 5.64 us: expert_rows(): lifted = jnp.dot(sel_rows, gate_up, preferred_element_type=jnp.float32)]
    all_to_all x1 -> x0, starting transfers between devices: 7.39 us -> none  [body(): lax.all_to_all(send_rows, 'expert', split_axis=0, concat_axis=0, tiled=True)]
    unnamed x6 -> x12, local copies, waits for them, and re-layouts: 0.54 us -> 6.78 us
    pallas_call x0 -> x1, Pallas kernels: none -> 4.35 us  [expert_rows(): pl.pallas_call(functools.partial(expert_kernel, copies, count), out_shape...]
  transfers between devices with their start and end apart: 1 -> 30, of which waited for: 1 -> 13; matrix products, arithmetic and copies ran while one was open for 0% -> 2% of each run, Pallas kernels for 0% -> 0%
where the time goes in v2:
time: 50.8 us; the launch traced here: 50.4 us
  starting transfers between devices  24 us (47%)
  waiting for transfers between devices  13.5 us (27%)
  local copies, waits for them, and re-layouts  7.54 us (15%)
  Pallas kernels  4.35 us (9%)
  other arithmetic  0.99 us (2%)
    ppermute x30, starting transfers between devices, swap(): lax.ppermute(block, 'expert', [(i, i ^ mask) for i in range(axis_len)])  24 us
    ppermute x30, waiting for transfers between devices, swap(): lax.ppermute(block, 'expert', [(i, i ^ mask) for i in range(axis_len)])  13.5 us
    unnamed x12, local copies, waits for them, and re-layouts  6.78 us
    pallas_call x1, Pallas kernels, expert_rows(): pl.pallas_call(functools.partial(expert_kernel, copies, count), out_shape...  4.35 us
  transfers between devices with their start and end apart: 30, of which 13 were waited for; matrix products, arithmetic and copies ran while one was open for 2% of the time, Pallas kernels for 0%

profile of v2, /device:TPU:0, one launch (start us, length us, event | category | flops | bytes accessed | tf_op | source)
XLA Modules:
  0.0 50.4 jit_solution(1543777576571908608)
XLA Ops:
  0.0 4.0 %collective-permute-start.3 = (bf16[8,6400]{1,0:T(8,128)(2,1)}, bf16[8,6400]{1,0:T(8,128)(2,1)S(1)}, u32[]{:S(2)}, u32[]{:S(2)}) collective-permute-start(bf16[8,6400]{1,0:T(8,128)(2,1)} %refs_0_.1), channel_id=1, source_target_pairs={{0,8},{1,9},{2,10},{3,11},{4,12},{5,13},{6,14},{7,15},{8,0},{9,1},... | collective-permute-start | bytes 307208 | tf_op jit(solution)/shard_map/ppermute | solution.py:87
  4.0 1.5 %collective-permute-start.2 = (bf16[8,6400]{1,0:T(8,128)(2,1)}, bf16[8,6400]{1,0:T(8,128)(2,1)S(1)}, u32[]{:S(2)}, u32[]{:S(2)}) collective-permute-start(bf16[8,6400]{1,0:T(8,128)(2,1)} %refs_0_.1), channel_id=1, source_target_pairs={{0,2},{1,3},{2,0},{3,1},{4,6},{5,7},{6,4},{7,5},{8,10},{9,11},{10,... | collective-permute-start | bytes 307208 | tf_op jit(solution)/shard_map/ppermute | solution.py:87
  5.6 1.5 %collective-permute-start = (bf16[8,6400]{1,0:T(8,128)(2,1)}, bf16[8,6400]{1,0:T(8,128)(2,1)S(1)}, u32[]{:S(2)}, u32[]{:S(2)}) collective-permute-start(bf16[8,6400]{1,0:T(8,128)(2,1)} %refs_0_.1), channel_id=1, source_target_pairs={{0,6},{1,7},{2,4},{3,5},{4,2},{5,3},{6,0},{7,1},{8,14},{9,15},{10,... | collective-permute-start | bytes 307208 | tf_op jit(solution)/shard_map/ppermute | solution.py:87
  7.1 0.4 collective-permute-start.1
  7.5 1.9 %collective-permute-done.3.refs_4_ = bf16[8,6400]{1,0:T(8,128)(2,1)S(1)} collective-permute-done((bf16[8,6400]{1,0:T(8,128)(2,1)}, bf16[8,6400]{1,0:T(8,128)(2,1)S(1)}, u32[]{:S(2)}, u32[]{:S(2)}) %collective-permute-start.3) | collective-permute-done | bytes 102432 | tf_op jit(solution)/shard_map/ppermute | solution.py:87
  9.4 1.7 %collective-permute-start.4 = (bf16[8,6400]{1,0:T(8,128)(2,1)S(1)}, bf16[8,6400]{1,0:T(8,128)(2,1)S(1)}, u32[]{:S(2)}, u32[]{:S(2)}) collective-permute-start(bf16[8,6400]{1,0:T(8,128)(2,1)S(1)} %collective-permute-done.3.refs_4_), channel_id=1, source_target_pairs={{0,6},{1,7},{2,4},{3,5},{4,2},{5,3},{6,0},{7,1},{8,14},{9,15},{10,... | collective-permute-start | bytes 307208 | tf_op jit(solution)/shard_map/ppermute | solution.py:87
  11.2 1.3 %collective-permute-start.5 = (bf16[8,6400]{1,0:T(8,128)(2,1)S(1)}, bf16[8,6400]{1,0:T(8,128)(2,1)S(1)}, u32[]{:S(2)}, u32[]{:S(2)}) collective-permute-start(bf16[8,6400]{1,0:T(8,128)(2,1)S(1)} %collective-permute-done.3.refs_4_), channel_id=1, source_target_pairs={{0,4},{1,5},{2,6},{3,7},{4,0},{5,1},{6,2},{7,3},{8,12},{9,13},{10,... | collective-permute-start | bytes 307208 | tf_op jit(solution)/shard_map/ppermute | solution.py:87
  12.7 0.6 %collective-permute-start.6 = (bf16[8,6400]{1,0:T(8,128)(2,1)S(1)}, bf16[8,6400]{1,0:T(8,128)(2,1)S(1)}, u32[]{:S(2)}, u32[]{:S(2)}) collective-permute-start(bf16[8,6400]{1,0:T(8,128)(2,1)S(1)} %collective-permute-done.3.refs_4_), channel_id=1, source_target_pairs={{0,2},{1,3},{2,0},{3,1},{4,6},{5,7},{6,4},{7,5},{8,10},{9,11},{10,... | collective-permute-start | bytes 307208 | tf_op jit(solution)/shard_map/ppermute | solution.py:87
  13.2 0.6 %collective-permute-done.1.refs_2_ = bf16[8,6400]{1,0:T(8,128)(2,1)S(1)} collective-permute-done((bf16[8,6400]{1,0:T(8,128)(2,1)}, bf16[8,6400]{1,0:T(8,128)(2,1)S(1)}, u32[]{:S(2)}, u32[]{:S(2)}) %collective-permute-start.1) | collective-permute-done | bytes 102432 | tf_op jit(solution)/shard_map/ppermute | solution.py:87
  13.9 0.5 %collective-permute-start.10 = (bf16[8,6400]{1,0:T(8,128)(2,1)S(1)}, bf16[8,6400]{1,0:T(8,128)(2,1)S(1)}, u32[]{:S(2)}, u32[]{:S(2)}) collective-permute-start(bf16[8,6400]{1,0:T(8,128)(2,1)S(1)} %collective-permute-done.2.refs_3_), channel_id=1, source_target_pairs={{0,1},{1,0},{2,3},{3,2},{4,5},{5,4},{6,7},{7,6},{8,9},{9,8},{10,11... | collective-permute-start | bytes 307208 | tf_op jit(solution)/shard_map/ppermute | solution.py:87
  14.4 2.7 %collective-permute-done.4.refs_5_ = bf16[8,6400]{1,0:T(8,128)(2,1)S(1)} collective-permute-done((bf16[8,6400]{1,0:T(8,128)(2,1)S(1)}, bf16[8,6400]{1,0:T(8,128)(2,1)S(1)}, u32[]{:S(2)}, u32[]{:S(2)}) %collective-permute-start.4) | collective-permute-done | bytes 102432 | tf_op jit(solution)/shard_map/ppermute | solution.py:87
  17.8 0.5 collective-permute-start.13
  18.3 0.8 %broadcast_in_dim.15.refs_16_ = f32[1,6400]{1,0:T(1,128)S(1)} reshape(f32[6400]{0:T(1024)} %param.7) | data formatting | bytes 51200 | tf_op jit(solution)/shard_map/broadcast_in_dim | solution.py:76
  19.6 3.1 %copy-done = bf16[1,6400,576]{1,2,0:T(8,128)(2,1)S(1)} copy-done((bf16[1,6400,576]{1,2,0:T(8,128)(2,1)S(1)}, bf16[1,6400,576]{1,2,0:T(8,128)(2,1)}, u32[]{:S(2)}) %copy-start) | copy-done | bytes 7372824
  22.7 2.0 %copy-done.1 = bf16[1,288,6400]{2,1,0:T(8,128)(2,1)S(1)} copy-done((bf16[1,288,6400]{2,1,0:T(8,128)(2,1)S(1)}, bf16[1,288,6400]{2,1,0:T(8,128)(2,1)}, u32[]{:S(2)}) %copy-start.1) | copy-done | bytes 3686424
  24.7 0.9 %copy-done.2 = bf16[8,6400]{1,0:T(8,128)(2,1)S(1)} copy-done((bf16[8,6400]{1,0:T(8,128)(2,1)S(1)}, bf16[8,6400]{1,0:T(8,128)(2,1)}, u32[]{:S(2)}) %copy-start.2) | copy-done | bytes 102424
  25.6 0.7 %copy-done.4 = bf16[6400,2]{0,1:T(2,128)(2,1)S(1)} copy-done((bf16[6400,2]{0,1:T(2,128)(2,1)S(1)}, bf16[6400,2]{0,1:T(2,128)(2,1)}, u32[]{:S(2)}) %copy-start.4) | copy-done | bytes 25624
  26.4 4.3 %shard_map.64 = (bf16[8,6400]{1,0:T(8,128)(2,1)S(1)}, bf16[8,6400]{1,0:T(8,128)(2,1)S(1)}, bf16[8,6400]{1,0:T(8,128)(2,1)S(1)}, bf16[8,6400]{1,0:T(8,128)(2,1)S(...) custom-call(bf16[8,6400]{1,0:T(8,128)(2,1)S(1)} %copy-done.2, ...), custom_call_target="tpu_custom_call" | custom-call | flops 1415577600 | bytes 11059200 | tf_op jit(solution)/shard_map/pallas_call | solution.py:64
  30.9 0.4 collective-permute-start.25
  31.4 0.4 collective-permute-start.22
  33.1 1.5 %collective-permute-start.24 = (bf16[8,6400]{1,0:T(8,128)(2,1)S(1)}, bf16[8,6400]{1,0:T(8,128)(2,1)S(1)}, u32[]{:S(2)}, u32[]{:S(2)}) collective-permute-start(bf16[8,6400]{1,0:T(8,128)(2,1)S(1)} %add_convert_fusion.4), channel_id=1, source_target_pairs={{0,6},{1,7},{2,4},{3,5},{4,2},{5,3},{6,0},{7,1},{8,14},{9,15},{10,... | collective-permute-start | bytes 307208 | tf_op jit(solution)/shard_map/ppermute | solution.py:87
  34.6 1.5 %collective-permute-start.26 = (bf16[8,6400]{1,0:T(8,128)(2,1)S(1)}, bf16[8,6400]{1,0:T(8,128)(2,1)S(1)}, u32[]{:S(2)}, u32[]{:S(2)}) collective-permute-start(bf16[8,6400]{1,0:T(8,128)(2,1)S(1)} %add_convert_fusion.3), channel_id=1, source_target_pairs={{0,4},{1,5},{2,6},{3,7},{4,0},{5,1},{6,2},{7,3},{8,12},{9,13},{10,... | collective-permute-start | bytes 307208 | tf_op jit(solution)/shard_map/ppermute | solution.py:87
  36.2 0.7 %collective-permute-start.28 = (bf16[8,6400]{1,0:T(8,128)(2,1)S(1)}, bf16[8,6400]{1,0:T(8,128)(2,1)S(1)}, u32[]{:S(2)}, u32[]{:S(2)}) collective-permute-start(bf16[8,6400]{1,0:T(8,128)(2,1)S(1)} %add_convert_fusion.2), channel_id=1, source_target_pairs={{0,2},{1,3},{2,0},{3,1},{4,6},{5,7},{6,4},{7,5},{8,10},{9,11},{10,... | collective-permute-start | bytes 307208 | tf_op jit(solution)/shard_map/ppermute | solution.py:87
  36.9 1.5 %collective-permute-start.17 = (bf16[8,6400]{1,0:T(8,128)(2,1)S(1)}, bf16[8,6400]{1,0:T(8,128)(2,1)S(1)}, u32[]{:S(2)}, u32[]{:S(2)}) collective-permute-start(bf16[8,6400]{1,0:T(8,128)(2,1)S(1)} %add_convert_fusion.7), channel_id=1, source_target_pairs={{0,6},{1,7},{2,4},{3,5},{4,2},{5,3},{6,0},{7,1},{8,14},{9,15},{10,... | collective-permute-start | bytes 307208 | tf_op jit(solution)/shard_map/ppermute | solution.py:87
  38.4 1.3 %collective-permute-done.24 = bf16[8,6400]{1,0:T(8,128)(2,1)S(1)} collective-permute-done((bf16[8,6400]{1,0:T(8,128)(2,1)S(1)}, bf16[8,6400]{1,0:T(8,128)(2,1)S(1)}, u32[]{:S(2)}, u32[]{:S(2)}) %collective-permute-start.24) | collective-permute-done | bytes 102432 | tf_op jit(solution)/shard_map/ppermute | solution.py:87
  39.8 1.1 %collective-permute-start.19 = (bf16[8,6400]{1,0:T(8,128)(2,1)S(1)}, bf16[8,6400]{1,0:T(8,128)(2,1)S(1)}, u32[]{:S(2)}, u32[]{:S(2)}) collective-permute-start(bf16[8,6400]{1,0:T(8,128)(2,1)S(1)} %add_convert_fusion.6), channel_id=1, source_target_pairs={{0,4},{1,5},{2,6},{3,7},{4,0},{5,1},{6,2},{7,3},{8,12},{9,13},{10,... | collective-permute-start | bytes 307208 | tf_op jit(solution)/shard_map/ppermute | solution.py:87
  40.9 1.0 %collective-permute-done.26 = bf16[8,6400]{1,0:T(8,128)(2,1)S(1)} collective-permute-done((bf16[8,6400]{1,0:T(8,128)(2,1)S(1)}, bf16[8,6400]{1,0:T(8,128)(2,1)S(1)}, u32[]{:S(2)}, u32[]{:S(2)}) %collective-permute-start.26) | collective-permute-done | bytes 102432 | tf_op jit(solution)/shard_map/ppermute | solution.py:87
  41.9 0.6 %collective-permute-start.21 = (bf16[8,6400]{1,0:T(8,128)(2,1)S(1)}, bf16[8,6400]{1,0:T(8,128)(2,1)S(1)}, u32[]{:S(2)}, u32[]{:S(2)}) collective-permute-start(bf16[8,6400]{1,0:T(8,128)(2,1)S(1)} %add_convert_fusion.5), channel_id=1, source_target_pairs={{0,2},{1,3},{2,0},{3,1},{4,6},{5,7},{6,4},{7,5},{8,10},{9,11},{10,... | collective-permute-start | bytes 307208 | tf_op jit(solution)/shard_map/ppermute | solution.py:87
  42.6 2.4 %collective-permute-start.29 = (bf16[8,6400]{1,0:T(8,128)(2,1)S(1)}, bf16[8,6400]{1,0:T(8,128)(2,1)S(1)}, u32[]{:S(2)}, u32[]{:S(2)}) collective-permute-start(bf16[8,6400]{1,0:T(8,128)(2,1)S(1)} %add_convert_fusion.1), channel_id=1, source_target_pairs={{0,8},{1,9},{2,10},{3,11},{4,12},{5,13},{6,14},{7,15},{8,0},{9,1},... | collective-permute-start | bytes 307208 | tf_op jit(solution)/shard_map/ppermute | solution.py:87
  45.1 1.6 %collective-permute-done.19 = bf16[8,6400]{1,0:T(8,128)(2,1)S(1)} collective-permute-done((bf16[8,6400]{1,0:T(8,128)(2,1)S(1)}, bf16[8,6400]{1,0:T(8,128)(2,1)S(1)}, u32[]{:S(2)}, u32[]{:S(2)}) %collective-permute-start.19) | collective-permute-done | bytes 102432 | tf_op jit(solution)/shard_map/ppermute | solution.py:87
  46.7 3.0 %collective-permute-done.29 = bf16[8,6400]{1,0:T(8,128)(2,1)S(1)} collective-permute-done((bf16[8,6400]{1,0:T(8,128)(2,1)S(1)}, bf16[8,6400]{1,0:T(8,128)(2,1)S(1)}, u32[]{:S(2)}, u32[]{:S(2)}) %collective-permute-start.29) | collective-permute-done | bytes 102432 | tf_op jit(solution)/shard_map/ppermute | solution.py:87
  49.7 0.8 %add_convert_fusion = bf16[8,6400]{1,0:T(8,128)(2,1)} fusion(bf16[8,6400]{1,0:T(8,128)(2,1)S(1)} %collective-permute-done.29, bf16[8,6400]{1,0:T(8,128)(2,1)S(1)} %collective-permute-done.21, bf16[8,6400]{1,0:T(8,128)(2,1)S(1)} %collective-permute-done.19, bf16[8,6400]{1,0:T(8,128)(2,1)S(1)} %collective-permute-done.17, ...), kind=kLoop, calls=%fused_computation | loop fusion | flops 716800 | bytes 819208 | tf_op jit(solution)/shard_map/convert_element_type | solution.py:114
  (51 shorter events, 3.3 us)
Async XLA Ops:
  0.0 9.4 %collective-permute-start.3 = (bf16[8,6400]{1,0:T(8,128)(2,1)}, bf16[8,6400]{1,0:T(8,128)(2,1)S(1)}, u32[]{:S(2)}, u32[]{:S(2)}) collective-permute-start(bf16[8,6400]{1,0:T(8,128)(2,1)} %refs_0_.1), channel_id=1, source_target_pairs={{0,8},{1,9},{2,10},{3,11},{4,12},{5,13},{6,14},{7,15},{8,0},{9,1},... | collective-permute-start | bytes 307208 | tf_op jit(solution)/shard_map/ppermute | solution.py:87
  4.0 7.1 %collective-permute-start.2 = (bf16[8,6400]{1,0:T(8,128)(2,1)}, bf16[8,6400]{1,0:T(8,128)(2,1)S(1)}, u32[]{:S(2)}, u32[]{:S(2)}) collective-permute-start(bf16[8,6400]{1,0:T(8,128)(2,1)} %refs_0_.1), channel_id=1, source_target_pairs={{0,2},{1,3},{2,0},{3,1},{4,6},{5,7},{6,4},{7,5},{8,10},{9,11},{10,... | collective-permute-start | bytes 307208 | tf_op jit(solution)/shard_map/ppermute | solution.py:87
  5.6 7.1 %collective-permute-start = (bf16[8,6400]{1,0:T(8,128)(2,1)}, bf16[8,6400]{1,0:T(8,128)(2,1)S(1)}, u32[]{:S(2)}, u32[]{:S(2)}) collective-permute-start(bf16[8,6400]{1,0:T(8,128)(2,1)} %refs_0_.1), channel_id=1, source_target_pairs={{0,6},{1,7},{2,4},{3,5},{4,2},{5,3},{6,0},{7,1},{8,14},{9,15},{10,... | collective-permute-start | bytes 307208 | tf_op jit(solution)/shard_map/ppermute | solution.py:87
  7.1 6.8 %collective-permute-start.1 = (bf16[8,6400]{1,0:T(8,128)(2,1)}, bf16[8,6400]{1,0:T(8,128)(2,1)S(1)}, u32[]{:S(2)}, u32[]{:S(2)}) collective-permute-start(bf16[8,6400]{1,0:T(8,128)(2,1)} %refs_0_.1), channel_id=1, source_target_pairs={{0,4},{1,5},{2,6},{3,7},{4,0},{5,1},{6,2},{7,3},{8,12},{9,13},{10,... | collective-permute-start | bytes 307208 | tf_op jit(solution)/shard_map/ppermute | solution.py:87
  7.5 6.3 %collective-permute-start.7 = (bf16[8,6400]{1,0:T(8,128)(2,1)}, bf16[8,6400]{1,0:T(8,128)(2,1)S(1)}, u32[]{:S(2)}, u32[]{:S(2)}) collective-permute-start(bf16[8,6400]{1,0:T(8,128)(2,1)} %refs_0_.1), channel_id=1, source_target_pairs={{0,1},{1,0},{2,3},{3,2},{4,5},{5,4},{6,7},{7,6},{8,9},{9,8},{10,11... | collective-permute-start | bytes 307208 | tf_op jit(solution)/shard_map/ppermute | solution.py:87
  9.4 7.7 %collective-permute-start.4 = (bf16[8,6400]{1,0:T(8,128)(2,1)S(1)}, bf16[8,6400]{1,0:T(8,128)(2,1)S(1)}, u32[]{:S(2)}, u32[]{:S(2)}) collective-permute-start(bf16[8,6400]{1,0:T(8,128)(2,1)S(1)} %collective-permute-done.3.refs_4_), channel_id=1, source_target_pairs={{0,6},{1,7},{2,4},{3,5},{4,2},{5,3},{6,0},{7,1},{8,14},{9,15},{10,... | collective-permute-start | bytes 307208 | tf_op jit(solution)/shard_map/ppermute | solution.py:87
  11.2 6.1 %collective-permute-start.5 = (bf16[8,6400]{1,0:T(8,128)(2,1)S(1)}, bf16[8,6400]{1,0:T(8,128)(2,1)S(1)}, u32[]{:S(2)}, u32[]{:S(2)}) collective-permute-start(bf16[8,6400]{1,0:T(8,128)(2,1)S(1)} %collective-permute-done.3.refs_4_), channel_id=1, source_target_pairs={{0,4},{1,5},{2,6},{3,7},{4,0},{5,1},{6,2},{7,3},{8,12},{9,13},{10,... | collective-permute-start | bytes 307208 | tf_op jit(solution)/shard_map/ppermute | solution.py:87
  12.7 5.1 %collective-permute-start.6 = (bf16[8,6400]{1,0:T(8,128)(2,1)S(1)}, bf16[8,6400]{1,0:T(8,128)(2,1)S(1)}, u32[]{:S(2)}, u32[]{:S(2)}) collective-permute-start(bf16[8,6400]{1,0:T(8,128)(2,1)S(1)} %collective-permute-done.3.refs_4_), channel_id=1, source_target_pairs={{0,2},{1,3},{2,0},{3,1},{4,6},{5,7},{6,4},{7,5},{8,10},{9,11},{10,... | collective-permute-start | bytes 307208 | tf_op jit(solution)/shard_map/ppermute | solution.py:87
  13.9 4.0 %collective-permute-start.11 = (bf16[8,6400]{1,0:T(8,128)(2,1)S(1)}, bf16[8,6400]{1,0:T(8,128)(2,1)S(1)}, u32[]{:S(2)}, u32[]{:S(2)}) collective-permute-start(bf16[8,6400]{1,0:T(8,128)(2,1)S(1)} %collective-permute-done.3.refs_4_), channel_id=1, source_target_pairs={{0,1},{1,0},{2,3},{3,2},{4,5},{5,4},{6,7},{7,6},{8,9},{9,8},{10,11... | collective-permute-start | bytes 307208 | tf_op jit(solution)/shard_map/ppermute | solution.py:87
  13.9 4.4 %collective-permute-start.10 = (bf16[8,6400]{1,0:T(8,128)(2,1)S(1)}, bf16[8,6400]{1,0:T(8,128)(2,1)S(1)}, u32[]{:S(2)}, u32[]{:S(2)}) collective-permute-start(bf16[8,6400]{1,0:T(8,128)(2,1)S(1)} %collective-permute-done.2.refs_3_), channel_id=1, source_target_pairs={{0,1},{1,0},{2,3},{3,2},{4,5},{5,4},{6,7},{7,6},{8,9},{9,8},{10,11... | collective-permute-start | bytes 307208 | tf_op jit(solution)/shard_map/ppermute | solution.py:87
  17.1 2.0 %collective-permute-start.8 = (bf16[8,6400]{1,0:T(8,128)(2,1)S(1)}, bf16[8,6400]{1,0:T(8,128)(2,1)S(1)}, u32[]{:S(2)}, u32[]{:S(2)}) collective-permute-start(bf16[8,6400]{1,0:T(8,128)(2,1)S(1)} %collective-permute-done.refs_1_), channel_id=1, source_target_pairs={{0,1},{1,0},{2,3},{3,2},{4,5},{5,4},{6,7},{7,6},{8,9},{9,8},{10,11... | collective-permute-start | bytes 307208 | tf_op jit(solution)/shard_map/ppermute | solution.py:87
  17.3 1.8 %collective-permute-start.9 = (bf16[8,6400]{1,0:T(8,128)(2,1)S(1)}, bf16[8,6400]{1,0:T(8,128)(2,1)S(1)}, u32[]{:S(2)}, u32[]{:S(2)}) collective-permute-start(bf16[8,6400]{1,0:T(8,128)(2,1)S(1)} %collective-permute-done.1.refs_2_), channel_id=1, source_target_pairs={{0,1},{1,0},{2,3},{3,2},{4,5},{5,4},{6,7},{7,6},{8,9},{9,8},{10,11... | collective-permute-start | bytes 307208 | tf_op jit(solution)/shard_map/ppermute | solution.py:87
  17.8 1.4 %collective-permute-start.12 = (bf16[8,6400]{1,0:T(8,128)(2,1)S(1)}, bf16[8,6400]{1,0:T(8,128)(2,1)S(1)}, u32[]{:S(2)}, u32[]{:S(2)}) collective-permute-start(bf16[8,6400]{1,0:T(8,128)(2,1)S(1)} %collective-permute-done.4.refs_5_), channel_id=1, source_target_pairs={{0,1},{1,0},{2,3},{3,2},{4,5},{5,4},{6,7},{7,6},{8,9},{9,8},{10,11... | collective-permute-start | bytes 307208 | tf_op jit(solution)/shard_map/ppermute | solution.py:87
  17.8 1.4 %collective-permute-start.13 = (bf16[8,6400]{1,0:T(8,128)(2,1)S(1)}, bf16[8,6400]{1,0:T(8,128)(2,1)S(1)}, u32[]{:S(2)}, u32[]{:S(2)}) collective-permute-start(bf16[8,6400]{1,0:T(8,128)(2,1)S(1)} %collective-permute-done.5.refs_6_), channel_id=1, source_target_pairs={{0,1},{1,0},{2,3},{3,2},{4,5},{5,4},{6,7},{7,6},{8,9},{9,8},{10,11... | collective-permute-start | bytes 307208 | tf_op jit(solution)/shard_map/ppermute | solution.py:87
  18.3 1.3 %collective-permute-start.14 = (bf16[8,6400]{1,0:T(8,128)(2,1)S(1)}, bf16[8,6400]{1,0:T(8,128)(2,1)S(1)}, u32[]{:S(2)}, u32[]{:S(2)}) collective-permute-start(bf16[8,6400]{1,0:T(8,128)(2,1)S(1)} %collective-permute-done.6.refs_7_), channel_id=1, source_target_pairs={{0,1},{1,0},{2,3},{3,2},{4,5},{5,4},{6,7},{7,6},{8,9},{9,8},{10,11... | collective-permute-start | bytes 307208 | tf_op jit(solution)/shard_map/ppermute | solution.py:87
  26.4 18.7 %copy-start.5 = (s32[8,1]{0,1:T(1,128)S(1)}, s32[8,1]{0,1:T(1,128)}, u32[]{:S(2)}) copy-start(s32[8,1]{0,1:T(1,128)} %param.9) | copy-start | bytes 100
  26.4 23.3 %copy-start.3 = (bf16[8,6400]{1,0:T(8,128)(2,1)S(1)}, bf16[8,6400]{1,0:T(8,128)(2,1)}, u32[]{:S(2)}) copy-start(bf16[8,6400]{1,0:T(8,128)(2,1)} %refs_0_.1) | copy-start | bytes 307204
  30.7 1.4 %collective-permute-start.23 = (bf16[8,6400]{1,0:T(8,128)(2,1)S(1)}, bf16[8,6400]{1,0:T(8,128)(2,1)S(1)}, u32[]{:S(2)}, u32[]{:S(2)}) collective-permute-start(bf16[8,6400]{1,0:T(8,128)(2,1)S(1)} %get-tuple-element.32), channel_id=1, source_target_pairs={{0,1},{1,0},{2,3},{3,2},{4,5},{5,4},{6,7},{7,6},{8,9},{9,8},{10,11... | collective-permute-start | bytes 307208 | tf_op jit(solution)/shard_map/ppermute | solution.py:87
  30.9 1.4 %collective-permute-start.25 = (bf16[8,6400]{1,0:T(8,128)(2,1)S(1)}, bf16[8,6400]{1,0:T(8,128)(2,1)S(1)}, u32[]{:S(2)}, u32[]{:S(2)}) collective-permute-start(bf16[8,6400]{1,0:T(8,128)(2,1)S(1)} %get-tuple-element.34), channel_id=1, source_target_pairs={{0,1},{1,0},{2,3},{3,2},{4,5},{5,4},{6,7},{7,6},{8,9},{9,8},{10,11... | collective-permute-start | bytes 307208 | tf_op jit(solution)/shard_map/ppermute | solution.py:87
  31.3 1.4 %collective-permute-start.27 = (bf16[8,6400]{1,0:T(8,128)(2,1)S(1)}, bf16[8,6400]{1,0:T(8,128)(2,1)S(1)}, u32[]{:S(2)}, u32[]{:S(2)}) collective-permute-start(bf16[8,6400]{1,0:T(8,128)(2,1)S(1)} %get-tuple-element.36), channel_id=1, source_target_pairs={{0,1},{1,0},{2,3},{3,2},{4,5},{5,4},{6,7},{7,6},{8,9},{9,8},{10,11... | collective-permute-start | bytes 307208 | tf_op jit(solution)/shard_map/ppermute | solution.py:87
  31.4 5.4 %collective-permute-start.22 = (bf16[8,6400]{1,0:T(8,128)(2,1)S(1)}, bf16[8,6400]{1,0:T(8,128)(2,1)S(1)}, u32[]{:S(2)}, u32[]{:S(2)}) collective-permute-start(bf16[8,6400]{1,0:T(8,128)(2,1)S(1)} %get-tuple-element.30), channel_id=1, source_target_pairs={{0,1},{1,0},{2,3},{3,2},{4,5},{5,4},{6,7},{7,6},{8,9},{9,8},{10,11... | collective-permute-start | bytes 307208 | tf_op jit(solution)/shard_map/ppermute | solution.py:87
  31.8 1.3 %collective-permute-start.16 = (bf16[8,6400]{1,0:T(8,128)(2,1)S(1)}, bf16[8,6400]{1,0:T(8,128)(2,1)S(1)}, u32[]{:S(2)}, u32[]{:S(2)}) collective-permute-start(bf16[8,6400]{1,0:T(8,128)(2,1)S(1)} %get-tuple-element.24), channel_id=1, source_target_pairs={{0,1},{1,0},{2,3},{3,2},{4,5},{5,4},{6,7},{7,6},{8,9},{9,8},{10,11... | collective-permute-start | bytes 307208 | tf_op jit(solution)/shard_map/ppermute | solution.py:87
  32.1 2.6 %collective-permute-start.18 = (bf16[8,6400]{1,0:T(8,128)(2,1)S(1)}, bf16[8,6400]{1,0:T(8,128)(2,1)S(1)}, u32[]{:S(2)}, u32[]{:S(2)}) collective-permute-start(bf16[8,6400]{1,0:T(8,128)(2,1)S(1)} %get-tuple-element.26), channel_id=1, source_target_pairs={{0,1},{1,0},{2,3},{3,2},{4,5},{5,4},{6,7},{7,6},{8,9},{9,8},{10,11... | collective-permute-start | bytes 307208 | tf_op jit(solution)/shard_map/ppermute | solution.py:87
  32.4 3.8 %collective-permute-start.20 = (bf16[8,6400]{1,0:T(8,128)(2,1)S(1)}, bf16[8,6400]{1,0:T(8,128)(2,1)S(1)}, u32[]{:S(2)}, u32[]{:S(2)}) collective-permute-start(bf16[8,6400]{1,0:T(8,128)(2,1)S(1)} %get-tuple-element.28), channel_id=1, source_target_pairs={{0,1},{1,0},{2,3},{3,2},{4,5},{5,4},{6,7},{7,6},{8,9},{9,8},{10,11... | collective-permute-start | bytes 307208 | tf_op jit(solution)/shard_map/ppermute | solution.py:87
  32.7 12.3 %collective-permute-start.15 = (bf16[8,6400]{1,0:T(8,128)(2,1)S(1)}, bf16[8,6400]{1,0:T(8,128)(2,1)S(1)}, u32[]{:S(2)}, u32[]{:S(2)}) collective-permute-start(bf16[8,6400]{1,0:T(8,128)(2,1)S(1)} %get-tuple-element.22), channel_id=1, source_target_pairs={{0,1},{1,0},{2,3},{3,2},{4,5},{5,4},{6,7},{7,6},{8,9},{9,8},{10,11... | collective-permute-start | bytes 307208 | tf_op jit(solution)/shard_map/ppermute | solution.py:87
  33.1 6.6 %collective-permute-start.24 = (bf16[8,6400]{1,0:T(8,128)(2,1)S(1)}, bf16[8,6400]{1,0:T(8,128)(2,1)S(1)}, u32[]{:S(2)}, u32[]{:S(2)}) collective-permute-start(bf16[8,6400]{1,0:T(8,128)(2,1)S(1)} %add_convert_fusion.4), channel_id=1, source_target_pairs={{0,6},{1,7},{2,4},{3,5},{4,2},{5,3},{6,0},{7,1},{8,14},{9,15},{10,... | collective-permute-start | bytes 307208 | tf_op jit(solution)/shard_map/ppermute | solution.py:87
  34.6 7.3 %collective-permute-start.26 = (bf16[8,6400]{1,0:T(8,128)(2,1)S(1)}, bf16[8,6400]{1,0:T(8,128)(2,1)S(1)}, u32[]{:S(2)}, u32[]{:S(2)}) collective-permute-start(bf16[8,6400]{1,0:T(8,128)(2,1)S(1)} %add_convert_fusion.3), channel_id=1, source_target_pairs={{0,4},{1,5},{2,6},{3,7},{4,0},{5,1},{6,2},{7,3},{8,12},{9,13},{10,... | collective-permute-start | bytes 307208 | tf_op jit(solution)/shard_map/ppermute | solution.py:87
  36.2 6.3 %collective-permute-start.28 = (bf16[8,6400]{1,0:T(8,128)(2,1)S(1)}, bf16[8,6400]{1,0:T(8,128)(2,1)S(1)}, u32[]{:S(2)}, u32[]{:S(2)}) collective-permute-start(bf16[8,6400]{1,0:T(8,128)(2,1)S(1)} %add_convert_fusion.2), channel_id=1, source_target_pairs={{0,2},{1,3},{2,0},{3,1},{4,6},{5,7},{6,4},{7,5},{8,10},{9,11},{10,... | collective-permute-start | bytes 307208 | tf_op jit(solution)/shard_map/ppermute | solution.py:87
  36.9 8.2 %collective-permute-start.17 = (bf16[8,6400]{1,0:T(8,128)(2,1)S(1)}, bf16[8,6400]{1,0:T(8,128)(2,1)S(1)}, u32[]{:S(2)}, u32[]{:S(2)}) collective-permute-start(bf16[8,6400]{1,0:T(8,128)(2,1)S(1)} %add_convert_fusion.7), channel_id=1, source_target_pairs={{0,6},{1,7},{2,4},{3,5},{4,2},{5,3},{6,0},{7,1},{8,14},{9,15},{10,... | collective-permute-start | bytes 307208 | tf_op jit(solution)/shard_map/ppermute | solution.py:87
  39.8 6.9 %collective-permute-start.19 = (bf16[8,6400]{1,0:T(8,128)(2,1)S(1)}, bf16[8,6400]{1,0:T(8,128)(2,1)S(1)}, u32[]{:S(2)}, u32[]{:S(2)}) collective-permute-start(bf16[8,6400]{1,0:T(8,128)(2,1)S(1)} %add_convert_fusion.6), channel_id=1, source_target_pairs={{0,4},{1,5},{2,6},{3,7},{4,0},{5,1},{6,2},{7,3},{8,12},{9,13},{10,... | collective-permute-start | bytes 307208 | tf_op jit(solution)/shard_map/ppermute | solution.py:87
  41.9 4.8 %collective-permute-start.21 = (bf16[8,6400]{1,0:T(8,128)(2,1)S(1)}, bf16[8,6400]{1,0:T(8,128)(2,1)S(1)}, u32[]{:S(2)}, u32[]{:S(2)}) collective-permute-start(bf16[8,6400]{1,0:T(8,128)(2,1)S(1)} %add_convert_fusion.5), channel_id=1, source_target_pairs={{0,2},{1,3},{2,0},{3,1},{4,6},{5,7},{6,4},{7,5},{8,10},{9,11},{10,... | collective-permute-start | bytes 307208 | tf_op jit(solution)/shard_map/ppermute | solution.py:87
  42.6 7.1 %collective-permute-start.29 = (bf16[8,6400]{1,0:T(8,128)(2,1)S(1)}, bf16[8,6400]{1,0:T(8,128)(2,1)S(1)}, u32[]{:S(2)}, u32[]{:S(2)}) collective-permute-start(bf16[8,6400]{1,0:T(8,128)(2,1)S(1)} %add_convert_fusion.1), channel_id=1, source_target_pairs={{0,8},{1,9},{2,10},{3,11},{4,12},{5,13},{6,14},{7,15},{8,0},{9,1},... | collective-permute-start | bytes 307208 | tf_op jit(solution)/shard_map/ppermute | solution.py:87
  (4 other events, 6.8 us)

commit v3 on v2

v3 whole, which is shorter than its diff:
```python
import functools

import jax
import jax.numpy as jnp
from jax import lax
from jax.experimental import pallas as pl
from jax.experimental.pallas import tpu as pltpu
from jax.sharding import PartitionSpec as P


def pick_chunk(width, most):
    chunk = most
    while width % chunk:
        chunk -= 128
    return chunk


def fetch_kernel(count, *refs):
    sources, targets, sems = refs[:count], refs[count + 1 : -1], refs[-1]
    moves = [pltpu.make_async_copy(a, b, sems.at[k]) for k, (a, b) in enumerate(zip(sources, targets))]
    for move in moves:
        move.start()
    for move in moves:
        move.wait()


def fetched(arrays, after):
    count = len(arrays)
    arrays = [pltpu.with_memory_space_constraint(x, pltpu.HBM) for x in arrays]
    size = sum(x.size * x.dtype.itemsize for x in arrays)
    return pl.pallas_call(
        functools.partial(fetch_kernel, count),
        out_shape=[jax.ShapeDtypeStruct(x.shape, x.dtype) for x in arrays],
        in_specs=[pl.BlockSpec(memory_space=pltpu.HBM)] * count + [pl.BlockSpec(memory_space=pl.ANY)],
        out_specs=[pl.BlockSpec(memory_space=pl.ANY)] * count,
        scratch_shapes=[pltpu.SemaphoreType.DMA((count,))],
        compiler_params=pltpu.CompilerParams(vmem_limit_bytes=1024 * 1024),
        cost_estimate=pl.CostEstimate(flops=0, bytes_accessed=size, transcendentals=0),
    )(*arrays, after)


def expert_kernel(copies, count, *refs):
    block_refs, refs = refs[:count], refs[count:]
    gain_ref, router_ref, up_ref, down_far = refs[:4]
    out_refs, (down_held, normed_ref, sems) = refs[4 : 4 + count], refs[4 + count :]
    tok_rows, width = block_refs[0].shape
    units = down_far.shape[0]
    chunk = pick_chunk(width, 1280)
    steps = range(0, width, chunk)
    piece = units // 3
    waits = []
    for k in range(3):
        window = pl.ds(k * piece, piece)
        waits.append(pltpu.make_async_copy(down_far.at[window], down_held.at[window], sems.at[k]))
        waits[-1].start()
    pairs = [(first, block_refs[first : first + 2]) for first in range(0, count, 2)]

    def load(pair, at):
        return jnp.concatenate([ref[:, at : at + chunk].astype(jnp.float32) for ref in pair], axis=0)

    factors = []
    for first, pair in pairs:
        total = jnp.zeros((2 * tok_rows, chunk), jnp.float32)
        for at in steps:
            values = load(pair, at)
            total = total + values * values
        mean_square = jnp.sum(total, axis=1, keepdims=True) * (1.0 / width)
        factors.append(lax.rsqrt(mean_square + 1e-06))
    nt = (((1,), (1,)), ((), ()))
    for at in steps:
        lines = [gain_ref[j : j + 1, :] for j in range(at // 128, (at + chunk) // 128)]
        gain = jnp.concatenate(lines, axis=1)
        for factor, (first, pair) in zip(factors, pairs):
            normed = load(pair, at) * factor * gain
            normed_ref[first * tok_rows : (first + 2) * tok_rows, at : at + chunk] = normed.astype(jnp.bfloat16)
    logits = lax.dot_general(normed_ref[...], router_ref[...], nt, preferred_element_type=jnp.float32)
    lifted = lax.dot_general(normed_ref[...], up_ref[...], nt, preferred_element_type=jnp.float32)
    own = lax.axis_index("expert") // copies
    columns = lax.broadcasted_iota(jnp.int32, logits.shape, 1)
    logit = jnp.sum(jnp.where(columns == own, logits, 0.0), axis=1, keepdims=True)
    scores = 1.0 / (1.0 + jnp.exp(-logit))
    gate, up = lifted[:, :units], lifted[:, units:]
    act = (gate / (1.0 + jnp.exp(-gate)) * up).astype(jnp.bfloat16)
    for move in waits:
        move.wait()
    for at in steps:
        output = jnp.dot(act, down_held[:, at : at + chunk], preferred_element_type=jnp.float32) * scores
        for k in range(count):
            out_refs[k][:, at : at + chunk] = output[k * tok_rows : (k + 1) * tok_rows].astype(jnp.bfloat16)


def expert_rows(blocks, norm_gain, router, gate_up, down_w, copies):
    count = len(blocks)
    tok_rows, width = blocks[0].shape
    units = down_w.shape[0]
    rows = count * tok_rows
    vmem = pl.BlockSpec(memory_space=pltpu.VMEM)
    return pl.pallas_call(
        functools.partial(expert_kernel, copies, count),
        out_shape=[jax.ShapeDtypeStruct((tok_rows, width), jnp.bfloat16)] * count,
        in_specs=[vmem] * (count + 3) + [pl.BlockSpec(memory_space=pltpu.HBM)],
        out_specs=[vmem] * count,
        scratch_shapes=[
            pltpu.VMEM(down_w.shape, jnp.bfloat16),
            pltpu.VMEM((rows, width), jnp.bfloat16),
            pltpu.SemaphoreType.DMA((3,)),
        ],
        compiler_params=pltpu.CompilerParams(vmem_limit_bytes=32 * 1024 * 1024),
        cost_estimate=pl.CostEstimate(
            flops=6 * rows * width * units,
            bytes_accessed=6 * units * width,
            transcendentals=rows * units,
        ),
    )(*blocks, norm_gain, router, gate_up, pltpu.with_memory_space_constraint(down_w, pltpu.HBM))


def body(hidden_in, norm_gain, router, routes, routed_gate_up, routed_down):
    axis_len = lax.axis_size("expert")
    experts = router.shape[1]
    copies = axis_len // experts
    own_expert = lax.axis_index("expert") // copies
    chips = list(range(2, copies, 2))[::-1]
    size = len(chips) + 1

    def swap(block, mask):
        return lax.ppermute(block, "expert", [(i, i ^ mask) for i in range(axis_len)])

    far = [swap(hidden_in, copies * k) for k in range(1, experts)]
    mine = [[source] + [swap(source, mask) for mask in chips] for source in [hidden_in] + far]
    local = [routed_gate_up[0].T, router.T, norm_gain.reshape(-1, 128), hidden_in]
    gate_up, router_t, gain, mine[0][0] = fetched(local, mine[0][-1])
    gate_up, mine[0][1:], mine[1:] = lax.optimization_barrier((gate_up, mine[0][1:], mine[1:]))
    theirs = [[swap(block, 1) for block in group] for group in [[hidden_in] + mine[0][1:]] + mine[1:]]
    outs = expert_rows(sum(mine, []) + sum(theirs, []), gain, router_t, gate_up, routed_down[0], copies)
    kept = [outs[k * size : (k + 1) * size] for k in range(experts)]
    given = [outs[(experts + k) * size : (experts + k + 1) * size] for k in range(experts)]

    def both_cores(own_parts, given_parts):
        back = [swap(part, 1) for part in given_parts]
        both = [a.astype(jnp.float32) + b.astype(jnp.float32) for a, b in zip(own_parts, back)]
        return both[:1] + [part.astype(jnp.bfloat16) for part in both[1:]]

    def fold(both):
        total = both[0]
        for part, mask in zip(both[1:], chips):
            total = total + swap(part, mask).astype(jnp.float32)
        return total

    sums = [fold(both_cores(kept[k], given[k])).astype(jnp.bfloat16) for k in range(1, experts)]
    near = both_cores(kept[0], given[0])
    sums, near[3:] = lax.optimization_barrier((sums, near[3:]))
    near = fold(near)
    chosen = near
    for k, total in enumerate(sums, start=1):
        arrived = swap(total, copies * k).astype(jnp.float32)
        chosen = jnp.where(routes == jnp.bitwise_xor(own_expert, k), arrived, chosen)
    return (hidden_in.astype(jnp.float32) + chosen).astype(jnp.bfloat16)


def solution(mesh):
    placed = (
        P(("groups", "expert"), None),
        P(),
        P(),
        P(("groups", "expert"), None),
        P("expert", None, None),
        P("expert", None, None),
    )
    return jax.shard_map(
        body, mesh=mesh, in_specs=placed, out_specs=P(("groups", "expert"), None), check_vma=False
    )
```

time: 50.8 us -> 44.7 us (0.88)
  local copies, waits for them, and re-layouts: 7.54 us -> 0.01 us
  Pallas kernels: 4.35 us -> 7.57 us
  waiting for transfers between devices: 13.5 us -> 11.6 us
    unnamed x12 -> x4, local copies, waits for them, and re-layouts: 6.78 us -> 0.01 us
    pallas_call x0 -> x1, Pallas kernels: none -> 3.13 us  [fetched(): pl.pallas_call(functools.partial(fetch_kernel, count), out_shape=[jax.Sha...]
    ppermute x30, waiting for transfers between devices: 13.5 us -> 11.6 us  [swap(): lax.ppermute(block, 'expert', [(i, i ^ mask) for i in range(axis_len)])]
    broadcast_in_dim x1 -> x0, local copies, waits for them, and re-layouts: 0.77 us -> none  [expert_rows(): norm_gain[None, :]]
  transfers between devices with their start and end apart: 30 -> 30, of which waited for: 13 -> 15; matrix products, arithmetic and copies ran while one was open for 2% -> 1% of each run, Pallas kernels for 0% -> 7%
where the time goes in v3:
time: 44.7 us; the launch traced here: 44.5 us
  starting transfers between devices  24.2 us (54%)
  waiting for transfers between devices  11.6 us (26%)
  Pallas kernels  7.57 us (17%)
  other arithmetic  0.99 us (2%)
    ppermute x30, starting transfers between devices, swap(): lax.ppermute(block, 'expert', [(i, i ^ mask) for i in range(axis_len)])  24.2 us
    ppermute x30, waiting for transfers between devices, swap(): lax.ppermute(block, 'expert', [(i, i ^ mask) for i in range(axis_len)])  11.6 us
    pallas_call x1, Pallas kernels, expert_rows(): pl.pallas_call(functools.partial(expert_kernel, copies, count), out_shape...  4.43 us
    pallas_call x1, Pallas kernels, fetched(): pl.pallas_call(functools.partial(fetch_kernel, count), out_shape=[jax.Sha...  3.13 us
  transfers between devices with their start and end apart: 30, of which 15 were waited for; matrix products, arithmetic and copies ran while one was open for 1% of the time, Pallas kernels for 7%

profile of v3, /device:TPU:0, one launch (start us, length us, event | category | flops | bytes accessed | tf_op | source)
XLA Modules:
  0.0 44.5 jit_solution(8934987427873732175)
XLA Ops:
  0.0 4.0 %collective-permute-start.3 = (bf16[8,6400]{1,0:T(8,128)(2,1)}, bf16[8,6400]{1,0:T(8,128)(2,1)S(1)}, u32[]{:S(2)}, u32[]{:S(2)}) collective-permute-start(bf16[8,6400]{1,0:T(8,128)(2,1)} %refs_3_.1), channel_id=1, source_target_pairs={{0,8},{1,9},{2,10},{3,11},{4,12},{5,13},{6,14},{7,15},{8,0},{9,1},... | collective-permute-start | bytes 307208 | tf_op jit(solution)/shard_map/ppermute | solution.py:126
  4.0 1.5 %collective-permute-start = (bf16[8,6400]{1,0:T(8,128)(2,1)}, bf16[8,6400]{1,0:T(8,128)(2,1)S(1)}, u32[]{:S(2)}, u32[]{:S(2)}) collective-permute-start(bf16[8,6400]{1,0:T(8,128)(2,1)} %refs_3_.1), channel_id=1, source_target_pairs={{0,2},{1,3},{2,0},{3,1},{4,6},{5,7},{6,4},{7,5},{8,10},{9,11},{10,... | collective-permute-start | bytes 307208 | tf_op jit(solution)/shard_map/ppermute | solution.py:126
  5.6 1.5 %collective-permute-start.1 = (bf16[8,6400]{1,0:T(8,128)(2,1)}, bf16[8,6400]{1,0:T(8,128)(2,1)S(1)}, u32[]{:S(2)}, u32[]{:S(2)}) collective-permute-start(bf16[8,6400]{1,0:T(8,128)(2,1)} %refs_3_.1), channel_id=1, source_target_pairs={{0,6},{1,7},{2,4},{3,5},{4,2},{5,3},{6,0},{7,1},{8,14},{9,15},{10,... | collective-permute-start | bytes 307208 | tf_op jit(solution)/shard_map/ppermute | solution.py:126
  7.1 0.4 %collective-permute-start.2 = (bf16[8,6400]{1,0:T(8,128)(2,1)}, bf16[8,6400]{1,0:T(8,128)(2,1)S(1)}, u32[]{:S(2)}, u32[]{:S(2)}) collective-permute-start(bf16[8,6400]{1,0:T(8,128)(2,1)} %refs_3_.1), channel_id=1, source_target_pairs={{0,4},{1,5},{2,6},{3,7},{4,0},{5,1},{6,2},{7,3},{8,12},{9,13},{10,... | collective-permute-start | bytes 307208 | tf_op jit(solution)/shard_map/ppermute | solution.py:126
  7.5 2.0 %collective-permute-done.3.refs_4_ = bf16[8,6400]{1,0:T(8,128)(2,1)S(1)} collective-permute-done((bf16[8,6400]{1,0:T(8,128)(2,1)}, bf16[8,6400]{1,0:T(8,128)(2,1)S(1)}, u32[]{:S(2)}, u32[]{:S(2)}) %collective-permute-start.3) | collective-permute-done | bytes 102432 | tf_op jit(solution)/shard_map/ppermute | solution.py:126
  9.5 1.7 %collective-permute-start.4 = (bf16[8,6400]{1,0:T(8,128)(2,1)S(1)}, bf16[8,6400]{1,0:T(8,128)(2,1)S(1)}, u32[]{:S(2)}, u32[]{:S(2)}) collective-permute-start(bf16[8,6400]{1,0:T(8,128)(2,1)S(1)} %collective-permute-done.3.refs_4_), channel_id=1, source_target_pairs={{0,6},{1,7},{2,4},{3,5},{4,2},{5,3},{6,0},{7,1},{8,14},{9,15},{10,... | collective-permute-start | bytes 307208 | tf_op jit(solution)/shard_map/ppermute | solution.py:126
  11.2 1.3 %collective-permute-start.5 = (bf16[8,6400]{1,0:T(8,128)(2,1)S(1)}, bf16[8,6400]{1,0:T(8,128)(2,1)S(1)}, u32[]{:S(2)}, u32[]{:S(2)}) collective-permute-start(bf16[8,6400]{1,0:T(8,128)(2,1)S(1)} %collective-permute-done.3.refs_4_), channel_id=1, source_target_pairs={{0,4},{1,5},{2,6},{3,7},{4,0},{5,1},{6,2},{7,3},{8,12},{9,13},{10,... | collective-permute-start | bytes 307208 | tf_op jit(solution)/shard_map/ppermute | solution.py:126
  12.5 0.5 %collective-permute-start.6 = (bf16[8,6400]{1,0:T(8,128)(2,1)S(1)}, bf16[8,6400]{1,0:T(8,128)(2,1)S(1)}, u32[]{:S(2)}, u32[]{:S(2)}) collective-permute-start(bf16[8,6400]{1,0:T(8,128)(2,1)S(1)} %collective-permute-done.3.refs_4_), channel_id=1, source_target_pairs={{0,2},{1,3},{2,0},{3,1},{4,6},{5,7},{6,4},{7,5},{8,10},{9,11},{10,... | collective-permute-start | bytes 307208 | tf_op jit(solution)/shard_map/ppermute | solution.py:126
  13.0 3.1 %shard_map.64 = (bf16[576,6400]{1,0:T(8,128)(2,1)S(1)}, bf16[2,6400]{1,0:T(2,128)(2,1)S(1)}, f32[50,128]{1,0:T(8,128)S(1)}, bf16[8,6400]{1,0:T(8,128)(2,1)S(1)}) custom-call(bf16[576,6400]{1,0:T(8,128)(2,1)} %bitcast.8, bf16[2,6400]{1,0:T(2,128)(2,1)} %bitcast.11, f32[50,128]{1,0:T(8,128)} %bitcast.10, bf16[8,6400]{1,0:T(8,128)(2,1)} %refs_3_.1, ...), custom_call_target="tpu_custom_call" | custom-call | bytes 7526400 | tf_op jit(solution)/shard_map/pallas_call | solution.py:31
  16.2 0.9 %collective-permute-done.4.refs_5_ = bf16[8,6400]{1,0:T(8,128)(2,1)S(1)} collective-permute-done((bf16[8,6400]{1,0:T(8,128)(2,1)S(1)}, bf16[8,6400]{1,0:T(8,128)(2,1)S(1)}, u32[]{:S(2)}, u32[]{:S(2)}) %collective-permute-start.4) | collective-permute-done | bytes 102432 | tf_op jit(solution)/shard_map/ppermute | solution.py:126
  17.1 0.3 collective-permute-done.5.refs_6_
  17.4 0.3 collective-permute-done.6.refs_7_
  17.7 0.5 %collective-permute-start.11 = (bf16[8,6400]{1,0:T(8,128)(2,1)S(1)}, bf16[8,6400]{1,0:T(8,128)(2,1)S(1)}, u32[]{:S(2)}, u32[]{:S(2)}) collective-permute-start(bf16[8,6400]{1,0:T(8,128)(2,1)S(1)} %collective-permute-done.3.refs_4_), channel_id=1, source_target_pairs={{0,1},{1,0},{2,3},{3,2},{4,5},{5,4},{6,7},{7,6},{8,9},{9,8},{10,11... | collective-permute-start | bytes 307208 | tf_op jit(solution)/shard_map/ppermute | solution.py:126
  18.2 0.5 %collective-permute-start.13 = (bf16[8,6400]{1,0:T(8,128)(2,1)S(1)}, bf16[8,6400]{1,0:T(8,128)(2,1)S(1)}, u32[]{:S(2)}, u32[]{:S(2)}) collective-permute-start(bf16[8,6400]{1,0:T(8,128)(2,1)S(1)} %collective-permute-done.5.refs_6_), channel_id=1, source_target_pairs={{0,1},{1,0},{2,3},{3,2},{4,5},{5,4},{6,7},{7,6},{8,9},{9,8},{10,11... | collective-permute-start | bytes 307208 | tf_op jit(solution)/shard_map/ppermute | solution.py:126
  19.2 0.3 collective-permute-start.9
  19.6 0.4 collective-permute-done.14.refs_15_
  20.0 0.3 collective-permute-done.8.refs_9_
  20.5 4.4 %shard_map.65 = (bf16[8,6400]{1,0:T(8,128)(2,1)S(1)}, bf16[8,6400]{1,0:T(8,128)(2,1)S(1)}, bf16[8,6400]{1,0:T(8,128)(2,1)S(1)}, bf16[8,6400]{1,0:T(8,128)(2,1)S(...) custom-call(bf16[8,6400]{1,0:T(8,128)(2,1)S(1)} %get-tuple-element.3, ...), custom_call_target="tpu_custom_call" | custom-call | flops 1415577600 | bytes 11059200 | tf_op jit(solution)/shard_map/pallas_call | solution.py:98
  25.0 0.3 collective-permute-start.25
  26.7 0.3 collective-permute-start.15
  27.4 1.4 %collective-permute-start.17 = (bf16[8,6400]{1,0:T(8,128)(2,1)S(1)}, bf16[8,6400]{1,0:T(8,128)(2,1)S(1)}, u32[]{:S(2)}, u32[]{:S(2)}) collective-permute-start(bf16[8,6400]{1,0:T(8,128)(2,1)S(1)} %add_convert_fusion.7), channel_id=1, source_target_pairs={{0,6},{1,7},{2,4},{3,5},{4,2},{5,3},{6,0},{7,1},{8,14},{9,15},{10,... | collective-permute-start | bytes 307208 | tf_op jit(solution)/shard_map/ppermute | solution.py:126
  28.9 1.4 %collective-permute-start.19 = (bf16[8,6400]{1,0:T(8,128)(2,1)S(1)}, bf16[8,6400]{1,0:T(8,128)(2,1)S(1)}, u32[]{:S(2)}, u32[]{:S(2)}) collective-permute-start(bf16[8,6400]{1,0:T(8,128)(2,1)S(1)} %add_convert_fusion.6), channel_id=1, source_target_pairs={{0,4},{1,5},{2,6},{3,7},{4,0},{5,1},{6,2},{7,3},{8,12},{9,13},{10,... | collective-permute-start | bytes 307208 | tf_op jit(solution)/shard_map/ppermute | solution.py:126
  30.3 0.9 %collective-permute-start.21 = (bf16[8,6400]{1,0:T(8,128)(2,1)S(1)}, bf16[8,6400]{1,0:T(8,128)(2,1)S(1)}, u32[]{:S(2)}, u32[]{:S(2)}) collective-permute-start(bf16[8,6400]{1,0:T(8,128)(2,1)S(1)} %add_convert_fusion.5), channel_id=1, source_target_pairs={{0,2},{1,3},{2,0},{3,1},{4,6},{5,7},{6,4},{7,5},{8,10},{9,11},{10,... | collective-permute-start | bytes 307208 | tf_op jit(solution)/shard_map/ppermute | solution.py:126
  31.2 1.4 %collective-permute-start.26 = (bf16[8,6400]{1,0:T(8,128)(2,1)S(1)}, bf16[8,6400]{1,0:T(8,128)(2,1)S(1)}, u32[]{:S(2)}, u32[]{:S(2)}) collective-permute-start(bf16[8,6400]{1,0:T(8,128)(2,1)S(1)} %add_convert_fusion.2), channel_id=1, source_target_pairs={{0,6},{1,7},{2,4},{3,5},{4,2},{5,3},{6,0},{7,1},{8,14},{9,15},{10,... | collective-permute-start | bytes 307208 | tf_op jit(solution)/shard_map/ppermute | solution.py:126
  32.6 1.4 %collective-permute-done.17 = bf16[8,6400]{1,0:T(8,128)(2,1)S(1)} collective-permute-done((bf16[8,6400]{1,0:T(8,128)(2,1)S(1)}, bf16[8,6400]{1,0:T(8,128)(2,1)S(1)}, u32[]{:S(2)}, u32[]{:S(2)}) %collective-permute-start.17) | collective-permute-done | bytes 102432 | tf_op jit(solution)/shard_map/ppermute | solution.py:126
  34.1 1.2 %collective-permute-start.28 = (bf16[8,6400]{1,0:T(8,128)(2,1)S(1)}, bf16[8,6400]{1,0:T(8,128)(2,1)S(1)}, u32[]{:S(2)}, u32[]{:S(2)}) collective-permute-start(bf16[8,6400]{1,0:T(8,128)(2,1)S(1)} %add_convert_fusion.1), channel_id=1, source_target_pairs={{0,4},{1,5},{2,6},{3,7},{4,0},{5,1},{6,2},{7,3},{8,12},{9,13},{10,... | collective-permute-start | bytes 307208 | tf_op jit(solution)/shard_map/ppermute | solution.py:126
  35.3 0.7 %collective-permute-done.19 = bf16[8,6400]{1,0:T(8,128)(2,1)S(1)} collective-permute-done((bf16[8,6400]{1,0:T(8,128)(2,1)S(1)}, bf16[8,6400]{1,0:T(8,128)(2,1)S(1)}, u32[]{:S(2)}, u32[]{:S(2)}) %collective-permute-start.19) | collective-permute-done | bytes 102432 | tf_op jit(solution)/shard_map/ppermute | solution.py:126
  36.3 2.0 %collective-permute-start.23 = (bf16[8,6400]{1,0:T(8,128)(2,1)S(1)}, bf16[8,6400]{1,0:T(8,128)(2,1)S(1)}, u32[]{:S(2)}, u32[]{:S(2)}) collective-permute-start(bf16[8,6400]{1,0:T(8,128)(2,1)S(1)} %add_convert_fusion.4), channel_id=1, source_target_pairs={{0,8},{1,9},{2,10},{3,11},{4,12},{5,13},{6,14},{7,15},{8,0},{9,1},... | collective-permute-start | bytes 307208 | tf_op jit(solution)/shard_map/ppermute | solution.py:126
  38.3 1.1 %collective-permute-start.29 = (bf16[8,6400]{1,0:T(8,128)(2,1)S(1)}, bf16[8,6400]{1,0:T(8,128)(2,1)S(1)}, u32[]{:S(2)}, u32[]{:S(2)}) collective-permute-start(bf16[8,6400]{1,0:T(8,128)(2,1)S(1)} %add_convert_fusion.3), channel_id=1, source_target_pairs={{0,2},{1,3},{2,0},{3,1},{4,6},{5,7},{6,4},{7,5},{8,10},{9,11},{10,... | collective-permute-start | bytes 307208 | tf_op jit(solution)/shard_map/ppermute | solution.py:126
  39.5 1.4 %collective-permute-done.28 = bf16[8,6400]{1,0:T(8,128)(2,1)S(1)} collective-permute-done((bf16[8,6400]{1,0:T(8,128)(2,1)S(1)}, bf16[8,6400]{1,0:T(8,128)(2,1)S(1)}, u32[]{:S(2)}, u32[]{:S(2)}) %collective-permute-start.28) | collective-permute-done | bytes 102432 | tf_op jit(solution)/shard_map/ppermute | solution.py:126
  40.9 2.8 %collective-permute-done.23 = bf16[8,6400]{1,0:T(8,128)(2,1)S(1)} collective-permute-done((bf16[8,6400]{1,0:T(8,128)(2,1)S(1)}, bf16[8,6400]{1,0:T(8,128)(2,1)S(1)}, u32[]{:S(2)}, u32[]{:S(2)}) %collective-permute-start.23) | collective-permute-done | bytes 102432 | tf_op jit(solution)/shard_map/ppermute | solution.py:126
  43.8 0.8 %add_convert_fusion = bf16[8,6400]{1,0:T(8,128)(2,1)} fusion(bf16[8,6400]{1,0:T(8,128)(2,1)S(1)} %collective-permute-done.29, bf16[8,6400]{1,0:T(8,128)(2,1)S(1)} %collective-permute-done.28, bf16[8,6400]{1,0:T(8,128)(2,1)S(1)} %collective-permute-done.26, bf16[8,6400]{1,0:T(8,128)(2,1)S(1)} %collective-permute-done.24, ...), kind=kLoop, calls=%fused_computation | loop fusion | flops 716800 | bytes 819208 | tf_op jit(solution)/shard_map/convert_element_type | solution.py:157
  (43 shorter events, 3.1 us)
Async XLA Ops:
  0.0 16.1 %copy-start = (bf16[8,6400]{1,0:T(8,128)(2,1)S(1)}, bf16[8,6400]{1,0:T(8,128)(2,1)}, u32[]{:S(2)}) copy-start(bf16[8,6400]{1,0:T(8,128)(2,1)} %refs_3_.1) | copy-start | bytes 307204
  0.0 9.5 %collective-permute-start.3 = (bf16[8,6400]{1,0:T(8,128)(2,1)}, bf16[8,6400]{1,0:T(8,128)(2,1)S(1)}, u32[]{:S(2)}, u32[]{:S(2)}) collective-permute-start(bf16[8,6400]{1,0:T(8,128)(2,1)} %refs_3_.1), channel_id=1, source_target_pairs={{0,8},{1,9},{2,10},{3,11},{4,12},{5,13},{6,14},{7,15},{8,0},{9,1},... | collective-permute-start | bytes 307208 | tf_op jit(solution)/shard_map/ppermute | solution.py:126
  4.0 8.4 %collective-permute-start = (bf16[8,6400]{1,0:T(8,128)(2,1)}, bf16[8,6400]{1,0:T(8,128)(2,1)S(1)}, u32[]{:S(2)}, u32[]{:S(2)}) collective-permute-start(bf16[8,6400]{1,0:T(8,128)(2,1)} %refs_3_.1), channel_id=1, source_target_pairs={{0,2},{1,3},{2,0},{3,1},{4,6},{5,7},{6,4},{7,5},{8,10},{9,11},{10,... | collective-permute-start | bytes 307208 | tf_op jit(solution)/shard_map/ppermute | solution.py:126
  5.6 10.6 %collective-permute-start.1 = (bf16[8,6400]{1,0:T(8,128)(2,1)}, bf16[8,6400]{1,0:T(8,128)(2,1)S(1)}, u32[]{:S(2)}, u32[]{:S(2)}) collective-permute-start(bf16[8,6400]{1,0:T(8,128)(2,1)} %refs_3_.1), channel_id=1, source_target_pairs={{0,6},{1,7},{2,4},{3,5},{4,2},{5,3},{6,0},{7,1},{8,14},{9,15},{10,... | collective-permute-start | bytes 307208 | tf_op jit(solution)/shard_map/ppermute | solution.py:126
  7.1 9.2 %collective-permute-start.2 = (bf16[8,6400]{1,0:T(8,128)(2,1)}, bf16[8,6400]{1,0:T(8,128)(2,1)S(1)}, u32[]{:S(2)}, u32[]{:S(2)}) collective-permute-start(bf16[8,6400]{1,0:T(8,128)(2,1)} %refs_3_.1), channel_id=1, source_target_pairs={{0,4},{1,5},{2,6},{3,7},{4,0},{5,1},{6,2},{7,3},{8,12},{9,13},{10,... | collective-permute-start | bytes 307208 | tf_op jit(solution)/shard_map/ppermute | solution.py:126
  9.5 7.6 %collective-permute-start.4 = (bf16[8,6400]{1,0:T(8,128)(2,1)S(1)}, bf16[8,6400]{1,0:T(8,128)(2,1)S(1)}, u32[]{:S(2)}, u32[]{:S(2)}) collective-permute-start(bf16[8,6400]{1,0:T(8,128)(2,1)S(1)} %collective-permute-done.3.refs_4_), channel_id=1, source_target_pairs={{0,6},{1,7},{2,4},{3,5},{4,2},{5,3},{6,0},{7,1},{8,14},{9,15},{10,... | collective-permute-start | bytes 307208 | tf_op jit(solution)/shard_map/ppermute | solution.py:126
  11.2 6.2 %collective-permute-start.5 = (bf16[8,6400]{1,0:T(8,128)(2,1)S(1)}, bf16[8,6400]{1,0:T(8,128)(2,1)S(1)}, u32[]{:S(2)}, u32[]{:S(2)}) collective-permute-start(bf16[8,6400]{1,0:T(8,128)(2,1)S(1)} %collective-permute-done.3.refs_4_), channel_id=1, source_target_pairs={{0,4},{1,5},{2,6},{3,7},{4,0},{5,1},{6,2},{7,3},{8,12},{9,13},{10,... | collective-permute-start | bytes 307208 | tf_op jit(solution)/shard_map/ppermute | solution.py:126
  12.5 5.2 %collective-permute-start.6 = (bf16[8,6400]{1,0:T(8,128)(2,1)S(1)}, bf16[8,6400]{1,0:T(8,128)(2,1)S(1)}, u32[]{:S(2)}, u32[]{:S(2)}) collective-permute-start(bf16[8,6400]{1,0:T(8,128)(2,1)S(1)} %collective-permute-done.3.refs_4_), channel_id=1, source_target_pairs={{0,2},{1,3},{2,0},{3,1},{4,6},{5,7},{6,4},{7,5},{8,10},{9,11},{10,... | collective-permute-start | bytes 307208 | tf_op jit(solution)/shard_map/ppermute | solution.py:126
  16.1 2.5 %collective-permute-start.7 = (bf16[8,6400]{1,0:T(8,128)(2,1)S(1)}, bf16[8,6400]{1,0:T(8,128)(2,1)S(1)}, u32[]{:S(2)}, u32[]{:S(2)}) collective-permute-start(bf16[8,6400]{1,0:T(8,128)(2,1)S(1)} %copy-done), channel_id=1, source_target_pairs={{0,1},{1,0},{2,3},{3,2},{4,5},{5,4},{6,7},{7,6},{8,9},{9,8},{10,11... | collective-permute-start | bytes 307208 | tf_op jit(solution)/shard_map/ppermute | solution.py:126
  17.7 1.3 %collective-permute-start.10 = (bf16[8,6400]{1,0:T(8,128)(2,1)S(1)}, bf16[8,6400]{1,0:T(8,128)(2,1)S(1)}, u32[]{:S(2)}, u32[]{:S(2)}) collective-permute-start(bf16[8,6400]{1,0:T(8,128)(2,1)S(1)} %collective-permute-done.refs_4_.refs_3_), channel_id=1, source_target_pairs={{0,1},{1,0},{2,3},{3,2},{4,5},{5,4},{6,7},{7,6},{8,9},{9,8},{10,11... | collective-permute-start | bytes 307208 | tf_op jit(solution)/shard_map/ppermute | solution.py:126
  17.7 1.5 %collective-permute-start.11 = (bf16[8,6400]{1,0:T(8,128)(2,1)S(1)}, bf16[8,6400]{1,0:T(8,128)(2,1)S(1)}, u32[]{:S(2)}, u32[]{:S(2)}) collective-permute-start(bf16[8,6400]{1,0:T(8,128)(2,1)S(1)} %collective-permute-done.3.refs_4_), channel_id=1, source_target_pairs={{0,1},{1,0},{2,3},{3,2},{4,5},{5,4},{6,7},{7,6},{8,9},{9,8},{10,11... | collective-permute-start | bytes 307208 | tf_op jit(solution)/shard_map/ppermute | solution.py:126
  18.2 1.3 %collective-permute-start.12 = (bf16[8,6400]{1,0:T(8,128)(2,1)S(1)}, bf16[8,6400]{1,0:T(8,128)(2,1)S(1)}, u32[]{:S(2)}, u32[]{:S(2)}) collective-permute-start(bf16[8,6400]{1,0:T(8,128)(2,1)S(1)} %collective-permute-done.4.refs_5_), channel_id=1, source_target_pairs={{0,1},{1,0},{2,3},{3,2},{4,5},{5,4},{6,7},{7,6},{8,9},{9,8},{10,11... | collective-permute-start | bytes 307208 | tf_op jit(solution)/shard_map/ppermute | solution.py:126
  18.2 1.5 %collective-permute-start.13 = (bf16[8,6400]{1,0:T(8,128)(2,1)S(1)}, bf16[8,6400]{1,0:T(8,128)(2,1)S(1)}, u32[]{:S(2)}, u32[]{:S(2)}) collective-permute-start(bf16[8,6400]{1,0:T(8,128)(2,1)S(1)} %collective-permute-done.5.refs_6_), channel_id=1, source_target_pairs={{0,1},{1,0},{2,3},{3,2},{4,5},{5,4},{6,7},{7,6},{8,9},{9,8},{10,11... | collective-permute-start | bytes 307208 | tf_op jit(solution)/shard_map/ppermute | solution.py:126
  18.7 1.3 %collective-permute-start.14 = (bf16[8,6400]{1,0:T(8,128)(2,1)S(1)}, bf16[8,6400]{1,0:T(8,128)(2,1)S(1)}, u32[]{:S(2)}, u32[]{:S(2)}) collective-permute-start(bf16[8,6400]{1,0:T(8,128)(2,1)S(1)} %collective-permute-done.6.refs_7_), channel_id=1, source_target_pairs={{0,1},{1,0},{2,3},{3,2},{4,5},{5,4},{6,7},{7,6},{8,9},{9,8},{10,11... | collective-permute-start | bytes 307208 | tf_op jit(solution)/shard_map/ppermute | solution.py:126
  19.0 1.3 %collective-permute-start.8 = (bf16[8,6400]{1,0:T(8,128)(2,1)S(1)}, bf16[8,6400]{1,0:T(8,128)(2,1)S(1)}, u32[]{:S(2)}, u32[]{:S(2)}) collective-permute-start(bf16[8,6400]{1,0:T(8,128)(2,1)S(1)} %collective-permute-done.1.refs_1_), channel_id=1, source_target_pairs={{0,1},{1,0},{2,3},{3,2},{4,5},{5,4},{6,7},{7,6},{8,9},{9,8},{10,11... | collective-permute-start | bytes 307208 | tf_op jit(solution)/shard_map/ppermute | solution.py:126
  19.2 1.3 %collective-permute-start.9 = (bf16[8,6400]{1,0:T(8,128)(2,1)S(1)}, bf16[8,6400]{1,0:T(8,128)(2,1)S(1)}, u32[]{:S(2)}, u32[]{:S(2)}) collective-permute-start(bf16[8,6400]{1,0:T(8,128)(2,1)S(1)} %collective-permute-done.2.refs_2_), channel_id=1, source_target_pairs={{0,1},{1,0},{2,3},{3,2},{4,5},{5,4},{6,7},{7,6},{8,9},{9,8},{10,11... | collective-permute-start | bytes 307208 | tf_op jit(solution)/shard_map/ppermute | solution.py:126
  20.5 18.9 %copy-start.1 = (s32[8,1]{0,1:T(1,128)S(1)}, s32[8,1]{0,1:T(1,128)}, u32[]{:S(2)}) copy-start(s32[8,1]{0,1:T(1,128)} %param.9) | copy-start | bytes 100
  25.0 1.4 %collective-permute-start.25 = (bf16[8,6400]{1,0:T(8,128)(2,1)S(1)}, bf16[8,6400]{1,0:T(8,128)(2,1)S(1)}, u32[]{:S(2)}, u32[]{:S(2)}) collective-permute-start(bf16[8,6400]{1,0:T(8,128)(2,1)S(1)} %get-tuple-element.61), channel_id=1, source_target_pairs={{0,1},{1,0},{2,3},{3,2},{4,5},{5,4},{6,7},{7,6},{8,9},{9,8},{10,11... | collective-permute-start | bytes 307208 | tf_op jit(solution)/shard_map/ppermute | solution.py:126
  25.3 1.3 %collective-permute-start.27 = (bf16[8,6400]{1,0:T(8,128)(2,1)S(1)}, bf16[8,6400]{1,0:T(8,128)(2,1)S(1)}, u32[]{:S(2)}, u32[]{:S(2)}) collective-permute-start(bf16[8,6400]{1,0:T(8,128)(2,1)S(1)} %get-tuple-element.63), channel_id=1, source_target_pairs={{0,1},{1,0},{2,3},{3,2},{4,5},{5,4},{6,7},{7,6},{8,9},{9,8},{10,11... | collective-permute-start | bytes 307208 | tf_op jit(solution)/shard_map/ppermute | solution.py:126
  25.5 4.8 %collective-permute-start.22 = (bf16[8,6400]{1,0:T(8,128)(2,1)S(1)}, bf16[8,6400]{1,0:T(8,128)(2,1)S(1)}, u32[]{:S(2)}, u32[]{:S(2)}) collective-permute-start(bf16[8,6400]{1,0:T(8,128)(2,1)S(1)} %get-tuple-element.56), channel_id=1, source_target_pairs={{0,1},{1,0},{2,3},{3,2},{4,5},{5,4},{6,7},{7,6},{8,9},{9,8},{10,11... | collective-permute-start | bytes 307208 | tf_op jit(solution)/shard_map/ppermute | solution.py:126
  25.8 1.3 %collective-permute-start.16 = (bf16[8,6400]{1,0:T(8,128)(2,1)S(1)}, bf16[8,6400]{1,0:T(8,128)(2,1)S(1)}, u32[]{:S(2)}, u32[]{:S(2)}) collective-permute-start(bf16[8,6400]{1,0:T(8,128)(2,1)S(1)} %get-tuple-element.50), channel_id=1, source_target_pairs={{0,1},{1,0},{2,3},{3,2},{4,5},{5,4},{6,7},{7,6},{8,9},{9,8},{10,11... | collective-permute-start | bytes 307208 | tf_op jit(solution)/shard_map/ppermute | solution.py:126
  26.1 1.3 %collective-permute-start.18 = (bf16[8,6400]{1,0:T(8,128)(2,1)S(1)}, bf16[8,6400]{1,0:T(8,128)(2,1)S(1)}, u32[]{:S(2)}, u32[]{:S(2)}) collective-permute-start(bf16[8,6400]{1,0:T(8,128)(2,1)S(1)} %get-tuple-element.52), channel_id=1, source_target_pairs={{0,1},{1,0},{2,3},{3,2},{4,5},{5,4},{6,7},{7,6},{8,9},{9,8},{10,11... | collective-permute-start | bytes 307208 | tf_op jit(solution)/shard_map/ppermute | solution.py:126
  26.3 2.5 %collective-permute-start.20 = (bf16[8,6400]{1,0:T(8,128)(2,1)S(1)}, bf16[8,6400]{1,0:T(8,128)(2,1)S(1)}, u32[]{:S(2)}, u32[]{:S(2)}) collective-permute-start(bf16[8,6400]{1,0:T(8,128)(2,1)S(1)} %get-tuple-element.54), channel_id=1, source_target_pairs={{0,1},{1,0},{2,3},{3,2},{4,5},{5,4},{6,7},{7,6},{8,9},{9,8},{10,11... | collective-permute-start | bytes 307208 | tf_op jit(solution)/shard_map/ppermute | solution.py:126
  26.7 4.5 %collective-permute-start.15 = (bf16[8,6400]{1,0:T(8,128)(2,1)S(1)}, bf16[8,6400]{1,0:T(8,128)(2,1)S(1)}, u32[]{:S(2)}, u32[]{:S(2)}) collective-permute-start(bf16[8,6400]{1,0:T(8,128)(2,1)S(1)} %get-tuple-element.48), channel_id=1, source_target_pairs={{0,1},{1,0},{2,3},{3,2},{4,5},{5,4},{6,7},{7,6},{8,9},{9,8},{10,11... | collective-permute-start | bytes 307208 | tf_op jit(solution)/shard_map/ppermute | solution.py:126
  27.1 12.3 %collective-permute-start.24 = (bf16[8,6400]{1,0:T(8,128)(2,1)S(1)}, bf16[8,6400]{1,0:T(8,128)(2,1)S(1)}, u32[]{:S(2)}, u32[]{:S(2)}) collective-permute-start(bf16[8,6400]{1,0:T(8,128)(2,1)S(1)} %get-tuple-element.59), channel_id=1, source_target_pairs={{0,1},{1,0},{2,3},{3,2},{4,5},{5,4},{6,7},{7,6},{8,9},{9,8},{10,11... | collective-permute-start | bytes 307208 | tf_op jit(solution)/shard_map/ppermute | solution.py:126
  27.4 6.7 %collective-permute-start.17 = (bf16[8,6400]{1,0:T(8,128)(2,1)S(1)}, bf16[8,6400]{1,0:T(8,128)(2,1)S(1)}, u32[]{:S(2)}, u32[]{:S(2)}) collective-permute-start(bf16[8,6400]{1,0:T(8,128)(2,1)S(1)} %add_convert_fusion.7), channel_id=1, source_target_pairs={{0,6},{1,7},{2,4},{3,5},{4,2},{5,3},{6,0},{7,1},{8,14},{9,15},{10,... | collective-permute-start | bytes 307208 | tf_op jit(solution)/shard_map/ppermute | solution.py:126
  28.9 7.2 %collective-permute-start.19 = (bf16[8,6400]{1,0:T(8,128)(2,1)S(1)}, bf16[8,6400]{1,0:T(8,128)(2,1)S(1)}, u32[]{:S(2)}, u32[]{:S(2)}) collective-permute-start(bf16[8,6400]{1,0:T(8,128)(2,1)S(1)} %add_convert_fusion.6), channel_id=1, source_target_pairs={{0,4},{1,5},{2,6},{3,7},{4,0},{5,1},{6,2},{7,3},{8,12},{9,13},{10,... | collective-permute-start | bytes 307208 | tf_op jit(solution)/shard_map/ppermute | solution.py:126
  30.3 6.0 %collective-permute-start.21 = (bf16[8,6400]{1,0:T(8,128)(2,1)S(1)}, bf16[8,6400]{1,0:T(8,128)(2,1)S(1)}, u32[]{:S(2)}, u32[]{:S(2)}) collective-permute-start(bf16[8,6400]{1,0:T(8,128)(2,1)S(1)} %add_convert_fusion.5), channel_id=1, source_target_pairs={{0,2},{1,3},{2,0},{3,1},{4,6},{5,7},{6,4},{7,5},{8,10},{9,11},{10,... | collective-permute-start | bytes 307208 | tf_op jit(solution)/shard_map/ppermute | solution.py:126
  31.2 8.3 %collective-permute-start.26 = (bf16[8,6400]{1,0:T(8,128)(2,1)S(1)}, bf16[8,6400]{1,0:T(8,128)(2,1)S(1)}, u32[]{:S(2)}, u32[]{:S(2)}) collective-permute-start(bf16[8,6400]{1,0:T(8,128)(2,1)S(1)} %add_convert_fusion.2), channel_id=1, source_target_pairs={{0,6},{1,7},{2,4},{3,5},{4,2},{5,3},{6,0},{7,1},{8,14},{9,15},{10,... | collective-permute-start | bytes 307208 | tf_op jit(solution)/shard_map/ppermute | solution.py:126
  34.1 6.8 %collective-permute-start.28 = (bf16[8,6400]{1,0:T(8,128)(2,1)S(1)}, bf16[8,6400]{1,0:T(8,128)(2,1)S(1)}, u32[]{:S(2)}, u32[]{:S(2)}) collective-permute-start(bf16[8,6400]{1,0:T(8,128)(2,1)S(1)} %add_convert_fusion.1), channel_id=1, source_target_pairs={{0,4},{1,5},{2,6},{3,7},{4,0},{5,1},{6,2},{7,3},{8,12},{9,13},{10,... | collective-permute-start | bytes 307208 | tf_op jit(solution)/shard_map/ppermute | solution.py:126
  36.3 7.4 %collective-permute-start.23 = (bf16[8,6400]{1,0:T(8,128)(2,1)S(1)}, bf16[8,6400]{1,0:T(8,128)(2,1)S(1)}, u32[]{:S(2)}, u32[]{:S(2)}) collective-permute-start(bf16[8,6400]{1,0:T(8,128)(2,1)S(1)} %add_convert_fusion.4), channel_id=1, source_target_pairs={{0,8},{1,9},{2,10},{3,11},{4,12},{5,13},{6,14},{7,15},{8,0},{9,1},... | collective-permute-start | bytes 307208 | tf_op jit(solution)/shard_map/ppermute | solution.py:126
  38.3 5.4 %collective-permute-start.29 = (bf16[8,6400]{1,0:T(8,128)(2,1)S(1)}, bf16[8,6400]{1,0:T(8,128)(2,1)S(1)}, u32[]{:S(2)}, u32[]{:S(2)}) collective-permute-start(bf16[8,6400]{1,0:T(8,128)(2,1)S(1)} %add_convert_fusion.3), channel_id=1, source_target_pairs={{0,2},{1,3},{2,0},{3,1},{4,6},{5,7},{6,4},{7,5},{8,10},{9,11},{10,... | collective-permute-start | bytes 307208 | tf_op jit(solution)/shard_map/ppermute | solution.py:126

commit v4 on v3

v4 whole, which is shorter than its diff:
```python
import functools

import jax
import jax.numpy as jnp
from jax import lax
from jax.experimental import pallas as pl
from jax.experimental.pallas import tpu as pltpu
from jax.sharding import PartitionSpec as P


def fold_of(tok_rows, width):
    slots = max(2, 3 * tok_rows // 4)
    per = -(-slots // (tok_rows - slots))
    rest = width // (per + 1) // 128 * 128
    return slots, per, width - rest


def folded(main, rest, slots, per):
    spare = []
    for first in range(0, slots, per):
        lines = [rest[k : k + 1] for k in range(first, min(first + per, slots))]
        pad = main.shape[1] - len(lines) * rest.shape[1]
        spare.append(jnp.concatenate(lines + [jnp.zeros((1, pad), jnp.float32)], axis=1))
    return jnp.concatenate([main[:slots]] + spare, axis=0)


def unfolded(load, tok_rows, rest, slots, per):
    lines = []
    for k in range(slots):
        at = k % per * rest
        lines.append(load(at, rest)[slots + k // per : slots + k // per + 1])
    return jnp.concatenate(lines + [jnp.zeros((tok_rows - slots, rest), jnp.float32)], axis=0)


def places(routes_ref, tok_rows):
    shape = (tok_rows, tok_rows)
    row = jnp.broadcast_to(routes_ref[...], shape)
    down = lax.broadcasted_iota(jnp.int32, shape, 0)
    across = lax.broadcasted_iota(jnp.int32, shape, 1)
    column = jnp.sum(jnp.where(down == across, row, 0), axis=1, keepdims=True)
    same = column == row
    rank_row = jnp.sum(jnp.where(same & (down < across), 1, 0), axis=0, keepdims=True)
    rank_column = jnp.sum(jnp.where(same & (across < down), 1, 0), axis=1, keepdims=True)
    return row, column, rank_row, rank_column, down, across


def pack_kernel(copies, experts, routes_far, hidden_far, *refs):
    out_refs, (routes_ref, hidden_ref, packed_ref, sems) = refs[:experts], refs[experts:]
    moves = [(routes_far, routes_ref), (hidden_far, hidden_ref)]
    moves = [pltpu.make_async_copy(x, y, sems.at[k]) for k, (x, y) in enumerate(moves)]
    for move in moves:
        move.start()
    tok_rows, width = hidden_ref.shape
    slots, per, stay = fold_of(tok_rows, width)
    own = lax.axis_index("expert") // copies
    moves[0].wait()
    row, _, rank, _, down, _ = places(routes_ref, tok_rows)
    picks = []
    for k in range(experts):
        expert = jnp.bitwise_xor(own, k)
        picks.append(jnp.where((row == expert) & (rank == down) & (down < slots), 1.0, 0.0))
    pick = jnp.concatenate(picks, axis=0).astype(jnp.bfloat16)
    moves[1].wait()
    sorted_rows = jnp.dot(pick, hidden_ref[...], preferred_element_type=jnp.float32)
    lasts = []
    for k in range(experts)[::-1]:
        rows = sorted_rows[k * tok_rows : (k + 1) * tok_rows]
        packed_ref[k] = folded(rows[:, :stay], rows[:, stay:], slots, per).astype(jnp.bfloat16)
        lasts.append(pltpu.make_async_copy(packed_ref.at[k], out_refs[k], sems.at[2 + k]))
        lasts[-1].start()
    for last in lasts:
        last.wait()


def packed_rows(routes, hidden_in, copies, experts):
    tok_rows, width = hidden_in.shape
    stay = fold_of(tok_rows, width)[2]
    far = [pltpu.with_memory_space_constraint(x, pltpu.HBM) for x in (routes, hidden_in)]
    return pl.pallas_call(
        functools.partial(pack_kernel, copies, experts),
        out_shape=[jax.ShapeDtypeStruct((tok_rows, stay), jnp.bfloat16)] * experts,
        in_specs=[pl.BlockSpec(memory_space=pltpu.HBM)] * 2,
        out_specs=[pl.BlockSpec(memory_space=pl.ANY)] * experts,
        scratch_shapes=[
            pltpu.VMEM(routes.shape, jnp.int32),
            pltpu.VMEM(hidden_in.shape, jnp.bfloat16),
            pltpu.VMEM((experts, tok_rows, stay), jnp.bfloat16),
            pltpu.SemaphoreType.DMA((2 + experts,)),
        ],
        compiler_params=pltpu.CompilerParams(vmem_limit_bytes=8 * 1024 * 1024),
    )(*far)


def final_kernel(copies, experts, count, routes_far, hidden_far, *refs):
    far_refs, near_refs, refs = refs[: experts - 1], refs[experts - 1 : experts - 1 + count], refs[experts - 1 + count :]
    out_ref, routes_ref, hidden_ref, sems = refs
    moves = [(routes_far, routes_ref), (hidden_far, hidden_ref)]
    moves = [pltpu.make_async_copy(x, y, sems.at[k]) for k, (x, y) in enumerate(moves)]
    for move in moves:
        move.start()
    tok_rows, width = hidden_ref.shape
    slots, per, stay = fold_of(tok_rows, width)
    near = near_refs[0][...]
    for ref in near_refs[1:]:
        near = near + ref[...].astype(jnp.float32)
    parts = []
    for values in [near] + [ref[...].astype(jnp.float32) for ref in far_refs]:
        rest = unfolded(lambda at, size: values[:, at : at + size], tok_rows, width - stay, slots, per)
        parts.append(jnp.concatenate([values[:, :stay], rest], axis=1))
    own = lax.axis_index("expert") // copies
    moves[0].wait()
    _, column, _, rank, _, across = places(routes_ref, tok_rows)
    picks = []
    for k in range(experts):
        expert = jnp.bitwise_xor(own, k)
        picks.append(jnp.where((column == expert) & (rank == across) & (across < slots), 1.0, 0.0))
    pick = jnp.concatenate(picks, axis=1).astype(jnp.bfloat16)
    rows = jnp.concatenate(parts, axis=0).astype(jnp.bfloat16)
    routed = jnp.dot(pick, rows, preferred_element_type=jnp.float32)
    moves[1].wait()
    out_ref[...] = (hidden_ref[...].astype(jnp.float32) + routed).astype(jnp.bfloat16)


def placed_rows(routes, hidden_in, far_parts, near_parts, copies):
    experts = len(far_parts) + 1
    vmem = pl.BlockSpec(memory_space=pltpu.VMEM)
    return pl.pallas_call(
        functools.partial(final_kernel, copies, experts, len(near_parts)),
        out_shape=jax.ShapeDtypeStruct(hidden_in.shape, jnp.bfloat16),
        in_specs=[pl.BlockSpec(memory_space=pl.ANY)] * 2 + [vmem] * (len(far_parts) + len(near_parts)),
        out_specs=vmem,
        scratch_shapes=[
            pltpu.VMEM(routes.shape, jnp.int32),
            pltpu.VMEM(hidden_in.shape, jnp.bfloat16),
            pltpu.SemaphoreType.DMA((2,)),
        ],
        compiler_params=pltpu.CompilerParams(vmem_limit_bytes=8 * 1024 * 1024),
    )(routes, hidden_in, *far_parts, *near_parts)


def fetch_kernel(count, *refs):
    sources, targets, sems = refs[:count], refs[count + 1 : -1], refs[-1]
    moves = [pltpu.make_async_copy(a, b, sems.at[k]) for k, (a, b) in enumerate(zip(sources, targets))]
    for move in moves:
        move.start()
    for move in moves:
        move.wait()


def fetched(arrays, after):
    count = len(arrays)
    arrays = [pltpu.with_memory_space_constraint(x, pltpu.HBM) for x in arrays]
    size = sum(x.size * x.dtype.itemsize for x in arrays)
    return pl.pallas_call(
        functools.partial(fetch_kernel, count),
        out_shape=[jax.ShapeDtypeStruct(x.shape, x.dtype) for x in arrays],
        in_specs=[pl.BlockSpec(memory_space=pltpu.HBM)] * count + [pl.BlockSpec(memory_space=pl.ANY)],
        out_specs=[pl.BlockSpec(memory_space=pl.ANY)] * count,
        scratch_shapes=[pltpu.SemaphoreType.DMA((count,))],
        compiler_params=pltpu.CompilerParams(vmem_limit_bytes=1024 * 1024),
        cost_estimate=pl.CostEstimate(flops=0, bytes_accessed=size, transcendentals=0),
    )(*arrays, after)


def expert_kernel(copies, count, *refs):
    block_refs, refs = refs[:count], refs[count:]
    gain_ref, router_ref, up_ref, down_far = refs[:4]
    out_refs, (down_held, normed_ref, rest_ref, sems) = refs[4 : 4 + count], refs[4 + count :]
    tok_rows, width = block_refs[0].shape[0], down_far.shape[1]
    units = down_far.shape[0]
    slots, per, stay = fold_of(tok_rows, width)
    rest = width - stay
    parts = ((0, stay // 2), (stay // 2, stay // 2), (stay, rest)) if stay % 256 == 0 else ((0, stay), (stay, rest))
    piece = units
    waits = []
    for k in range(1):
        window = pl.ds(k * piece, piece)
        waits.append(pltpu.make_async_copy(down_far.at[window], down_held.at[window], sems.at[k]))
        waits[-1].start()
    pairs = [(first, block_refs[first : first + 2]) for first in range(0, count, 2)]

    def load(pair, at, size):
        return jnp.concatenate([ref[:, at : at + size].astype(jnp.float32) for ref in pair], axis=0)

    def unfold(ref):
        def window(at, size):
            return ref[:, at : at + size].astype(jnp.float32)

        return unfolded(window, tok_rows, rest, slots, per)

    factors = []
    for first, pair in pairs:
        values = jnp.concatenate([unfold(ref) for ref in pair], axis=0)
        rest_ref[first * tok_rows : (first + 2) * tok_rows, :] = values.astype(jnp.bfloat16)
        total = jnp.sum(values * values, axis=1, keepdims=True)
        for at, size in parts[:-1]:
            values = load(pair, at, size)
            total = total + jnp.sum(values * values, axis=1, keepdims=True)
        factors.append(lax.rsqrt(total * (1.0 / width) + 1e-06))
    nt = (((1,), (1,)), ((), ()))
    for at, size in parts:
        lines = [gain_ref[j : j + 1, :] for j in range(at // 128, (at + size) // 128)]
        gain = jnp.concatenate(lines, axis=1)
        for factor, (first, pair) in zip(factors, pairs):
            rows = slice(first * tok_rows, (first + 2) * tok_rows)
            values = load(pair, at, size) if at < stay else rest_ref[rows, :].astype(jnp.float32)
            normed_ref[rows, at : at + size] = (values * factor * gain).astype(jnp.bfloat16)
    logits = lax.dot_general(normed_ref[...], router_ref[...], nt, preferred_element_type=jnp.float32)
    lifted = lax.dot_general(normed_ref[...], up_ref[...], nt, preferred_element_type=jnp.float32)
    own = lax.axis_index("expert") // copies
    columns = lax.broadcasted_iota(jnp.int32, logits.shape, 1)
    logit = jnp.sum(jnp.where(columns == own, logits, 0.0), axis=1, keepdims=True)
    scores = 1.0 / (1.0 + jnp.exp(-logit))
    gate, up = lifted[:, :units], lifted[:, units:]
    act = (gate / (1.0 + jnp.exp(-gate)) * up).astype(jnp.bfloat16)
    for move in waits:
        move.wait()
    main = jnp.dot(act, down_held[:, :stay], preferred_element_type=jnp.float32) * scores
    ends = jnp.dot(act, down_held[:, stay:], preferred_element_type=jnp.float32) * scores
    for k in range(count):
        rows = slice(k * tok_rows, (k + 1) * tok_rows)
        out_refs[k][...] = folded(main[rows], ends[rows], slots, per).astype(jnp.bfloat16)


def expert_rows(blocks, norm_gain, router, gate_up, down_w, copies):
    count = len(blocks)
    tok_rows, width = blocks[0].shape[0], down_w.shape[1]
    units = down_w.shape[0]
    rows = count * tok_rows
    vmem = pl.BlockSpec(memory_space=pltpu.VMEM)
    return pl.pallas_call(
        functools.partial(expert_kernel, copies, count),
        out_shape=[jax.ShapeDtypeStruct(x.shape, jnp.bfloat16) for x in blocks],
        in_specs=[vmem] * (count + 3) + [pl.BlockSpec(memory_space=pltpu.HBM)],
        out_specs=[vmem] * count,
        scratch_shapes=[
            pltpu.VMEM(down_w.shape, jnp.bfloat16),
            pltpu.VMEM((rows, width), jnp.bfloat16),
            pltpu.VMEM((rows, width - blocks[0].shape[1]), jnp.bfloat16),
            pltpu.SemaphoreType.DMA((1,)),
        ],
        compiler_params=pltpu.CompilerParams(vmem_limit_bytes=32 * 1024 * 1024),
        cost_estimate=pl.CostEstimate(
            flops=6 * rows * width * units,
            bytes_accessed=6 * units * width,
            transcendentals=rows * units,
        ),
    )(*blocks, norm_gain, router, gate_up, pltpu.with_memory_space_constraint(down_w, pltpu.HBM))


def body(hidden_in, norm_gain, router, routes, routed_gate_up, routed_down):
    axis_len = lax.axis_size("expert")
    experts = router.shape[1]
    copies = axis_len // experts
    chips = list(range(2, copies, 2))[::-1]
    size = len(chips) + 1

    def swap(block, mask):
        return lax.ppermute(block, "expert", [(i, i ^ mask) for i in range(axis_len)])

    sources = list(packed_rows(routes.T, hidden_in, copies, experts))
    sources[1:] = [swap(sources[k], copies * k) for k in range(1, experts)]
    mine = [[source] + [swap(source, mask) for mask in chips] for source in sources]
    local = [routed_gate_up[0].T, router.T, norm_gain.reshape(-1, 128)]
    gate_up, router_t, gain = fetched(local, mine[0][-1])
    late = (mine[0][1:], [group[1:] for group in mine[1:]])
    gate_up, late = lax.optimization_barrier((gate_up, late))
    mine[0][1:] = late[0]
    for group, blocks in zip(mine[1:], late[1]):
        group[1:] = blocks
    theirs = [[swap(block, 1) for block in group] for group in mine]
    outs = expert_rows(sum(mine, []) + sum(theirs, []), gain, router_t, gate_up, routed_down[0], copies)
    kept = [outs[k * size : (k + 1) * size] for k in range(experts)]
    given = [outs[(experts + k) * size : (experts + k + 1) * size] for k in range(experts)]

    def both_cores(own_parts, given_parts):
        back = [swap(part, 1) for part in given_parts]
        both = [a.astype(jnp.float32) + b.astype(jnp.float32) for a, b in zip(own_parts, back)]
        return both[:1] + [part.astype(jnp.bfloat16) for part in both[1:]]

    def fold(both):
        total = both[0]
        for part, mask in zip(both[1:], chips):
            total = total + swap(part, mask).astype(jnp.float32)
        return total

    far_both = [both_cores(kept[k], given[k]) for k in range(1, experts)]
    firsts = [both[1] for both in far_both]
    firsts, given[0] = lax.optimization_barrier((firsts, given[0]))
    far_both = [both[:1] + [first] + both[2:] for both, first in zip(far_both, firsts)]
    sums = [fold(both).astype(jnp.bfloat16) for both in far_both]
    near = both_cores(kept[0], given[0])
    sums, near[3:] = lax.optimization_barrier((sums, near[3:]))
    near[1:] = [swap(part, mask) for part, mask in zip(near[1:], chips)]
    far_parts = [swap(total, copies * k) for k, total in enumerate(sums, start=1)]
    return placed_rows(routes.T, hidden_in, far_parts, near, copies)


def solution(mesh):
    placed = (
        P(("groups", "expert"), None),
        P(),
        P(),
        P(("groups", "expert"), None),
        P("expert", None, None),
        P("expert", None, None),
    )
    return jax.shard_map(
        body, mesh=mesh, in_specs=placed, out_specs=P(("groups", "expert"), None), check_vma=False
    )
```

time: 44.7 us -> 43.8 us (0.980)
  waiting for transfers between devices: 11.6 us -> 6.78 us
  Pallas kernels: 7.57 us -> 11.1 us
  starting transfers between devices: 24.2 us -> 25.4 us
  other arithmetic: 0.99 us -> 0.2 us
    ppermute x30, waiting for transfers between devices: 11.6 us -> 6.78 us  [swap(): lax.ppermute(block, 'expert', [(i, i ^ mask) for i in range(axis_len)])]
    pallas_call x0 -> x2, Pallas kernels: none -> 2.68 us  [the longest x1 1.37 us: packed_rows(): pl.pallas_call(functools.partial(pack_kernel, copies, experts), out_shape...]
    ppermute x30, starting transfers between devices: 24.2 us -> 25.4 us  [swap(): lax.ppermute(block, 'expert', [(i, i ^ mask) for i in range(axis_len)])]
    pallas_call x1, Pallas kernels: 4.43 us -> 5.29 us  [expert_rows(): pl.pallas_call(functools.partial(expert_kernel, copies, count), out_shape...]
    convert_element_type x2 -> x1, other arithmetic: 0.82 us -> 0.05 us  [body(): sums = [fold(both).astype(jnp.bfloat16) for both in far_both]]
  transfers between devices with their start and end apart: 30 -> 30, of which waited for: 15 -> 13; matrix products, arithmetic and copies ran while one was open for 1% -> 0% of each run, Pallas kernels for 7% -> 7%
where the time goes in v4:
time: 43.8 us; the launch traced here: 43.7 us
  starting transfers between devices  25.4 us (58%)
  Pallas kernels  11.1 us (25%)
  waiting for transfers between devices  6.78 us (15%)
    ppermute x30, starting transfers between devices, swap(): lax.ppermute(block, 'expert', [(i, i ^ mask) for i in range(axis_len)])  25.4 us
    ppermute x30, waiting for transfers between devices, swap(): lax.ppermute(block, 'expert', [(i, i ^ mask) for i in range(axis_len)])  6.78 us
    pallas_call x1, Pallas kernels, expert_rows(): pl.pallas_call(functools.partial(expert_kernel, copies, count), out_shape...  5.29 us
    pallas_call x1, Pallas kernels, fetched(): pl.pallas_call(functools.partial(fetch_kernel, count), out_shape=[jax.Sha...  3.12 us
    pallas_call x1, Pallas kernels, packed_rows(): pl.pallas_call(functools.partial(pack_kernel, copies, experts), out_shape...  1.37 us
    pallas_call x1, Pallas kernels, placed_rows(): pl.pallas_call(functools.partial(final_kernel, copies, experts, len(near_...  1.32 us
  transfers between devices with their start and end apart: 30, of which 13 were waited for; matrix products, arithmetic and copies ran while one was open for 0% of the time, Pallas kernels for 7%

profile of v4, /device:TPU:0, one launch (start us, length us, event | category | flops | bytes accessed | tf_op | source)
XLA Modules:
  0.0 43.7 jit_solution(17830234927718172154)
XLA Ops:
  0.0 1.4 %shard_map.64 = (bf16[8,4864]{1,0:T(8,128)(2,1)S(1)}, bf16[8,4864]{1,0:T(8,128)(2,1)S(1)}) custom-call(s32[1,8]{1,0:T(1,128)} %bitcast.7, bf16[8,6400]{1,0:T(8,128)(2,1)} %hidden_far.3), custom_call_target="tpu_custom_call" | custom-call | tf_op jit(solution)/shard_map/pallas_call | solution.py:79
  1.4 4.1 %collective-permute-start.3 = (bf16[8,4864]{1,0:T(8,128)(2,1)S(1)}, bf16[8,4864]{1,0:T(8,128)(2,1)S(1)}, u32[]{:S(2)}, u32[]{:S(2)}) collective-permute-start(bf16[8,4864]{1,0:T(8,128)(2,1)S(1)} %get-tuple-element.42), channel_id=1, source_target_pairs={{0,8},{1,9},{2,10},{3,11},{4,12},{5,13},{6,14},{7,15},{8,0},{9,1},... | collective-permute-start | bytes 233480 | tf_op jit(solution)/shard_map/ppermute | solution.py:259
  5.5 1.5 %collective-permute-start = (bf16[8,4864]{1,0:T(8,128)(2,1)S(1)}, bf16[8,4864]{1,0:T(8,128)(2,1)S(1)}, u32[]{:S(2)}, u32[]{:S(2)}) collective-permute-start(bf16[8,4864]{1,0:T(8,128)(2,1)S(1)} %get-tuple-element.40.refs_0_), channel_id=1, source_target_pairs={{0,2},{1,3},{2,0},{3,1},{4,6},{5,7},{6,4},{7,5},{8,10},{9,11},{10,... | collective-permute-start | bytes 233480 | tf_op jit(solution)/shard_map/ppermute | solution.py:259
  7.0 1.6 %collective-permute-start.2 = (bf16[8,4864]{1,0:T(8,128)(2,1)S(1)}, bf16[8,4864]{1,0:T(8,128)(2,1)S(1)}, u32[]{:S(2)}, u32[]{:S(2)}) collective-permute-start(bf16[8,4864]{1,0:T(8,128)(2,1)S(1)} %get-tuple-element.40.refs_0_), channel_id=1, source_target_pairs={{0,4},{1,5},{2,6},{3,7},{4,0},{5,1},{6,2},{7,3},{8,12},{9,13},{10,... | collective-permute-start | bytes 233480 | tf_op jit(solution)/shard_map/ppermute | solution.py:259
  8.6 0.4 collective-permute-start.1
  9.0 0.3 collective-permute-done.3.refs_4_
  9.3 1.6 %collective-permute-start.6 = (bf16[8,4864]{1,0:T(8,128)(2,1)S(1)}, bf16[8,4864]{1,0:T(8,128)(2,1)S(1)}, u32[]{:S(2)}, u32[]{:S(2)}) collective-permute-start(bf16[8,4864]{1,0:T(8,128)(2,1)S(1)} %collective-permute-done.3.refs_4_), channel_id=1, source_target_pairs={{0,2},{1,3},{2,0},{3,1},{4,6},{5,7},{6,4},{7,5},{8,10},{9,11},{10,... | collective-permute-start | bytes 233480 | tf_op jit(solution)/shard_map/ppermute | solution.py:259
  10.9 1.1 %collective-permute-start.5 = (bf16[8,4864]{1,0:T(8,128)(2,1)S(1)}, bf16[8,4864]{1,0:T(8,128)(2,1)S(1)}, u32[]{:S(2)}, u32[]{:S(2)}) collective-permute-start(bf16[8,4864]{1,0:T(8,128)(2,1)S(1)} %collective-permute-done.3.refs_4_), channel_id=1, source_target_pairs={{0,4},{1,5},{2,6},{3,7},{4,0},{5,1},{6,2},{7,3},{8,12},{9,13},{10,... | collective-permute-start | bytes 233480 | tf_op jit(solution)/shard_map/ppermute | solution.py:259
  12.1 1.2 %collective-permute-start.4 = (bf16[8,4864]{1,0:T(8,128)(2,1)S(1)}, bf16[8,4864]{1,0:T(8,128)(2,1)S(1)}, u32[]{:S(2)}, u32[]{:S(2)}) collective-permute-start(bf16[8,4864]{1,0:T(8,128)(2,1)S(1)} %collective-permute-done.3.refs_4_), channel_id=1, source_target_pairs={{0,6},{1,7},{2,4},{3,5},{4,2},{5,3},{6,0},{7,1},{8,14},{9,15},{10,... | collective-permute-start | bytes 233480 | tf_op jit(solution)/shard_map/ppermute | solution.py:259
  13.2 3.1 %shard_map.65 = (bf16[576,6400]{1,0:T(8,128)(2,1)S(1)}, bf16[2,6400]{1,0:T(2,128)(2,1)S(1)}, f32[50,128]{1,0:T(8,128)S(1)}) custom-call(bf16[576,6400]{1,0:T(8,128)(2,1)} %bitcast.9, bf16[2,6400]{1,0:T(2,128)(2,1)} %bitcast.12, f32[50,128]{1,0:T(8,128)} %bitcast.11, bf16[8,4864]{1,0:T(8,128)(2,1)S(1)} %collective-permute-done.refs_3_), custom_call_target="tpu_custom_call" | custom-call | bytes 7424000 | tf_op jit(solution)/shard_map/pallas_call | solution.py:154
  16.5 0.5 %collective-permute-start.11 = (bf16[8,4864]{1,0:T(8,128)(2,1)S(1)}, bf16[8,4864]{1,0:T(8,128)(2,1)S(1)}, u32[]{:S(2)}, u32[]{:S(2)}) collective-permute-start(bf16[8,4864]{1,0:T(8,128)(2,1)S(1)} %collective-permute-done.3.refs_4_), channel_id=1, source_target_pairs={{0,1},{1,0},{2,3},{3,2},{4,5},{5,4},{6,7},{7,6},{8,9},{9,8},{10,11... | collective-permute-start | bytes 233480 | tf_op jit(solution)/shard_map/ppermute | solution.py:259
  17.0 0.4 collective-permute-done.4.refs_5_
  17.4 0.5 %collective-permute-start.9 = (bf16[8,4864]{1,0:T(8,128)(2,1)S(1)}, bf16[8,4864]{1,0:T(8,128)(2,1)S(1)}, u32[]{:S(2)}, u32[]{:S(2)}) collective-permute-start(bf16[8,4864]{1,0:T(8,128)(2,1)S(1)} %collective-permute-done.2.refs_2_), channel_id=1, source_target_pairs={{0,1},{1,0},{2,3},{3,2},{4,5},{5,4},{6,7},{7,6},{8,9},{9,8},{10,11... | collective-permute-start | bytes 233480 | tf_op jit(solution)/shard_map/ppermute | solution.py:259
  17.9 0.5 %collective-permute-start.12 = (bf16[8,4864]{1,0:T(8,128)(2,1)S(1)}, bf16[8,4864]{1,0:T(8,128)(2,1)S(1)}, u32[]{:S(2)}, u32[]{:S(2)}) collective-permute-start(bf16[8,4864]{1,0:T(8,128)(2,1)S(1)} %collective-permute-done.4.refs_5_), channel_id=1, source_target_pairs={{0,1},{1,0},{2,3},{3,2},{4,5},{5,4},{6,7},{7,6},{8,9},{9,8},{10,11... | collective-permute-start | bytes 233480 | tf_op jit(solution)/shard_map/ppermute | solution.py:259
  19.3 0.4 collective-permute-done.13.refs_14_
  19.9 5.3 %shard_map.66 = (bf16[8,4864]{1,0:T(8,128)(2,1)S(1)}, bf16[8,4864]{1,0:T(8,128)(2,1)S(1)}, bf16[8,4864]{1,0:T(8,128)(2,1)S(1)}, bf16[8,4864]{1,0:T(8,128)(2,1)S(...) custom-call(bf16[8,4864]{1,0:T(8,128)(2,1)S(1)} %get-tuple-element.4, ...), custom_call_target="tpu_custom_call" | custom-call | flops 1415577600 | bytes 11059200 | tf_op jit(solution)/shard_map/pallas_call | solution.py:231
  25.2 0.3 collective-permute-start.16
  25.8 0.3 collective-permute-start.18
  26.6 1.5 %collective-permute-start.17 = (bf16[8,4864]{1,0:T(8,128)(2,1)S(1)}, bf16[8,4864]{1,0:T(8,128)(2,1)S(1)}, u32[]{:S(2)}, u32[]{:S(2)}) collective-permute-start(bf16[8,4864]{1,0:T(8,128)(2,1)S(1)} %add_convert_fusion.6), channel_id=1, source_target_pairs={{0,6},{1,7},{2,4},{3,5},{4,2},{5,3},{6,0},{7,1},{8,14},{9,15},{10,... | collective-permute-start | bytes 233480 | tf_op jit(solution)/shard_map/ppermute | solution.py:259
  28.1 0.5 %collective-permute-start.25 = (bf16[8,4864]{1,0:T(8,128)(2,1)S(1)}, bf16[8,4864]{1,0:T(8,128)(2,1)S(1)}, u32[]{:S(2)}, u32[]{:S(2)}) collective-permute-start(bf16[8,4864]{1,0:T(8,128)(2,1)S(1)} %get-tuple-element.71), channel_id=1, source_target_pairs={{0,1},{1,0},{2,3},{3,2},{4,5},{5,4},{6,7},{7,6},{8,9},{9,8},{10,11... | collective-permute-start | bytes 233480 | tf_op jit(solution)/shard_map/ppermute | solution.py:259
  28.7 0.8 %collective-permute-done.25 = bf16[8,4864]{1,0:T(8,128)(2,1)S(1)} collective-permute-done((bf16[8,4864]{1,0:T(8,128)(2,1)S(1)}, bf16[8,4864]{1,0:T(8,128)(2,1)S(1)}, u32[]{:S(2)}, u32[]{:S(2)}) %collective-permute-start.25) | collective-permute-done | bytes 77856 | tf_op jit(solution)/shard_map/ppermute | solution.py:259
  29.5 0.9 %collective-permute-start.19 = (bf16[8,4864]{1,0:T(8,128)(2,1)S(1)}, bf16[8,4864]{1,0:T(8,128)(2,1)S(1)}, u32[]{:S(2)}, u32[]{:S(2)}) collective-permute-start(bf16[8,4864]{1,0:T(8,128)(2,1)S(1)} %add_convert_fusion.5), channel_id=1, source_target_pairs={{0,4},{1,5},{2,6},{3,7},{4,0},{5,1},{6,2},{7,3},{8,12},{9,13},{10,... | collective-permute-start | bytes 233480 | tf_op jit(solution)/shard_map/ppermute | solution.py:259
  30.4 1.2 %collective-permute-start.21 = (bf16[8,4864]{1,0:T(8,128)(2,1)S(1)}, bf16[8,4864]{1,0:T(8,128)(2,1)S(1)}, u32[]{:S(2)}, u32[]{:S(2)}) collective-permute-start(bf16[8,4864]{1,0:T(8,128)(2,1)S(1)} %add_convert_fusion.4), channel_id=1, source_target_pairs={{0,2},{1,3},{2,0},{3,1},{4,6},{5,7},{6,4},{7,5},{8,10},{9,11},{10,... | collective-permute-start | bytes 233480 | tf_op jit(solution)/shard_map/ppermute | solution.py:259
  31.8 0.3 collective-permute-done.17
  32.1 1.4 %collective-permute-start.26 = (bf16[8,4864]{1,0:T(8,128)(2,1)S(1)}, bf16[8,4864]{1,0:T(8,128)(2,1)S(1)}, u32[]{:S(2)}, u32[]{:S(2)}) collective-permute-start(bf16[8,4864]{1,0:T(8,128)(2,1)S(1)} %add_convert_fusion.1), channel_id=1, source_target_pairs={{0,6},{1,7},{2,4},{3,5},{4,2},{5,3},{6,0},{7,1},{8,14},{9,15},{10,... | collective-permute-start | bytes 233480 | tf_op jit(solution)/shard_map/ppermute | solution.py:259
  33.5 0.6 %collective-permute-done.19 = bf16[8,4864]{1,0:T(8,128)(2,1)S(1)} collective-permute-done((bf16[8,4864]{1,0:T(8,128)(2,1)S(1)}, bf16[8,4864]{1,0:T(8,128)(2,1)S(1)}, u32[]{:S(2)}, u32[]{:S(2)}) %collective-permute-start.19) | collective-permute-done | bytes 77856 | tf_op jit(solution)/shard_map/ppermute | solution.py:259
  34.1 0.9 %collective-permute-start.28 = (bf16[8,4864]{1,0:T(8,128)(2,1)S(1)}, bf16[8,4864]{1,0:T(8,128)(2,1)S(1)}, u32[]{:S(2)}, u32[]{:S(2)}) collective-permute-start(bf16[8,4864]{1,0:T(8,128)(2,1)S(1)} %add_convert_fusion), channel_id=1, source_target_pairs={{0,4},{1,5},{2,6},{3,7},{4,0},{5,1},{6,2},{7,3},{8,12},{9,13},{10,... | collective-permute-start | bytes 233480 | tf_op jit(solution)/shard_map/ppermute | solution.py:259
  35.1 2.9 %collective-permute-start.23 = (bf16[8,4864]{1,0:T(8,128)(2,1)S(1)}, bf16[8,4864]{1,0:T(8,128)(2,1)S(1)}, u32[]{:S(2)}, u32[]{:S(2)}) collective-permute-start(bf16[8,4864]{1,0:T(8,128)(2,1)S(1)} %add_convert_fusion.3), channel_id=1, source_target_pairs={{0,8},{1,9},{2,10},{3,11},{4,12},{5,13},{6,14},{7,15},{8,0},{9,1},... | collective-permute-start | bytes 233480 | tf_op jit(solution)/shard_map/ppermute | solution.py:259
  38.0 1.4 %collective-permute-start.29 = (bf16[8,4864]{1,0:T(8,128)(2,1)S(1)}, bf16[8,4864]{1,0:T(8,128)(2,1)S(1)}, u32[]{:S(2)}, u32[]{:S(2)}) collective-permute-start(bf16[8,4864]{1,0:T(8,128)(2,1)S(1)} %add_convert_fusion.2), channel_id=1, source_target_pairs={{0,2},{1,3},{2,0},{3,1},{4,6},{5,7},{6,4},{7,5},{8,10},{9,11},{10,... | collective-permute-start | bytes 233480 | tf_op jit(solution)/shard_map/ppermute | solution.py:259
  39.4 1.9 %collective-permute-done.23.refs_0_ = bf16[8,4864]{1,0:T(8,128)(2,1)S(1)} collective-permute-done((bf16[8,4864]{1,0:T(8,128)(2,1)S(1)}, bf16[8,4864]{1,0:T(8,128)(2,1)S(1)}, u32[]{:S(2)}, u32[]{:S(2)}) %collective-permute-start.23) | collective-permute-done | bytes 77856 | tf_op jit(solution)/shard_map/ppermute | solution.py:259
  41.3 1.1 %collective-permute-done.29.refs_4_ = bf16[8,4864]{1,0:T(8,128)(2,1)S(1)} collective-permute-done((bf16[8,4864]{1,0:T(8,128)(2,1)S(1)}, bf16[8,4864]{1,0:T(8,128)(2,1)S(1)}, u32[]{:S(2)}, u32[]{:S(2)}) %collective-permute-start.29) | collective-permute-done | bytes 77856 | tf_op jit(solution)/shard_map/ppermute | solution.py:259
  42.4 1.3 %shard_map.67 = bf16[8,6400]{1,0:T(8,128)(2,1)} custom-call(s32[1,8]{1,0:T(1,128)S(1)} %bitcast.8, bf16[8,6400]{1,0:T(8,128)(2,1)S(1)} %copy-done, bf16[8,4864]{1,0:T(8,128)(2,1)S(1)} %collective-permute-done.23.refs_0_, f32[8,4864]{1,0:T(8,128)S(1)} %convert_add_fusion.refs_1_, bf16[8,4864]{1,0:T(8,128)(2,1)S(1)} %collective-permute-done.26.refs_2_, ...), custom_call_target="tpu_custom_call" | custom-call | tf_op jit(solution)/shard_map/pallas_call | solution.py:127
  (44 shorter events, 2.4 us)
Async XLA Ops:
  1.4 7.9 %collective-permute-start.3 = (bf16[8,4864]{1,0:T(8,128)(2,1)S(1)}, bf16[8,4864]{1,0:T(8,128)(2,1)S(1)}, u32[]{:S(2)}, u32[]{:S(2)}) collective-permute-start(bf16[8,4864]{1,0:T(8,128)(2,1)S(1)} %get-tuple-element.42), channel_id=1, source_target_pairs={{0,8},{1,9},{2,10},{3,11},{4,12},{5,13},{6,14},{7,15},{8,0},{9,1},... | collective-permute-start | bytes 233480 | tf_op jit(solution)/shard_map/ppermute | solution.py:259
  5.5 6.6 %collective-permute-start = (bf16[8,4864]{1,0:T(8,128)(2,1)S(1)}, bf16[8,4864]{1,0:T(8,128)(2,1)S(1)}, u32[]{:S(2)}, u32[]{:S(2)}) collective-permute-start(bf16[8,4864]{1,0:T(8,128)(2,1)S(1)} %get-tuple-element.40.refs_0_), channel_id=1, source_target_pairs={{0,2},{1,3},{2,0},{3,1},{4,6},{5,7},{6,4},{7,5},{8,10},{9,11},{10,... | collective-permute-start | bytes 233480 | tf_op jit(solution)/shard_map/ppermute | solution.py:259
  7.0 9.4 %collective-permute-start.2 = (bf16[8,4864]{1,0:T(8,128)(2,1)S(1)}, bf16[8,4864]{1,0:T(8,128)(2,1)S(1)}, u32[]{:S(2)}, u32[]{:S(2)}) collective-permute-start(bf16[8,4864]{1,0:T(8,128)(2,1)S(1)} %get-tuple-element.40.refs_0_), channel_id=1, source_target_pairs={{0,4},{1,5},{2,6},{3,7},{4,0},{5,1},{6,2},{7,3},{8,12},{9,13},{10,... | collective-permute-start | bytes 233480 | tf_op jit(solution)/shard_map/ppermute | solution.py:259
  8.6 7.9 %collective-permute-start.1 = (bf16[8,4864]{1,0:T(8,128)(2,1)S(1)}, bf16[8,4864]{1,0:T(8,128)(2,1)S(1)}, u32[]{:S(2)}, u32[]{:S(2)}) collective-permute-start(bf16[8,4864]{1,0:T(8,128)(2,1)S(1)} %get-tuple-element.40.refs_0_), channel_id=1, source_target_pairs={{0,6},{1,7},{2,4},{3,5},{4,2},{5,3},{6,0},{7,1},{8,14},{9,15},{10,... | collective-permute-start | bytes 233480 | tf_op jit(solution)/shard_map/ppermute | solution.py:259
  9.3 7.7 %collective-permute-start.6 = (bf16[8,4864]{1,0:T(8,128)(2,1)S(1)}, bf16[8,4864]{1,0:T(8,128)(2,1)S(1)}, u32[]{:S(2)}, u32[]{:S(2)}) collective-permute-start(bf16[8,4864]{1,0:T(8,128)(2,1)S(1)} %collective-permute-done.3.refs_4_), channel_id=1, source_target_pairs={{0,2},{1,3},{2,0},{3,1},{4,6},{5,7},{6,4},{7,5},{8,10},{9,11},{10,... | collective-permute-start | bytes 233480 | tf_op jit(solution)/shard_map/ppermute | solution.py:259
  10.9 6.1 %collective-permute-start.5 = (bf16[8,4864]{1,0:T(8,128)(2,1)S(1)}, bf16[8,4864]{1,0:T(8,128)(2,1)S(1)}, u32[]{:S(2)}, u32[]{:S(2)}) collective-permute-start(bf16[8,4864]{1,0:T(8,128)(2,1)S(1)} %collective-permute-done.3.refs_4_), channel_id=1, source_target_pairs={{0,4},{1,5},{2,6},{3,7},{4,0},{5,1},{6,2},{7,3},{8,12},{9,13},{10,... | collective-permute-start | bytes 233480 | tf_op jit(solution)/shard_map/ppermute | solution.py:259
  12.1 5.3 %collective-permute-start.4 = (bf16[8,4864]{1,0:T(8,128)(2,1)S(1)}, bf16[8,4864]{1,0:T(8,128)(2,1)S(1)}, u32[]{:S(2)}, u32[]{:S(2)}) collective-permute-start(bf16[8,4864]{1,0:T(8,128)(2,1)S(1)} %collective-permute-done.3.refs_4_), channel_id=1, source_target_pairs={{0,6},{1,7},{2,4},{3,5},{4,2},{5,3},{6,0},{7,1},{8,14},{9,15},{10,... | collective-permute-start | bytes 233480 | tf_op jit(solution)/shard_map/ppermute | solution.py:259
  16.4 26.0 %copy-start = (bf16[8,6400]{1,0:T(8,128)(2,1)S(1)}, bf16[8,6400]{1,0:T(8,128)(2,1)}, u32[]{:S(2)}) copy-start(bf16[8,6400]{1,0:T(8,128)(2,1)} %hidden_far.3) | copy-start | bytes 307204
  16.4 26.0 %copy-start.1 = (s32[8,1]{0,1:T(1,128)S(1)}, s32[8,1]{0,1:T(1,128)}, u32[]{:S(2)}) copy-start(s32[8,1]{0,1:T(1,128)} %param.9) | copy-start | bytes 100
  16.4 1.5 %collective-permute-start.7 = (bf16[8,4864]{1,0:T(8,128)(2,1)S(1)}, bf16[8,4864]{1,0:T(8,128)(2,1)S(1)}, u32[]{:S(2)}, u32[]{:S(2)}) collective-permute-start(bf16[8,4864]{1,0:T(8,128)(2,1)S(1)} %get-tuple-element.40.refs_0_), channel_id=1, source_target_pairs={{0,1},{1,0},{2,3},{3,2},{4,5},{5,4},{6,7},{7,6},{8,9},{9,8},{10,11... | collective-permute-start | bytes 233480 | tf_op jit(solution)/shard_map/ppermute | solution.py:259
  16.5 1.9 %collective-permute-start.11 = (bf16[8,4864]{1,0:T(8,128)(2,1)S(1)}, bf16[8,4864]{1,0:T(8,128)(2,1)S(1)}, u32[]{:S(2)}, u32[]{:S(2)}) collective-permute-start(bf16[8,4864]{1,0:T(8,128)(2,1)S(1)} %collective-permute-done.3.refs_4_), channel_id=1, source_target_pairs={{0,1},{1,0},{2,3},{3,2},{4,5},{5,4},{6,7},{7,6},{8,9},{9,8},{10,11... | collective-permute-start | bytes 233480 | tf_op jit(solution)/shard_map/ppermute | solution.py:259
  17.4 1.3 %collective-permute-start.8 = (bf16[8,4864]{1,0:T(8,128)(2,1)S(1)}, bf16[8,4864]{1,0:T(8,128)(2,1)S(1)}, u32[]{:S(2)}, u32[]{:S(2)}) collective-permute-start(bf16[8,4864]{1,0:T(8,128)(2,1)S(1)} %collective-permute-done.1.refs_1_), channel_id=1, source_target_pairs={{0,1},{1,0},{2,3},{3,2},{4,5},{5,4},{6,7},{7,6},{8,9},{9,8},{10,11... | collective-permute-start | bytes 233480 | tf_op jit(solution)/shard_map/ppermute | solution.py:259
  17.4 1.5 %collective-permute-start.9 = (bf16[8,4864]{1,0:T(8,128)(2,1)S(1)}, bf16[8,4864]{1,0:T(8,128)(2,1)S(1)}, u32[]{:S(2)}, u32[]{:S(2)}) collective-permute-start(bf16[8,4864]{1,0:T(8,128)(2,1)S(1)} %collective-permute-done.2.refs_2_), channel_id=1, source_target_pairs={{0,1},{1,0},{2,3},{3,2},{4,5},{5,4},{6,7},{7,6},{8,9},{9,8},{10,11... | collective-permute-start | bytes 233480 | tf_op jit(solution)/shard_map/ppermute | solution.py:259
  17.9 1.3 %collective-permute-start.10 = (bf16[8,4864]{1,0:T(8,128)(2,1)S(1)}, bf16[8,4864]{1,0:T(8,128)(2,1)S(1)}, u32[]{:S(2)}, u32[]{:S(2)}) collective-permute-start(bf16[8,4864]{1,0:T(8,128)(2,1)S(1)} %collective-permute-done.refs_3_), channel_id=1, source_target_pairs={{0,1},{1,0},{2,3},{3,2},{4,5},{5,4},{6,7},{7,6},{8,9},{9,8},{10,11... | collective-permute-start | bytes 233480 | tf_op jit(solution)/shard_map/ppermute | solution.py:259
  17.9 1.4 %collective-permute-start.12 = (bf16[8,4864]{1,0:T(8,128)(2,1)S(1)}, bf16[8,4864]{1,0:T(8,128)(2,1)S(1)}, u32[]{:S(2)}, u32[]{:S(2)}) collective-permute-start(bf16[8,4864]{1,0:T(8,128)(2,1)S(1)} %collective-permute-done.4.refs_5_), channel_id=1, source_target_pairs={{0,1},{1,0},{2,3},{3,2},{4,5},{5,4},{6,7},{7,6},{8,9},{9,8},{10,11... | collective-permute-start | bytes 233480 | tf_op jit(solution)/shard_map/ppermute | solution.py:259
  18.4 1.3 %collective-permute-start.13 = (bf16[8,4864]{1,0:T(8,128)(2,1)S(1)}, bf16[8,4864]{1,0:T(8,128)(2,1)S(1)}, u32[]{:S(2)}, u32[]{:S(2)}) collective-permute-start(bf16[8,4864]{1,0:T(8,128)(2,1)S(1)} %collective-permute-done.5.refs_6_), channel_id=1, source_target_pairs={{0,1},{1,0},{2,3},{3,2},{4,5},{5,4},{6,7},{7,6},{8,9},{9,8},{10,11... | collective-permute-start | bytes 233480 | tf_op jit(solution)/shard_map/ppermute | solution.py:259
  18.6 1.3 %collective-permute-start.14 = (bf16[8,4864]{1,0:T(8,128)(2,1)S(1)}, bf16[8,4864]{1,0:T(8,128)(2,1)S(1)}, u32[]{:S(2)}, u32[]{:S(2)}) collective-permute-start(bf16[8,4864]{1,0:T(8,128)(2,1)S(1)} %collective-permute-done.6.refs_7_), channel_id=1, source_target_pairs={{0,1},{1,0},{2,3},{3,2},{4,5},{5,4},{6,7},{7,6},{8,9},{9,8},{10,11... | collective-permute-start | bytes 233480 | tf_op jit(solution)/shard_map/ppermute | solution.py:259
  25.2 1.3 %collective-permute-start.16 = (bf16[8,4864]{1,0:T(8,128)(2,1)S(1)}, bf16[8,4864]{1,0:T(8,128)(2,1)S(1)}, u32[]{:S(2)}, u32[]{:S(2)}) collective-permute-start(bf16[8,4864]{1,0:T(8,128)(2,1)S(1)} %get-tuple-element.55), channel_id=1, source_target_pairs={{0,1},{1,0},{2,3},{3,2},{4,5},{5,4},{6,7},{7,6},{8,9},{9,8},{10,11... | collective-permute-start | bytes 233480 | tf_op jit(solution)/shard_map/ppermute | solution.py:259
  25.5 6.1 %collective-permute-start.15 = (bf16[8,4864]{1,0:T(8,128)(2,1)S(1)}, bf16[8,4864]{1,0:T(8,128)(2,1)S(1)}, u32[]{:S(2)}, u32[]{:S(2)}) collective-permute-start(bf16[8,4864]{1,0:T(8,128)(2,1)S(1)} %get-tuple-element.53), channel_id=1, source_target_pairs={{0,1},{1,0},{2,3},{3,2},{4,5},{5,4},{6,7},{7,6},{8,9},{9,8},{10,11... | collective-permute-start | bytes 233480 | tf_op jit(solution)/shard_map/ppermute | solution.py:259
  25.8 2.3 %collective-permute-start.18 = (bf16[8,4864]{1,0:T(8,128)(2,1)S(1)}, bf16[8,4864]{1,0:T(8,128)(2,1)S(1)}, u32[]{:S(2)}, u32[]{:S(2)}) collective-permute-start(bf16[8,4864]{1,0:T(8,128)(2,1)S(1)} %get-tuple-element.62), channel_id=1, source_target_pairs={{0,1},{1,0},{2,3},{3,2},{4,5},{5,4},{6,7},{7,6},{8,9},{9,8},{10,11... | collective-permute-start | bytes 233480 | tf_op jit(solution)/shard_map/ppermute | solution.py:259
  26.1 2.6 %collective-permute-start.20 = (bf16[8,4864]{1,0:T(8,128)(2,1)S(1)}, bf16[8,4864]{1,0:T(8,128)(2,1)S(1)}, u32[]{:S(2)}, u32[]{:S(2)}) collective-permute-start(bf16[8,4864]{1,0:T(8,128)(2,1)S(1)} %get-tuple-element.64), channel_id=1, source_target_pairs={{0,1},{1,0},{2,3},{3,2},{4,5},{5,4},{6,7},{7,6},{8,9},{9,8},{10,11... | collective-permute-start | bytes 233480 | tf_op jit(solution)/shard_map/ppermute | solution.py:259
  26.6 5.5 %collective-permute-start.17 = (bf16[8,4864]{1,0:T(8,128)(2,1)S(1)}, bf16[8,4864]{1,0:T(8,128)(2,1)S(1)}, u32[]{:S(2)}, u32[]{:S(2)}) collective-permute-start(bf16[8,4864]{1,0:T(8,128)(2,1)S(1)} %add_convert_fusion.6), channel_id=1, source_target_pairs={{0,6},{1,7},{2,4},{3,5},{4,2},{5,3},{6,0},{7,1},{8,14},{9,15},{10,... | collective-permute-start | bytes 233480 | tf_op jit(solution)/shard_map/ppermute | solution.py:259
  28.1 7.0 %collective-permute-start.22 = (bf16[8,4864]{1,0:T(8,128)(2,1)S(1)}, bf16[8,4864]{1,0:T(8,128)(2,1)S(1)}, u32[]{:S(2)}, u32[]{:S(2)}) collective-permute-start(bf16[8,4864]{1,0:T(8,128)(2,1)S(1)} %get-tuple-element.66), channel_id=1, source_target_pairs={{0,1},{1,0},{2,3},{3,2},{4,5},{5,4},{6,7},{7,6},{8,9},{9,8},{10,11... | collective-permute-start | bytes 233480 | tf_op jit(solution)/shard_map/ppermute | solution.py:259
  28.1 1.4 %collective-permute-start.25 = (bf16[8,4864]{1,0:T(8,128)(2,1)S(1)}, bf16[8,4864]{1,0:T(8,128)(2,1)S(1)}, u32[]{:S(2)}, u32[]{:S(2)}) collective-permute-start(bf16[8,4864]{1,0:T(8,128)(2,1)S(1)} %get-tuple-element.71), channel_id=1, source_target_pairs={{0,1},{1,0},{2,3},{3,2},{4,5},{5,4},{6,7},{7,6},{8,9},{9,8},{10,11... | collective-permute-start | bytes 233480 | tf_op jit(solution)/shard_map/ppermute | solution.py:259
  28.6 1.8 %collective-permute-start.27 = (bf16[8,4864]{1,0:T(8,128)(2,1)S(1)}, bf16[8,4864]{1,0:T(8,128)(2,1)S(1)}, u32[]{:S(2)}, u32[]{:S(2)}) collective-permute-start(bf16[8,4864]{1,0:T(8,128)(2,1)S(1)} %get-tuple-element.73), channel_id=1, source_target_pairs={{0,1},{1,0},{2,3},{3,2},{4,5},{5,4},{6,7},{7,6},{8,9},{9,8},{10,11... | collective-permute-start | bytes 233480 | tf_op jit(solution)/shard_map/ppermute | solution.py:259
  29.5 4.6 %collective-permute-start.19 = (bf16[8,4864]{1,0:T(8,128)(2,1)S(1)}, bf16[8,4864]{1,0:T(8,128)(2,1)S(1)}, u32[]{:S(2)}, u32[]{:S(2)}) collective-permute-start(bf16[8,4864]{1,0:T(8,128)(2,1)S(1)} %add_convert_fusion.5), channel_id=1, source_target_pairs={{0,4},{1,5},{2,6},{3,7},{4,0},{5,1},{6,2},{7,3},{8,12},{9,13},{10,... | collective-permute-start | bytes 233480 | tf_op jit(solution)/shard_map/ppermute | solution.py:259
  30.4 4.6 %collective-permute-start.21 = (bf16[8,4864]{1,0:T(8,128)(2,1)S(1)}, bf16[8,4864]{1,0:T(8,128)(2,1)S(1)}, u32[]{:S(2)}, u32[]{:S(2)}) collective-permute-start(bf16[8,4864]{1,0:T(8,128)(2,1)S(1)} %add_convert_fusion.4), channel_id=1, source_target_pairs={{0,2},{1,3},{2,0},{3,1},{4,6},{5,7},{6,4},{7,5},{8,10},{9,11},{10,... | collective-permute-start | bytes 233480 | tf_op jit(solution)/shard_map/ppermute | solution.py:259
  31.7 7.7 %collective-permute-start.24 = (bf16[8,4864]{1,0:T(8,128)(2,1)S(1)}, bf16[8,4864]{1,0:T(8,128)(2,1)S(1)}, u32[]{:S(2)}, u32[]{:S(2)}) collective-permute-start(bf16[8,4864]{1,0:T(8,128)(2,1)S(1)} %get-tuple-element.69), channel_id=1, source_target_pairs={{0,1},{1,0},{2,3},{3,2},{4,5},{5,4},{6,7},{7,6},{8,9},{9,8},{10,11... | collective-permute-start | bytes 233480 | tf_op jit(solution)/shard_map/ppermute | solution.py:259
  32.1 7.4 %collective-permute-start.26 = (bf16[8,4864]{1,0:T(8,128)(2,1)S(1)}, bf16[8,4864]{1,0:T(8,128)(2,1)S(1)}, u32[]{:S(2)}, u32[]{:S(2)}) collective-permute-start(bf16[8,4864]{1,0:T(8,128)(2,1)S(1)} %add_convert_fusion.1), channel_id=1, source_target_pairs={{0,6},{1,7},{2,4},{3,5},{4,2},{5,3},{6,0},{7,1},{8,14},{9,15},{10,... | collective-permute-start | bytes 233480 | tf_op jit(solution)/shard_map/ppermute | solution.py:259
  34.1 5.3 %collective-permute-start.28 = (bf16[8,4864]{1,0:T(8,128)(2,1)S(1)}, bf16[8,4864]{1,0:T(8,128)(2,1)S(1)}, u32[]{:S(2)}, u32[]{:S(2)}) collective-permute-start(bf16[8,4864]{1,0:T(8,128)(2,1)S(1)} %add_convert_fusion), channel_id=1, source_target_pairs={{0,4},{1,5},{2,6},{3,7},{4,0},{5,1},{6,2},{7,3},{8,12},{9,13},{10,... | collective-permute-start | bytes 233480 | tf_op jit(solution)/shard_map/ppermute | solution.py:259
  35.1 6.2 %collective-permute-start.23 = (bf16[8,4864]{1,0:T(8,128)(2,1)S(1)}, bf16[8,4864]{1,0:T(8,128)(2,1)S(1)}, u32[]{:S(2)}, u32[]{:S(2)}) collective-permute-start(bf16[8,4864]{1,0:T(8,128)(2,1)S(1)} %add_convert_fusion.3), channel_id=1, source_target_pairs={{0,8},{1,9},{2,10},{3,11},{4,12},{5,13},{6,14},{7,15},{8,0},{9,1},... | collective-permute-start | bytes 233480 | tf_op jit(solution)/shard_map/ppermute | solution.py:259
  38.0 4.4 %collective-permute-start.29 = (bf16[8,4864]{1,0:T(8,128)(2,1)S(1)}, bf16[8,4864]{1,0:T(8,128)(2,1)S(1)}, u32[]{:S(2)}, u32[]{:S(2)}) collective-permute-start(bf16[8,4864]{1,0:T(8,128)(2,1)S(1)} %add_convert_fusion.2), channel_id=1, source_target_pairs={{0,2},{1,3},{2,0},{3,1},{4,6},{5,7},{6,4},{7,5},{8,10},{9,11},{10,... | collective-permute-start | bytes 233480 | tf_op jit(solution)/shard_map/ppermute | solution.py:259

commit v5 on v4

--- a/solution.py
+++ b/solution.py
@@ -138,32 +138,38 @@
     )(routes, hidden_in, *far_parts, *near_parts)
 
 
-def fetch_kernel(count, *refs):
-    sources, targets, sems = refs[:count], refs[count + 1 : -1], refs[-1]
-    moves = [pltpu.make_async_copy(a, b, sems.at[k]) for k, (a, b) in enumerate(zip(sources, targets))]
+def fetch_kernel(count, size, *refs):
+    sources, blocks, refs = refs[:count], refs[count : count + size], refs[count + size :]
+    targets, joined, sems = refs[:count], refs[count], refs[count + 1]
+    pairs = list(zip(sources, targets)) + [(block, joined.at[k]) for k, block in enumerate(blocks)]
+    moves = [pltpu.make_async_copy(a, b, sems.at[k]) for k, (a, b) in enumerate(pairs)]
     for move in moves:
         move.start()
     for move in moves:
         move.wait()
 
 
-def fetched(arrays, after):
-    count = len(arrays)
+def fetched(arrays, blocks):
+    count, size = len(arrays), len(blocks)
     arrays = [pltpu.with_memory_space_constraint(x, pltpu.HBM) for x in arrays]
-    size = sum(x.size * x.dtype.itemsize for x in arrays)
+    total = sum(x.size * x.dtype.itemsize for x in arrays)
+    joined = jax.ShapeDtypeStruct((size,) + blocks[0].shape, blocks[0].dtype)
     return pl.pallas_call(
-        functools.partial(fetch_kernel, count),
-        out_shape=[jax.ShapeDtypeStruct(x.shape, x.dtype) for x in arrays],
-        in_specs=[pl.BlockSpec(memory_space=pltpu.HBM)] * count + [pl.BlockSpec(memory_space=pl.ANY)],
-        out_specs=[pl.BlockSpec(memory_space=pl.ANY)] * count,
-        scratch_shapes=[pltpu.SemaphoreType.DMA((count,))],
+        functools.partial(fetch_kernel, count, size),
+        out_shape=[jax.ShapeDtypeStruct(x.shape, x.dtype) for x in arrays] + [joined],
+        in_specs=[pl.BlockSpec(memory_space=pltpu.HBM)] * count + [pl.BlockSpec(memory_space=pl.ANY)] * size,
+        out_specs=[pl.BlockSpec(memory_space=pl.ANY)] * (count + 1),
+        scratch_shapes=[pltpu.SemaphoreType.DMA((count + size,))],
         compiler_params=pltpu.CompilerParams(vmem_limit_bytes=1024 * 1024),
-        cost_estimate=pl.CostEstimate(flops=0, bytes_accessed=size, transcendentals=0),
-    )(*arrays, after)
-
-
-def expert_kernel(copies, count, *refs):
-    block_refs, refs = refs[:count], refs[count:]
+        cost_estimate=pl.CostEstimate(flops=0, bytes_accessed=total, transcendentals=0),
+    )(*arrays, *blocks)
+
+
+def expert_kernel(copies, size, count, *refs):
+    (mine_ref, theirs_ref), refs = refs[:2], refs[2:]
+    mine_far, theirs_far, refs = refs[: count // 2 - size], refs[count // 2 - size : count - 2 * size], refs[count - 2 * size :]
+    block_refs = [mine_ref.at[k] for k in range(size)] + list(mine_far)
+    block_refs += [theirs_ref.at[k] for k in range(size)] + list(theirs_far)
     gain_ref, router_ref, up_ref, down_far = refs[:4]
     out_refs, (down_held, normed_ref, rest_ref, sems) = refs[4 : 4 + count], refs[4 + count :]
     tok_rows, width = block_refs[0].shape[0], down_far.shape[1]
@@ -215,23 +221,29 @@
     act = (gate / (1.0 + jnp.exp(-gate)) * up).astype(jnp.bfloat16)
     for move in waits:
         move.wait()
-    main = jnp.dot(act, down_held[:, :stay], preferred_element_type=jnp.float32) * scores
     ends = jnp.dot(act, down_held[:, stay:], preferred_element_type=jnp.float32) * scores
+    lines = {}
     for k in range(count):
-        rows = slice(k * tok_rows, (k + 1) * tok_rows)
-        out_refs[k][...] = folded(main[rows], ends[rows], slots, per).astype(jnp.bfloat16)
-
-
-def expert_rows(blocks, norm_gain, router, gate_up, down_w, copies):
-    count = len(blocks)
+        rest_rows = ends[k * tok_rows : (k + 1) * tok_rows]
+        lines[k] = folded(jnp.zeros((tok_rows, stay), jnp.float32), rest_rows, slots, per)[slots:]
+    for at, size_at in parts[:-1]:
+        output = jnp.dot(act, down_held[:, at : at + size_at], preferred_element_type=jnp.float32) * scores
+        for k in range(count):
+            rows = [output[k * tok_rows : k * tok_rows + slots], lines[k][:, at : at + size_at]]
+            out_refs[k][:, at : at + size_at] = jnp.concatenate(rows, axis=0).astype(jnp.bfloat16)
+
+
+def expert_rows(own, blocks, norm_gain, router, gate_up, down_w, copies):
+    size = own[0].shape[0]
+    count = len(blocks) + 2 * size
     tok_rows, width = blocks[0].shape[0], down_w.shape[1]
     units = down_w.shape[0]
     rows = count * tok_rows
     vmem = pl.BlockSpec(memory_space=pltpu.VMEM)
     return pl.pallas_call(
-        functools.partial(expert_kernel, copies, count),
-        out_shape=[jax.ShapeDtypeStruct(x.shape, jnp.bfloat16) for x in blocks],
-        in_specs=[vmem] * (count + 3) + [pl.BlockSpec(memory_space=pltpu.HBM)],
+        functools.partial(expert_kernel, copies, size, count),
+        out_shape=[jax.ShapeDtypeStruct(blocks[0].shape, jnp.bfloat16)] * count,
+        in_specs=[vmem] * (len(blocks) + 5) + [pl.BlockSpec(memory_space=pltpu.HBM)],
         out_specs=[vmem] * count,
         scratch_shapes=[
             pltpu.VMEM(down_w.shape, jnp.bfloat16),
@@ -245,7 +257,7 @@
             bytes_accessed=6 * units * width,
             transcendentals=rows * units,
         ),
-    )(*blocks, norm_gain, router, gate_up, pltpu.with_memory_space_constraint(down_w, pltpu.HBM))
+    )(*own, *blocks, norm_gain, router, gate_up, pltpu.with_memory_space_constraint(down_w, pltpu.HBM))
 
 
 def body(hidden_in, norm_gain, router, routes, routed_gate_up, routed_down):
@@ -260,16 +272,16 @@
 
     sources = list(packed_rows(routes.T, hidden_in, copies, experts))
     sources[1:] = [swap(sources[k], copies * k) for k in range(1, experts)]
-    mine = [[source] + [swap(source, mask) for mask in chips] for source in sources]
+    own_mine = [sources[0]] + [swap(sources[0], mask) for mask in chips]
+    early = [swap(source, 1) for source in sources[1:]]
+    late = [[swap(source, mask) for mask in chips] for source in sources[1:]]
     local = [routed_gate_up[0].T, router.T, norm_gain.reshape(-1, 128)]
-    gate_up, router_t, gain = fetched(local, mine[0][-1])
-    late = (mine[0][1:], [group[1:] for group in mine[1:]])
-    gate_up, late = lax.optimization_barrier((gate_up, late))
-    mine[0][1:] = late[0]
-    for group, blocks in zip(mine[1:], late[1]):
-        group[1:] = blocks
-    theirs = [[swap(block, 1) for block in group] for group in mine]
-    outs = expert_rows(sum(mine, []) + sum(theirs, []), gain, router_t, gate_up, routed_down[0], copies)
+    gate_up, router_t, gain, own = fetched(local, own_mine)
+    gate_up, own, late = lax.optimization_barrier((gate_up, own, late))
+    own = (own, swap(own, 1))
+    mine = sum([[source] + group for source, group in zip(sources[1:], late)], [])
+    theirs = sum([[first] + [swap(block, 1) for block in group] for first, group in zip(early, late)], [])
+    outs = expert_rows(own, mine + theirs, gain, router_t, gate_up, routed_down[0], copies)
     kept = [outs[k * size : (k + 1) * size] for k in range(experts)]
     given = [outs[(experts + k) * size : (experts + k + 1) * size] for k in range(experts)]
 

time: 43.8 us -> 43.2 us (0.986)
  starting transfers between devices: 25.4 us -> 24.5 us
  waiting for transfers between devices: 6.78 us -> 7.41 us
    ppermute x30 -> x27, starting transfers between devices: 25.4 us -> 24.5 us  [swap(): lax.ppermute(block, 'expert', [(i, i ^ mask) for i in range(axis_len)])]
    ppermute x30 -> x27, waiting for transfers between devices: 6.78 us -> 7.41 us  [swap(): lax.ppermute(block, 'expert', [(i, i ^ mask) for i in range(axis_len)])]
  transfers between devices with their start and end apart: 30 -> 27, of which waited for: 13 -> 14; matrix products, arithmetic and copies ran while one was open for 0% -> 0% of each run, Pallas kernels for 7% -> 7%
where the time goes in v5:
time: 43.2 us; the launch traced here: 43 us
  starting transfers between devices  24.5 us (57%)
  Pallas kernels  10.7 us (25%)
  waiting for transfers between devices  7.41 us (17%)
    ppermute x27, starting transfers between devices, swap(): lax.ppermute(block, 'expert', [(i, i ^ mask) for i in range(axis_len)])  24.5 us
    ppermute x27, waiting for transfers between devices, swap(): lax.ppermute(block, 'expert', [(i, i ^ mask) for i in range(axis_len)])  7.41 us
    pallas_call x1, Pallas kernels, expert_rows(): pl.pallas_call(functools.partial(expert_kernel, copies, size, count), out...  4.85 us
    pallas_call x1, Pallas kernels, fetched(): pl.pallas_call(functools.partial(fetch_kernel, count, size), out_shape=[j...  3.16 us
    pallas_call x1, Pallas kernels, packed_rows(): pl.pallas_call(functools.partial(pack_kernel, copies, experts), out_shape...  1.37 us
    pallas_call x1, Pallas kernels, placed_rows(): pl.pallas_call(functools.partial(final_kernel, copies, experts, len(near_...  1.32 us
  transfers between devices with their start and end apart: 27, of which 14 were waited for; matrix products, arithmetic and copies ran while one was open for 0% of the time, Pallas kernels for 7%

profile of v5, /device:TPU:0, one launch (start us, length us, event | category | flops | bytes accessed | tf_op | source)
XLA Modules:
  0.0 43.0 jit_solution(11171667431213382626)
XLA Ops:
  0.0 1.4 %shard_map.64 = (bf16[8,4864]{1,0:T(8,128)(2,1)S(1)}, bf16[8,4864]{1,0:T(8,128)(2,1)S(1)}) custom-call(s32[1,8]{1,0:T(1,128)} %bitcast.7, bf16[8,6400]{1,0:T(8,128)(2,1)} %hidden_far.3), custom_call_target="tpu_custom_call" | custom-call | tf_op jit(solution)/shard_map/pallas_call | solution.py:79
  1.4 4.1 %collective-permute-start.3 = (bf16[8,4864]{1,0:T(8,128)(2,1)S(1)}, bf16[8,4864]{1,0:T(8,128)(2,1)S(1)}, u32[]{:S(2)}, u32[]{:S(2)}) collective-permute-start(bf16[8,4864]{1,0:T(8,128)(2,1)S(1)} %get-tuple-element.42), channel_id=1, source_target_pairs={{0,8},{1,9},{2,10},{3,11},{4,12},{5,13},{6,14},{7,15},{8,0},{9,1},... | collective-permute-start | bytes 233480 | tf_op jit(solution)/shard_map/ppermute | solution.py:271
  5.5 1.5 %collective-permute-start.2 = (bf16[8,4864]{1,0:T(8,128)(2,1)S(1)}, bf16[8,4864]{1,0:T(8,128)(2,1)S(1)}, u32[]{:S(2)}, u32[]{:S(2)}) collective-permute-start(bf16[8,4864]{1,0:T(8,128)(2,1)S(1)} %get-tuple-element.39.refs_3_), channel_id=1, source_target_pairs={{0,2},{1,3},{2,0},{3,1},{4,6},{5,7},{6,4},{7,5},{8,10},{9,11},{10,... | collective-permute-start | bytes 233480 | tf_op jit(solution)/shard_map/ppermute | solution.py:271
  7.0 1.6 %collective-permute-start.1 = (bf16[8,4864]{1,0:T(8,128)(2,1)S(1)}, bf16[8,4864]{1,0:T(8,128)(2,1)S(1)}, u32[]{:S(2)}, u32[]{:S(2)}) collective-permute-start(bf16[8,4864]{1,0:T(8,128)(2,1)S(1)} %get-tuple-element.39.refs_3_), channel_id=1, source_target_pairs={{0,4},{1,5},{2,6},{3,7},{4,0},{5,1},{6,2},{7,3},{8,12},{9,13},{10,... | collective-permute-start | bytes 233480 | tf_op jit(solution)/shard_map/ppermute | solution.py:271
  8.6 0.4 collective-permute-start
  9.0 0.3 collective-permute-done.3.refs_2_
  9.3 1.6 %collective-permute-start.6 = (bf16[8,4864]{1,0:T(8,128)(2,1)S(1)}, bf16[8,4864]{1,0:T(8,128)(2,1)S(1)}, u32[]{:S(2)}, u32[]{:S(2)}) collective-permute-start(bf16[8,4864]{1,0:T(8,128)(2,1)S(1)} %collective-permute-done.3.refs_2_), channel_id=1, source_target_pairs={{0,2},{1,3},{2,0},{3,1},{4,6},{5,7},{6,4},{7,5},{8,10},{9,11},{10,... | collective-permute-start | bytes 233480 | tf_op jit(solution)/shard_map/ppermute | solution.py:271
  10.9 1.1 %collective-permute-start.5 = (bf16[8,4864]{1,0:T(8,128)(2,1)S(1)}, bf16[8,4864]{1,0:T(8,128)(2,1)S(1)}, u32[]{:S(2)}, u32[]{:S(2)}) collective-permute-start(bf16[8,4864]{1,0:T(8,128)(2,1)S(1)} %collective-permute-done.3.refs_2_), channel_id=1, source_target_pairs={{0,4},{1,5},{2,6},{3,7},{4,0},{5,1},{6,2},{7,3},{8,12},{9,13},{10,... | collective-permute-start | bytes 233480 | tf_op jit(solution)/shard_map/ppermute | solution.py:271
  12.1 1.2 %collective-permute-start.4 = (bf16[8,4864]{1,0:T(8,128)(2,1)S(1)}, bf16[8,4864]{1,0:T(8,128)(2,1)S(1)}, u32[]{:S(2)}, u32[]{:S(2)}) collective-permute-start(bf16[8,4864]{1,0:T(8,128)(2,1)S(1)} %collective-permute-done.3.refs_2_), channel_id=1, source_target_pairs={{0,6},{1,7},{2,4},{3,5},{4,2},{5,3},{6,0},{7,1},{8,14},{9,15},{10,... | collective-permute-start | bytes 233480 | tf_op jit(solution)/shard_map/ppermute | solution.py:271
  13.2 0.7 %collective-permute-done.refs_4_ = bf16[8,4864]{1,0:T(8,128)(2,1)S(1)} collective-permute-done((bf16[8,4864]{1,0:T(8,128)(2,1)S(1)}, bf16[8,4864]{1,0:T(8,128)(2,1)S(1)}, u32[]{:S(2)}, u32[]{:S(2)}) %collective-permute-start) | collective-permute-done | bytes 77856 | tf_op jit(solution)/shard_map/ppermute | solution.py:271
  14.0 3.2 %shard_map.65 = (bf16[576,6400]{1,0:T(8,128)(2,1)S(1)}, bf16[2,6400]{1,0:T(2,128)(2,1)S(1)}, f32[50,128]{1,0:T(8,128)S(1)}, bf16[4,8,4864]{2,1,0:T(8,128)(2,1)S(1)}) custom-call(bf16[576,6400]{1,0:T(8,128)(2,1)} %bitcast.9, bf16[2,6400]{1,0:T(2,128)(2,1)} %bitcast.12, f32[50,128]{1,0:T(8,128)} %bitcast.11, bf16[8,4864]{1,0:T(8,128)(2,1)S(1)} %get-tuple-element.39.refs_3_, ...), custom_call_target="tpu_custom_call" | custom-call | bytes 7424000 | tf_op jit(solution)/shard_map/pallas_call | solution.py:157
  17.4 0.5 %collective-permute-start.8 = (bf16[8,4864]{1,0:T(8,128)(2,1)S(1)}, bf16[8,4864]{1,0:T(8,128)(2,1)S(1)}, u32[]{:S(2)}, u32[]{:S(2)}) collective-permute-start(bf16[8,4864]{1,0:T(8,128)(2,1)S(1)} %collective-permute-done.3.refs_2_), channel_id=1, source_target_pairs={{0,1},{1,0},{2,3},{3,2},{4,5},{5,4},{6,7},{7,6},{8,9},{9,8},{10,11... | collective-permute-start | bytes 233480 | tf_op jit(solution)/shard_map/ppermute | solution.py:271
  17.9 0.5 %collective-permute-start.10 = (bf16[8,4864]{1,0:T(8,128)(2,1)S(1)}, bf16[8,4864]{1,0:T(8,128)(2,1)S(1)}, u32[]{:S(2)}, u32[]{:S(2)}) collective-permute-start(bf16[8,4864]{1,0:T(8,128)(2,1)S(1)} %collective-permute-done.5.refs_4_), channel_id=1, source_target_pairs={{0,1},{1,0},{2,3},{3,2},{4,5},{5,4},{6,7},{7,6},{8,9},{9,8},{10,11... | collective-permute-start | bytes 233480 | tf_op jit(solution)/shard_map/ppermute | solution.py:271
  18.4 0.7 %collective-permute-done.8.refs_6_ = bf16[8,4864]{1,0:T(8,128)(2,1)S(1)} collective-permute-done((bf16[8,4864]{1,0:T(8,128)(2,1)S(1)}, bf16[8,4864]{1,0:T(8,128)(2,1)S(1)}, u32[]{:S(2)}, u32[]{:S(2)}) %collective-permute-start.8) | collective-permute-done | bytes 77856 | tf_op jit(solution)/shard_map/ppermute | solution.py:271
  19.3 0.4 collective-permute-done.11.refs_9_
  19.7 4.9 %shard_map.66 = (bf16[8,4864]{1,0:T(8,128)(2,1)S(1)}, bf16[8,4864]{1,0:T(8,128)(2,1)S(1)}, bf16[8,4864]{1,0:T(8,128)(2,1)S(1)}, bf16[8,4864]{1,0:T(8,128)(2,1)S(...) custom-call(bf16[4,8,4864]{2,1,0:T(8,128)(2,1)S(1)} %get-tuple-eleme, ...), custom_call_target="tpu_custom_call" | custom-call | flops 1415577600 | bytes 11059200 | tf_op jit(solution)/shard_map/pallas_call | solution.py:243
  24.7 0.4 collective-permute-start.12
  25.3 0.4 collective-permute-start.17
  25.9 1.2 %collective-permute-start.14 = (bf16[8,4864]{1,0:T(8,128)(2,1)S(1)}, bf16[8,4864]{1,0:T(8,128)(2,1)S(1)}, u32[]{:S(2)}, u32[]{:S(2)}) collective-permute-start(bf16[8,4864]{1,0:T(8,128)(2,1)S(1)} %add_convert_fusion.6), channel_id=1, source_target_pairs={{0,6},{1,7},{2,4},{3,5},{4,2},{5,3},{6,0},{7,1},{8,14},{9,15},{10,... | collective-permute-start | bytes 233480 | tf_op jit(solution)/shard_map/ppermute | solution.py:271
  27.1 0.5 %collective-permute-start.22 = (bf16[8,4864]{1,0:T(8,128)(2,1)S(1)}, bf16[8,4864]{1,0:T(8,128)(2,1)S(1)}, u32[]{:S(2)}, u32[]{:S(2)}) collective-permute-start(bf16[8,4864]{1,0:T(8,128)(2,1)S(1)} %get-tuple-element.69), channel_id=1, source_target_pairs={{0,1},{1,0},{2,3},{3,2},{4,5},{5,4},{6,7},{7,6},{8,9},{9,8},{10,11... | collective-permute-start | bytes 233480 | tf_op jit(solution)/shard_map/ppermute | solution.py:271
  27.8 0.8 %collective-permute-done.22 = bf16[8,4864]{1,0:T(8,128)(2,1)S(1)} collective-permute-done((bf16[8,4864]{1,0:T(8,128)(2,1)S(1)}, bf16[8,4864]{1,0:T(8,128)(2,1)S(1)}, u32[]{:S(2)}, u32[]{:S(2)}) %collective-permute-start.22) | collective-permute-done | bytes 77856 | tf_op jit(solution)/shard_map/ppermute | solution.py:271
  28.5 1.5 %collective-permute-start.16 = (bf16[8,4864]{1,0:T(8,128)(2,1)S(1)}, bf16[8,4864]{1,0:T(8,128)(2,1)S(1)}, u32[]{:S(2)}, u32[]{:S(2)}) collective-permute-start(bf16[8,4864]{1,0:T(8,128)(2,1)S(1)} %add_convert_fusion.5), channel_id=1, source_target_pairs={{0,4},{1,5},{2,6},{3,7},{4,0},{5,1},{6,2},{7,3},{8,12},{9,13},{10,... | collective-permute-start | bytes 233480 | tf_op jit(solution)/shard_map/ppermute | solution.py:271
  30.1 0.9 %collective-permute-start.18 = (bf16[8,4864]{1,0:T(8,128)(2,1)S(1)}, bf16[8,4864]{1,0:T(8,128)(2,1)S(1)}, u32[]{:S(2)}, u32[]{:S(2)}) collective-permute-start(bf16[8,4864]{1,0:T(8,128)(2,1)S(1)} %add_convert_fusion.4), channel_id=1, source_target_pairs={{0,2},{1,3},{2,0},{3,1},{4,6},{5,7},{6,4},{7,5},{8,10},{9,11},{10,... | collective-permute-start | bytes 233480 | tf_op jit(solution)/shard_map/ppermute | solution.py:271
  31.3 1.2 %collective-permute-start.23 = (bf16[8,4864]{1,0:T(8,128)(2,1)S(1)}, bf16[8,4864]{1,0:T(8,128)(2,1)S(1)}, u32[]{:S(2)}, u32[]{:S(2)}) collective-permute-start(bf16[8,4864]{1,0:T(8,128)(2,1)S(1)} %add_convert_fusion.1), channel_id=1, source_target_pairs={{0,6},{1,7},{2,4},{3,5},{4,2},{5,3},{6,0},{7,1},{8,14},{9,15},{10,... | collective-permute-start | bytes 233480 | tf_op jit(solution)/shard_map/ppermute | solution.py:271
  32.4 0.7 %collective-permute-done.16 = bf16[8,4864]{1,0:T(8,128)(2,1)S(1)} collective-permute-done((bf16[8,4864]{1,0:T(8,128)(2,1)S(1)}, bf16[8,4864]{1,0:T(8,128)(2,1)S(1)}, u32[]{:S(2)}, u32[]{:S(2)}) %collective-permute-start.16) | collective-permute-done | bytes 77856 | tf_op jit(solution)/shard_map/ppermute | solution.py:271
  33.2 1.5 %collective-permute-start.25 = (bf16[8,4864]{1,0:T(8,128)(2,1)S(1)}, bf16[8,4864]{1,0:T(8,128)(2,1)S(1)}, u32[]{:S(2)}, u32[]{:S(2)}) collective-permute-start(bf16[8,4864]{1,0:T(8,128)(2,1)S(1)} %add_convert_fusion), channel_id=1, source_target_pairs={{0,4},{1,5},{2,6},{3,7},{4,0},{5,1},{6,2},{7,3},{8,12},{9,13},{10,... | collective-permute-start | bytes 233480 | tf_op jit(solution)/shard_map/ppermute | solution.py:271
  34.8 2.5 %collective-permute-start.20 = (bf16[8,4864]{1,0:T(8,128)(2,1)S(1)}, bf16[8,4864]{1,0:T(8,128)(2,1)S(1)}, u32[]{:S(2)}, u32[]{:S(2)}) collective-permute-start(bf16[8,4864]{1,0:T(8,128)(2,1)S(1)} %add_convert_fusion.3), channel_id=1, source_target_pairs={{0,8},{1,9},{2,10},{3,11},{4,12},{5,13},{6,14},{7,15},{8,0},{9,1},... | collective-permute-start | bytes 233480 | tf_op jit(solution)/shard_map/ppermute | solution.py:271
  37.3 1.4 %collective-permute-start.26 = (bf16[8,4864]{1,0:T(8,128)(2,1)S(1)}, bf16[8,4864]{1,0:T(8,128)(2,1)S(1)}, u32[]{:S(2)}, u32[]{:S(2)}) collective-permute-start(bf16[8,4864]{1,0:T(8,128)(2,1)S(1)} %add_convert_fusion.2), channel_id=1, source_target_pairs={{0,2},{1,3},{2,0},{3,1},{4,6},{5,7},{6,4},{7,5},{8,10},{9,11},{10,... | collective-permute-start | bytes 233480 | tf_op jit(solution)/shard_map/ppermute | solution.py:271
  38.7 0.3 collective-permute-done.25.refs_3_
  39.0 1.9 %collective-permute-done.20.refs_0_ = bf16[8,4864]{1,0:T(8,128)(2,1)S(1)} collective-permute-done((bf16[8,4864]{1,0:T(8,128)(2,1)S(1)}, bf16[8,4864]{1,0:T(8,128)(2,1)S(1)}, u32[]{:S(2)}, u32[]{:S(2)}) %collective-permute-start.20) | collective-permute-done | bytes 77856 | tf_op jit(solution)/shard_map/ppermute | solution.py:271
  40.9 0.8 %collective-permute-done.26.refs_4_ = bf16[8,4864]{1,0:T(8,128)(2,1)S(1)} collective-permute-done((bf16[8,4864]{1,0:T(8,128)(2,1)S(1)}, bf16[8,4864]{1,0:T(8,128)(2,1)S(1)}, u32[]{:S(2)}, u32[]{:S(2)}) %collective-permute-start.26) | collective-permute-done | bytes 77856 | tf_op jit(solution)/shard_map/ppermute | solution.py:271
  41.7 1.3 %shard_map.67 = bf16[8,6400]{1,0:T(8,128)(2,1)} custom-call(s32[1,8]{1,0:T(1,128)S(1)} %bitcast.8, bf16[8,6400]{1,0:T(8,128)(2,1)S(1)} %copy-done, bf16[8,4864]{1,0:T(8,128)(2,1)S(1)} %collective-permute-done.20.refs_0_, f32[8,4864]{1,0:T(8,128)S(1)} %convert_add_fusion.refs_1_, bf16[8,4864]{1,0:T(8,128)(2,1)S(1)} %collective-permute-done.23.refs_2_, ...), custom_call_target="tpu_custom_call" | custom-call | tf_op jit(solution)/shard_map/pallas_call | solution.py:127
  (38 shorter events, 1.6 us)
Async XLA Ops:
  1.4 7.9 %collective-permute-start.3 = (bf16[8,4864]{1,0:T(8,128)(2,1)S(1)}, bf16[8,4864]{1,0:T(8,128)(2,1)S(1)}, u32[]{:S(2)}, u32[]{:S(2)}) collective-permute-start(bf16[8,4864]{1,0:T(8,128)(2,1)S(1)} %get-tuple-element.42), channel_id=1, source_target_pairs={{0,8},{1,9},{2,10},{3,11},{4,12},{5,13},{6,14},{7,15},{8,0},{9,1},... | collective-permute-start | bytes 233480 | tf_op jit(solution)/shard_map/ppermute | solution.py:271
  5.5 6.6 %collective-permute-start.2 = (bf16[8,4864]{1,0:T(8,128)(2,1)S(1)}, bf16[8,4864]{1,0:T(8,128)(2,1)S(1)}, u32[]{:S(2)}, u32[]{:S(2)}) collective-permute-start(bf16[8,4864]{1,0:T(8,128)(2,1)S(1)} %get-tuple-element.39.refs_3_), channel_id=1, source_target_pairs={{0,2},{1,3},{2,0},{3,1},{4,6},{5,7},{6,4},{7,5},{8,10},{9,11},{10,... | collective-permute-start | bytes 233480 | tf_op jit(solution)/shard_map/ppermute | solution.py:271
  7.0 6.2 %collective-permute-start.1 = (bf16[8,4864]{1,0:T(8,128)(2,1)S(1)}, bf16[8,4864]{1,0:T(8,128)(2,1)S(1)}, u32[]{:S(2)}, u32[]{:S(2)}) collective-permute-start(bf16[8,4864]{1,0:T(8,128)(2,1)S(1)} %get-tuple-element.39.refs_3_), channel_id=1, source_target_pairs={{0,4},{1,5},{2,6},{3,7},{4,0},{5,1},{6,2},{7,3},{8,12},{9,13},{10,... | collective-permute-start | bytes 233480 | tf_op jit(solution)/shard_map/ppermute | solution.py:271
  8.6 5.4 %collective-permute-start = (bf16[8,4864]{1,0:T(8,128)(2,1)S(1)}, bf16[8,4864]{1,0:T(8,128)(2,1)S(1)}, u32[]{:S(2)}, u32[]{:S(2)}) collective-permute-start(bf16[8,4864]{1,0:T(8,128)(2,1)S(1)} %get-tuple-element.39.refs_3_), channel_id=1, source_target_pairs={{0,6},{1,7},{2,4},{3,5},{4,2},{5,3},{6,0},{7,1},{8,14},{9,15},{10,... | collective-permute-start | bytes 233480 | tf_op jit(solution)/shard_map/ppermute | solution.py:271
  9.3 7.9 %collective-permute-start.6 = (bf16[8,4864]{1,0:T(8,128)(2,1)S(1)}, bf16[8,4864]{1,0:T(8,128)(2,1)S(1)}, u32[]{:S(2)}, u32[]{:S(2)}) collective-permute-start(bf16[8,4864]{1,0:T(8,128)(2,1)S(1)} %collective-permute-done.3.refs_2_), channel_id=1, source_target_pairs={{0,2},{1,3},{2,0},{3,1},{4,6},{5,7},{6,4},{7,5},{8,10},{9,11},{10,... | collective-permute-start | bytes 233480 | tf_op jit(solution)/shard_map/ppermute | solution.py:271
  10.9 6.3 %collective-permute-start.5 = (bf16[8,4864]{1,0:T(8,128)(2,1)S(1)}, bf16[8,4864]{1,0:T(8,128)(2,1)S(1)}, u32[]{:S(2)}, u32[]{:S(2)}) collective-permute-start(bf16[8,4864]{1,0:T(8,128)(2,1)S(1)} %collective-permute-done.3.refs_2_), channel_id=1, source_target_pairs={{0,4},{1,5},{2,6},{3,7},{4,0},{5,1},{6,2},{7,3},{8,12},{9,13},{10,... | collective-permute-start | bytes 233480 | tf_op jit(solution)/shard_map/ppermute | solution.py:271
  12.1 5.3 %collective-permute-start.4 = (bf16[8,4864]{1,0:T(8,128)(2,1)S(1)}, bf16[8,4864]{1,0:T(8,128)(2,1)S(1)}, u32[]{:S(2)}, u32[]{:S(2)}) collective-permute-start(bf16[8,4864]{1,0:T(8,128)(2,1)S(1)} %collective-permute-done.3.refs_2_), channel_id=1, source_target_pairs={{0,6},{1,7},{2,4},{3,5},{4,2},{5,3},{6,0},{7,1},{8,14},{9,15},{10,... | collective-permute-start | bytes 233480 | tf_op jit(solution)/shard_map/ppermute | solution.py:271
  17.1 24.5 %copy-start = (bf16[8,6400]{1,0:T(8,128)(2,1)S(1)}, bf16[8,6400]{1,0:T(8,128)(2,1)}, u32[]{:S(2)}) copy-start(bf16[8,6400]{1,0:T(8,128)(2,1)} %hidden_far.3) | copy-start | bytes 307204
  17.2 24.5 %copy-start.1 = (s32[8,1]{0,1:T(1,128)S(1)}, s32[8,1]{0,1:T(1,128)}, u32[]{:S(2)}) copy-start(s32[8,1]{0,1:T(1,128)} %param.9) | copy-start | bytes 100
  17.4 2.3 %collective-permute-start.7 = (bf16[4,8,4864]{2,1,0:T(8,128)(2,1)S(1)}, bf16[4,8,4864]{2,1,0:T(8,128)(2,1)S(1)}, u32[]{:S(2)}, u32[]{:S(2)}) collective-permute-start(bf16[4,8,4864]{2,1,0:T(8,128)(2,1)S(1)} %get-tuple-element.43.refs_0_), channel_id=1, source_target_pairs={{0,1},{1,0},{2,3},{3,2},{4,5},{5,4},{6,7},{7,6},{8,9},{9,8},{10,11... | collective-permute-start | bytes 933896 | tf_op jit(solution)/shard_map/ppermute | solution.py:271
  17.4 1.7 %collective-permute-start.8 = (bf16[8,4864]{1,0:T(8,128)(2,1)S(1)}, bf16[8,4864]{1,0:T(8,128)(2,1)S(1)}, u32[]{:S(2)}, u32[]{:S(2)}) collective-permute-start(bf16[8,4864]{1,0:T(8,128)(2,1)S(1)} %collective-permute-done.3.refs_2_), channel_id=1, source_target_pairs={{0,1},{1,0},{2,3},{3,2},{4,5},{5,4},{6,7},{7,6},{8,9},{9,8},{10,11... | collective-permute-start | bytes 233480 | tf_op jit(solution)/shard_map/ppermute | solution.py:271
  17.9 1.3 %collective-permute-start.9 = (bf16[8,4864]{1,0:T(8,128)(2,1)S(1)}, bf16[8,4864]{1,0:T(8,128)(2,1)S(1)}, u32[]{:S(2)}, u32[]{:S(2)}) collective-permute-start(bf16[8,4864]{1,0:T(8,128)(2,1)S(1)} %collective-permute-done.4.refs_3_), channel_id=1, source_target_pairs={{0,1},{1,0},{2,3},{3,2},{4,5},{5,4},{6,7},{7,6},{8,9},{9,8},{10,11... | collective-permute-start | bytes 233480 | tf_op jit(solution)/shard_map/ppermute | solution.py:271
  17.9 1.4 %collective-permute-start.10 = (bf16[8,4864]{1,0:T(8,128)(2,1)S(1)}, bf16[8,4864]{1,0:T(8,128)(2,1)S(1)}, u32[]{:S(2)}, u32[]{:S(2)}) collective-permute-start(bf16[8,4864]{1,0:T(8,128)(2,1)S(1)} %collective-permute-done.5.refs_4_), channel_id=1, source_target_pairs={{0,1},{1,0},{2,3},{3,2},{4,5},{5,4},{6,7},{7,6},{8,9},{9,8},{10,11... | collective-permute-start | bytes 233480 | tf_op jit(solution)/shard_map/ppermute | solution.py:271
  18.4 1.3 %collective-permute-start.11 = (bf16[8,4864]{1,0:T(8,128)(2,1)S(1)}, bf16[8,4864]{1,0:T(8,128)(2,1)S(1)}, u32[]{:S(2)}, u32[]{:S(2)}) collective-permute-start(bf16[8,4864]{1,0:T(8,128)(2,1)S(1)} %collective-permute-done.6.refs_5_), channel_id=1, source_target_pairs={{0,1},{1,0},{2,3},{3,2},{4,5},{5,4},{6,7},{7,6},{8,9},{9,8},{10,11... | collective-permute-start | bytes 233480 | tf_op jit(solution)/shard_map/ppermute | solution.py:271
  24.5 1.3 %collective-permute-start.13 = (bf16[8,4864]{1,0:T(8,128)(2,1)S(1)}, bf16[8,4864]{1,0:T(8,128)(2,1)S(1)}, u32[]{:S(2)}, u32[]{:S(2)}) collective-permute-start(bf16[8,4864]{1,0:T(8,128)(2,1)S(1)} %get-tuple-element.53), channel_id=1, source_target_pairs={{0,1},{1,0},{2,3},{3,2},{4,5},{5,4},{6,7},{7,6},{8,9},{9,8},{10,11... | collective-permute-start | bytes 233480 | tf_op jit(solution)/shard_map/ppermute | solution.py:271
  24.7 6.3 %collective-permute-start.12 = (bf16[8,4864]{1,0:T(8,128)(2,1)S(1)}, bf16[8,4864]{1,0:T(8,128)(2,1)S(1)}, u32[]{:S(2)}, u32[]{:S(2)}) collective-permute-start(bf16[8,4864]{1,0:T(8,128)(2,1)S(1)} %get-tuple-element.51), channel_id=1, source_target_pairs={{0,1},{1,0},{2,3},{3,2},{4,5},{5,4},{6,7},{7,6},{8,9},{9,8},{10,11... | collective-permute-start | bytes 233480 | tf_op jit(solution)/shard_map/ppermute | solution.py:271
  25.1 2.0 %collective-permute-start.15 = (bf16[8,4864]{1,0:T(8,128)(2,1)S(1)}, bf16[8,4864]{1,0:T(8,128)(2,1)S(1)}, u32[]{:S(2)}, u32[]{:S(2)}) collective-permute-start(bf16[8,4864]{1,0:T(8,128)(2,1)S(1)} %get-tuple-element.60), channel_id=1, source_target_pairs={{0,1},{1,0},{2,3},{3,2},{4,5},{5,4},{6,7},{7,6},{8,9},{9,8},{10,11... | collective-permute-start | bytes 233480 | tf_op jit(solution)/shard_map/ppermute | solution.py:271
  25.3 2.4 %collective-permute-start.17 = (bf16[8,4864]{1,0:T(8,128)(2,1)S(1)}, bf16[8,4864]{1,0:T(8,128)(2,1)S(1)}, u32[]{:S(2)}, u32[]{:S(2)}) collective-permute-start(bf16[8,4864]{1,0:T(8,128)(2,1)S(1)} %get-tuple-element.62), channel_id=1, source_target_pairs={{0,1},{1,0},{2,3},{3,2},{4,5},{5,4},{6,7},{7,6},{8,9},{9,8},{10,11... | collective-permute-start | bytes 233480 | tf_op jit(solution)/shard_map/ppermute | solution.py:271
  25.9 5.4 %collective-permute-start.14 = (bf16[8,4864]{1,0:T(8,128)(2,1)S(1)}, bf16[8,4864]{1,0:T(8,128)(2,1)S(1)}, u32[]{:S(2)}, u32[]{:S(2)}) collective-permute-start(bf16[8,4864]{1,0:T(8,128)(2,1)S(1)} %add_convert_fusion.6), channel_id=1, source_target_pairs={{0,6},{1,7},{2,4},{3,5},{4,2},{5,3},{6,0},{7,1},{8,14},{9,15},{10,... | collective-permute-start | bytes 233480 | tf_op jit(solution)/shard_map/ppermute | solution.py:271
  27.1 7.6 %collective-permute-start.19 = (bf16[8,4864]{1,0:T(8,128)(2,1)S(1)}, bf16[8,4864]{1,0:T(8,128)(2,1)S(1)}, u32[]{:S(2)}, u32[]{:S(2)}) collective-permute-start(bf16[8,4864]{1,0:T(8,128)(2,1)S(1)} %get-tuple-element.64), channel_id=1, source_target_pairs={{0,1},{1,0},{2,3},{3,2},{4,5},{5,4},{6,7},{7,6},{8,9},{9,8},{10,11... | collective-permute-start | bytes 233480 | tf_op jit(solution)/shard_map/ppermute | solution.py:271
  27.1 1.4 %collective-permute-start.22 = (bf16[8,4864]{1,0:T(8,128)(2,1)S(1)}, bf16[8,4864]{1,0:T(8,128)(2,1)S(1)}, u32[]{:S(2)}, u32[]{:S(2)}) collective-permute-start(bf16[8,4864]{1,0:T(8,128)(2,1)S(1)} %get-tuple-element.69), channel_id=1, source_target_pairs={{0,1},{1,0},{2,3},{3,2},{4,5},{5,4},{6,7},{7,6},{8,9},{9,8},{10,11... | collective-permute-start | bytes 233480 | tf_op jit(solution)/shard_map/ppermute | solution.py:271
  27.7 2.4 %collective-permute-start.24 = (bf16[8,4864]{1,0:T(8,128)(2,1)S(1)}, bf16[8,4864]{1,0:T(8,128)(2,1)S(1)}, u32[]{:S(2)}, u32[]{:S(2)}) collective-permute-start(bf16[8,4864]{1,0:T(8,128)(2,1)S(1)} %get-tuple-element.71), channel_id=1, source_target_pairs={{0,1},{1,0},{2,3},{3,2},{4,5},{5,4},{6,7},{7,6},{8,9},{9,8},{10,11... | collective-permute-start | bytes 233480 | tf_op jit(solution)/shard_map/ppermute | solution.py:271
  28.5 4.6 %collective-permute-start.16 = (bf16[8,4864]{1,0:T(8,128)(2,1)S(1)}, bf16[8,4864]{1,0:T(8,128)(2,1)S(1)}, u32[]{:S(2)}, u32[]{:S(2)}) collective-permute-start(bf16[8,4864]{1,0:T(8,128)(2,1)S(1)} %add_convert_fusion.5), channel_id=1, source_target_pairs={{0,4},{1,5},{2,6},{3,7},{4,0},{5,1},{6,2},{7,3},{8,12},{9,13},{10,... | collective-permute-start | bytes 233480 | tf_op jit(solution)/shard_map/ppermute | solution.py:271
  30.1 4.6 %collective-permute-start.18 = (bf16[8,4864]{1,0:T(8,128)(2,1)S(1)}, bf16[8,4864]{1,0:T(8,128)(2,1)S(1)}, u32[]{:S(2)}, u32[]{:S(2)}) collective-permute-start(bf16[8,4864]{1,0:T(8,128)(2,1)S(1)} %add_convert_fusion.4), channel_id=1, source_target_pairs={{0,2},{1,3},{2,0},{3,1},{4,6},{5,7},{6,4},{7,5},{8,10},{9,11},{10,... | collective-permute-start | bytes 233480 | tf_op jit(solution)/shard_map/ppermute | solution.py:271
  31.0 7.7 %collective-permute-start.21 = (bf16[8,4864]{1,0:T(8,128)(2,1)S(1)}, bf16[8,4864]{1,0:T(8,128)(2,1)S(1)}, u32[]{:S(2)}, u32[]{:S(2)}) collective-permute-start(bf16[8,4864]{1,0:T(8,128)(2,1)S(1)} %get-tuple-element.67), channel_id=1, source_target_pairs={{0,1},{1,0},{2,3},{3,2},{4,5},{5,4},{6,7},{7,6},{8,9},{9,8},{10,11... | collective-permute-start | bytes 233480 | tf_op jit(solution)/shard_map/ppermute | solution.py:271
  31.3 7.5 %collective-permute-start.23 = (bf16[8,4864]{1,0:T(8,128)(2,1)S(1)}, bf16[8,4864]{1,0:T(8,128)(2,1)S(1)}, u32[]{:S(2)}, u32[]{:S(2)}) collective-permute-start(bf16[8,4864]{1,0:T(8,128)(2,1)S(1)} %add_convert_fusion.1), channel_id=1, source_target_pairs={{0,6},{1,7},{2,4},{3,5},{4,2},{5,3},{6,0},{7,1},{8,14},{9,15},{10,... | collective-permute-start | bytes 233480 | tf_op jit(solution)/shard_map/ppermute | solution.py:271
  33.2 5.8 %collective-permute-start.25 = (bf16[8,4864]{1,0:T(8,128)(2,1)S(1)}, bf16[8,4864]{1,0:T(8,128)(2,1)S(1)}, u32[]{:S(2)}, u32[]{:S(2)}) collective-permute-start(bf16[8,4864]{1,0:T(8,128)(2,1)S(1)} %add_convert_fusion), channel_id=1, source_target_pairs={{0,4},{1,5},{2,6},{3,7},{4,0},{5,1},{6,2},{7,3},{8,12},{9,13},{10,... | collective-permute-start | bytes 233480 | tf_op jit(solution)/shard_map/ppermute | solution.py:271
  34.8 6.1 %collective-permute-start.20 = (bf16[8,4864]{1,0:T(8,128)(2,1)S(1)}, bf16[8,4864]{1,0:T(8,128)(2,1)S(1)}, u32[]{:S(2)}, u32[]{:S(2)}) collective-permute-start(bf16[8,4864]{1,0:T(8,128)(2,1)S(1)} %add_convert_fusion.3), channel_id=1, source_target_pairs={{0,8},{1,9},{2,10},{3,11},{4,12},{5,13},{6,14},{7,15},{8,0},{9,1},... | collective-permute-start | bytes 233480 | tf_op jit(solution)/shard_map/ppermute | solution.py:271
  37.3 4.4 %collective-permute-start.26 = (bf16[8,4864]{1,0:T(8,128)(2,1)S(1)}, bf16[8,4864]{1,0:T(8,128)(2,1)S(1)}, u32[]{:S(2)}, u32[]{:S(2)}) collective-permute-start(bf16[8,4864]{1,0:T(8,128)(2,1)S(1)} %add_convert_fusion.2), channel_id=1, source_target_pairs={{0,2},{1,3},{2,0},{3,1},{4,6},{5,7},{6,4},{7,5},{8,10},{9,11},{10,... | collective-permute-start | bytes 233480 | tf_op jit(solution)/shard_map/ppermute | solution.py:271

commit v6 on v5

--- a/solution.py
+++ b/solution.py
@@ -45,7 +45,7 @@
 
 
 def pack_kernel(copies, experts, routes_far, hidden_far, *refs):
-    out_refs, (routes_ref, hidden_ref, packed_ref, sems) = refs[:experts], refs[experts:]
+    out_refs, (routes_ref, hidden_ref, sems) = refs[:experts], refs[experts:]
     moves = [(routes_far, routes_ref), (hidden_far, hidden_ref)]
     moves = [pltpu.make_async_copy(x, y, sems.at[k]) for k, (x, y) in enumerate(moves)]
     for move in moves:
@@ -62,14 +62,9 @@
     pick = jnp.concatenate(picks, axis=0).astype(jnp.bfloat16)
     moves[1].wait()
     sorted_rows = jnp.dot(pick, hidden_ref[...], preferred_element_type=jnp.float32)
-    lasts = []
-    for k in range(experts)[::-1]:
+    for k in range(experts):
         rows = sorted_rows[k * tok_rows : (k + 1) * tok_rows]
-        packed_ref[k] = folded(rows[:, :stay], rows[:, stay:], slots, per).astype(jnp.bfloat16)
-        lasts.append(pltpu.make_async_copy(packed_ref.at[k], out_refs[k], sems.at[2 + k]))
-        lasts[-1].start()
-    for last in lasts:
-        last.wait()
+        out_refs[k][...] = folded(rows[:, :stay], rows[:, stay:], slots, per).astype(jnp.bfloat16)
 
 
 def packed_rows(routes, hidden_in, copies, experts):
@@ -80,12 +75,11 @@
         functools.partial(pack_kernel, copies, experts),
         out_shape=[jax.ShapeDtypeStruct((tok_rows, stay), jnp.bfloat16)] * experts,
         in_specs=[pl.BlockSpec(memory_space=pltpu.HBM)] * 2,
-        out_specs=[pl.BlockSpec(memory_space=pl.ANY)] * experts,
+        out_specs=[pl.BlockSpec(memory_space=pltpu.VMEM)] * experts,
         scratch_shapes=[
             pltpu.VMEM(routes.shape, jnp.int32),
             pltpu.VMEM(hidden_in.shape, jnp.bfloat16),
-            pltpu.VMEM((experts, tok_rows, stay), jnp.bfloat16),
-            pltpu.SemaphoreType.DMA((2 + experts,)),
+            pltpu.SemaphoreType.DMA((2,)),
         ],
         compiler_params=pltpu.CompilerParams(vmem_limit_bytes=8 * 1024 * 1024),
     )(*far)
@@ -218,16 +212,16 @@
     logit = jnp.sum(jnp.where(columns == own, logits, 0.0), axis=1, keepdims=True)
     scores = 1.0 / (1.0 + jnp.exp(-logit))
     gate, up = lifted[:, :units], lifted[:, units:]
-    act = (gate / (1.0 + jnp.exp(-gate)) * up).astype(jnp.bfloat16)
+    act = (gate / (1.0 + jnp.exp(-gate)) * up * scores).astype(jnp.bfloat16)
     for move in waits:
         move.wait()
-    ends = jnp.dot(act, down_held[:, stay:], preferred_element_type=jnp.float32) * scores
+    ends = jnp.dot(act, down_held[:, stay:], preferred_element_type=jnp.float32)
     lines = {}
     for k in range(count):
         rest_rows = ends[k * tok_rows : (k + 1) * tok_rows]
         lines[k] = folded(jnp.zeros((tok_rows, stay), jnp.float32), rest_rows, slots, per)[slots:]
     for at, size_at in parts[:-1]:
-        output = jnp.dot(act, down_held[:, at : at + size_at], preferred_element_type=jnp.float32) * scores
+        output = jnp.dot(act, down_held[:, at : at + size_at], preferred_element_type=jnp.float32)
         for k in range(count):
             rows = [output[k * tok_rows : k * tok_rows + slots], lines[k][:, at : at + size_at]]
             out_refs[k][:, at : at + size_at] = jnp.concatenate(rows, axis=0).astype(jnp.bfloat16)

time: 43.2 us -> 42.9 us (level)
  no operation moved by 1% of the time
where the time goes in v6:
time: 42.9 us; the launch traced here: 42.8 us
  starting transfers between devices  24.5 us (57%)
  Pallas kernels  10.5 us (24%)
  waiting for transfers between devices  7.41 us (17%)
    ppermute x27, starting transfers between devices, swap(): lax.ppermute(block, 'expert', [(i, i ^ mask) for i in range(axis_len)])  24.5 us
    ppermute x27, waiting for transfers between devices, swap(): lax.ppermute(block, 'expert', [(i, i ^ mask) for i in range(axis_len)])  7.41 us
    pallas_call x1, Pallas kernels, expert_rows(): pl.pallas_call(functools.partial(expert_kernel, copies, size, count), out...  4.82 us
    pallas_call x1, Pallas kernels, fetched(): pl.pallas_call(functools.partial(fetch_kernel, count, size), out_shape=[j...  3.16 us
    pallas_call x1, Pallas kernels, placed_rows(): pl.pallas_call(functools.partial(final_kernel, copies, experts, len(near_...  1.32 us
    pallas_call x1, Pallas kernels, packed_rows(): pl.pallas_call(functools.partial(pack_kernel, copies, experts), out_shape...  1.15 us
  transfers between devices with their start and end apart: 27, of which 14 were waited for; matrix products, arithmetic and copies ran while one was open for 0% of the time, Pallas kernels for 7%

profile of v6, /device:TPU:0, one launch (start us, length us, event | category | flops | bytes accessed | tf_op | source)
XLA Modules:
  0.0 42.8 jit_solution(13336075029720519849)
XLA Ops:
  0.0 1.1 %shard_map.64 = (bf16[8,4864]{1,0:T(8,128)(2,1)S(1)}, bf16[8,4864]{1,0:T(8,128)(2,1)S(1)}) custom-call(s32[1,8]{1,0:T(1,128)} %bitcast.7, bf16[8,6400]{1,0:T(8,128)(2,1)} %hidden_far.3), custom_call_target="tpu_custom_call" | custom-call | tf_op jit(solution)/shard_map/pallas_call | solution.py:74
  1.2 4.1 %collective-permute-start.3 = (bf16[8,4864]{1,0:T(8,128)(2,1)S(1)}, bf16[8,4864]{1,0:T(8,128)(2,1)S(1)}, u32[]{:S(2)}, u32[]{:S(2)}) collective-permute-start(bf16[8,4864]{1,0:T(8,128)(2,1)S(1)} %get-tuple-element.42), channel_id=1, source_target_pairs={{0,8},{1,9},{2,10},{3,11},{4,12},{5,13},{6,14},{7,15},{8,0},{9,1},... | collective-permute-start | bytes 233480 | tf_op jit(solution)/shard_map/ppermute | solution.py:265
  5.3 1.5 %collective-permute-start.2 = (bf16[8,4864]{1,0:T(8,128)(2,1)S(1)}, bf16[8,4864]{1,0:T(8,128)(2,1)S(1)}, u32[]{:S(2)}, u32[]{:S(2)}) collective-permute-start(bf16[8,4864]{1,0:T(8,128)(2,1)S(1)} %get-tuple-element.39.refs_3_), channel_id=1, source_target_pairs={{0,2},{1,3},{2,0},{3,1},{4,6},{5,7},{6,4},{7,5},{8,10},{9,11},{10,... | collective-permute-start | bytes 233480 | tf_op jit(solution)/shard_map/ppermute | solution.py:265
  6.8 1.6 %collective-permute-start.1 = (bf16[8,4864]{1,0:T(8,128)(2,1)S(1)}, bf16[8,4864]{1,0:T(8,128)(2,1)S(1)}, u32[]{:S(2)}, u32[]{:S(2)}) collective-permute-start(bf16[8,4864]{1,0:T(8,128)(2,1)S(1)} %get-tuple-element.39.refs_3_), channel_id=1, source_target_pairs={{0,4},{1,5},{2,6},{3,7},{4,0},{5,1},{6,2},{7,3},{8,12},{9,13},{10,... | collective-permute-start | bytes 233480 | tf_op jit(solution)/shard_map/ppermute | solution.py:265
  8.3 0.4 collective-permute-start
  8.7 0.3 collective-permute-done.3.refs_2_
  9.1 1.6 %collective-permute-start.6 = (bf16[8,4864]{1,0:T(8,128)(2,1)S(1)}, bf16[8,4864]{1,0:T(8,128)(2,1)S(1)}, u32[]{:S(2)}, u32[]{:S(2)}) collective-permute-start(bf16[8,4864]{1,0:T(8,128)(2,1)S(1)} %collective-permute-done.3.refs_2_), channel_id=1, source_target_pairs={{0,2},{1,3},{2,0},{3,1},{4,6},{5,7},{6,4},{7,5},{8,10},{9,11},{10,... | collective-permute-start | bytes 233480 | tf_op jit(solution)/shard_map/ppermute | solution.py:265
  10.7 1.1 %collective-permute-start.5 = (bf16[8,4864]{1,0:T(8,128)(2,1)S(1)}, bf16[8,4864]{1,0:T(8,128)(2,1)S(1)}, u32[]{:S(2)}, u32[]{:S(2)}) collective-permute-start(bf16[8,4864]{1,0:T(8,128)(2,1)S(1)} %collective-permute-done.3.refs_2_), channel_id=1, source_target_pairs={{0,4},{1,5},{2,6},{3,7},{4,0},{5,1},{6,2},{7,3},{8,12},{9,13},{10,... | collective-permute-start | bytes 233480 | tf_op jit(solution)/shard_map/ppermute | solution.py:265
  11.8 1.2 %collective-permute-start.4 = (bf16[8,4864]{1,0:T(8,128)(2,1)S(1)}, bf16[8,4864]{1,0:T(8,128)(2,1)S(1)}, u32[]{:S(2)}, u32[]{:S(2)}) collective-permute-start(bf16[8,4864]{1,0:T(8,128)(2,1)S(1)} %collective-permute-done.3.refs_2_), channel_id=1, source_target_pairs={{0,6},{1,7},{2,4},{3,5},{4,2},{5,3},{6,0},{7,1},{8,14},{9,15},{10,... | collective-permute-start | bytes 233480 | tf_op jit(solution)/shard_map/ppermute | solution.py:265
  13.0 0.7 %collective-permute-done.refs_4_ = bf16[8,4864]{1,0:T(8,128)(2,1)S(1)} collective-permute-done((bf16[8,4864]{1,0:T(8,128)(2,1)S(1)}, bf16[8,4864]{1,0:T(8,128)(2,1)S(1)}, u32[]{:S(2)}, u32[]{:S(2)}) %collective-permute-start) | collective-permute-done | bytes 77856 | tf_op jit(solution)/shard_map/ppermute | solution.py:265
  13.8 3.2 %shard_map.65 = (bf16[576,6400]{1,0:T(8,128)(2,1)S(1)}, bf16[2,6400]{1,0:T(2,128)(2,1)S(1)}, f32[50,128]{1,0:T(8,128)S(1)}, bf16[4,8,4864]{2,1,0:T(8,128)(2,1)S(1)}) custom-call(bf16[576,6400]{1,0:T(8,128)(2,1)} %bitcast.9, bf16[2,6400]{1,0:T(2,128)(2,1)} %bitcast.12, f32[50,128]{1,0:T(8,128)} %bitcast.11, bf16[8,4864]{1,0:T(8,128)(2,1)S(1)} %get-tuple-element.39.refs_3_, ...), custom_call_target="tpu_custom_call" | custom-call | bytes 7424000 | tf_op jit(solution)/shard_map/pallas_call | solution.py:151
  17.1 0.5 %collective-permute-start.8 = (bf16[8,4864]{1,0:T(8,128)(2,1)S(1)}, bf16[8,4864]{1,0:T(8,128)(2,1)S(1)}, u32[]{:S(2)}, u32[]{:S(2)}) collective-permute-start(bf16[8,4864]{1,0:T(8,128)(2,1)S(1)} %collective-permute-done.3.refs_2_), channel_id=1, source_target_pairs={{0,1},{1,0},{2,3},{3,2},{4,5},{5,4},{6,7},{7,6},{8,9},{9,8},{10,11... | collective-permute-start | bytes 233480 | tf_op jit(solution)/shard_map/ppermute | solution.py:265
  17.7 0.5 %collective-permute-start.10 = (bf16[8,4864]{1,0:T(8,128)(2,1)S(1)}, bf16[8,4864]{1,0:T(8,128)(2,1)S(1)}, u32[]{:S(2)}, u32[]{:S(2)}) collective-permute-start(bf16[8,4864]{1,0:T(8,128)(2,1)S(1)} %collective-permute-done.5.refs_4_), channel_id=1, source_target_pairs={{0,1},{1,0},{2,3},{3,2},{4,5},{5,4},{6,7},{7,6},{8,9},{9,8},{10,11... | collective-permute-start | bytes 233480 | tf_op jit(solution)/shard_map/ppermute | solution.py:265
  18.2 0.7 %collective-permute-done.8.refs_6_ = bf16[8,4864]{1,0:T(8,128)(2,1)S(1)} collective-permute-done((bf16[8,4864]{1,0:T(8,128)(2,1)S(1)}, bf16[8,4864]{1,0:T(8,128)(2,1)S(1)}, u32[]{:S(2)}, u32[]{:S(2)}) %collective-permute-start.8) | collective-permute-done | bytes 77856 | tf_op jit(solution)/shard_map/ppermute | solution.py:265
  19.1 0.4 collective-permute-done.11.refs_9_
  19.4 4.8 %shard_map.66 = (bf16[8,4864]{1,0:T(8,128)(2,1)S(1)}, bf16[8,4864]{1,0:T(8,128)(2,1)S(1)}, bf16[8,4864]{1,0:T(8,128)(2,1)S(1)}, bf16[8,4864]{1,0:T(8,128)(2,1)S(...) custom-call(bf16[4,8,4864]{2,1,0:T(8,128)(2,1)S(1)} %get-tuple-eleme, ...), custom_call_target="tpu_custom_call" | custom-call | flops 1415577600 | bytes 11059200 | tf_op jit(solution)/shard_map/pallas_call | solution.py:237
  24.5 0.4 collective-permute-start.12
  25.0 0.4 collective-permute-start.17
  25.6 1.2 %collective-permute-start.14 = (bf16[8,4864]{1,0:T(8,128)(2,1)S(1)}, bf16[8,4864]{1,0:T(8,128)(2,1)S(1)}, u32[]{:S(2)}, u32[]{:S(2)}) collective-permute-start(bf16[8,4864]{1,0:T(8,128)(2,1)S(1)} %add_convert_fusion.6), channel_id=1, source_target_pairs={{0,6},{1,7},{2,4},{3,5},{4,2},{5,3},{6,0},{7,1},{8,14},{9,15},{10,... | collective-permute-start | bytes 233480 | tf_op jit(solution)/shard_map/ppermute | solution.py:265
  26.9 0.5 %collective-permute-start.22 = (bf16[8,4864]{1,0:T(8,128)(2,1)S(1)}, bf16[8,4864]{1,0:T(8,128)(2,1)S(1)}, u32[]{:S(2)}, u32[]{:S(2)}) collective-permute-start(bf16[8,4864]{1,0:T(8,128)(2,1)S(1)} %get-tuple-element.69), channel_id=1, source_target_pairs={{0,1},{1,0},{2,3},{3,2},{4,5},{5,4},{6,7},{7,6},{8,9},{9,8},{10,11... | collective-permute-start | bytes 233480 | tf_op jit(solution)/shard_map/ppermute | solution.py:265
  27.5 0.8 %collective-permute-done.22 = bf16[8,4864]{1,0:T(8,128)(2,1)S(1)} collective-permute-done((bf16[8,4864]{1,0:T(8,128)(2,1)S(1)}, bf16[8,4864]{1,0:T(8,128)(2,1)S(1)}, u32[]{:S(2)}, u32[]{:S(2)}) %collective-permute-start.22) | collective-permute-done | bytes 77856 | tf_op jit(solution)/shard_map/ppermute | solution.py:265
  28.3 1.5 %collective-permute-start.16 = (bf16[8,4864]{1,0:T(8,128)(2,1)S(1)}, bf16[8,4864]{1,0:T(8,128)(2,1)S(1)}, u32[]{:S(2)}, u32[]{:S(2)}) collective-permute-start(bf16[8,4864]{1,0:T(8,128)(2,1)S(1)} %add_convert_fusion.5), channel_id=1, source_target_pairs={{0,4},{1,5},{2,6},{3,7},{4,0},{5,1},{6,2},{7,3},{8,12},{9,13},{10,... | collective-permute-start | bytes 233480 | tf_op jit(solution)/shard_map/ppermute | solution.py:265
  29.9 0.9 %collective-permute-start.18 = (bf16[8,4864]{1,0:T(8,128)(2,1)S(1)}, bf16[8,4864]{1,0:T(8,128)(2,1)S(1)}, u32[]{:S(2)}, u32[]{:S(2)}) collective-permute-start(bf16[8,4864]{1,0:T(8,128)(2,1)S(1)} %add_convert_fusion.4), channel_id=1, source_target_pairs={{0,2},{1,3},{2,0},{3,1},{4,6},{5,7},{6,4},{7,5},{8,10},{9,11},{10,... | collective-permute-start | bytes 233480 | tf_op jit(solution)/shard_map/ppermute | solution.py:265
  31.0 1.2 %collective-permute-start.23 = (bf16[8,4864]{1,0:T(8,128)(2,1)S(1)}, bf16[8,4864]{1,0:T(8,128)(2,1)S(1)}, u32[]{:S(2)}, u32[]{:S(2)}) collective-permute-start(bf16[8,4864]{1,0:T(8,128)(2,1)S(1)} %add_convert_fusion.1), channel_id=1, source_target_pairs={{0,6},{1,7},{2,4},{3,5},{4,2},{5,3},{6,0},{7,1},{8,14},{9,15},{10,... | collective-permute-start | bytes 233480 | tf_op jit(solution)/shard_map/ppermute | solution.py:265
  32.2 0.7 %collective-permute-done.16 = bf16[8,4864]{1,0:T(8,128)(2,1)S(1)} collective-permute-done((bf16[8,4864]{1,0:T(8,128)(2,1)S(1)}, bf16[8,4864]{1,0:T(8,128)(2,1)S(1)}, u32[]{:S(2)}, u32[]{:S(2)}) %collective-permute-start.16) | collective-permute-done | bytes 77856 | tf_op jit(solution)/shard_map/ppermute | solution.py:265
  32.9 1.5 %collective-permute-start.25 = (bf16[8,4864]{1,0:T(8,128)(2,1)S(1)}, bf16[8,4864]{1,0:T(8,128)(2,1)S(1)}, u32[]{:S(2)}, u32[]{:S(2)}) collective-permute-start(bf16[8,4864]{1,0:T(8,128)(2,1)S(1)} %add_convert_fusion), channel_id=1, source_target_pairs={{0,4},{1,5},{2,6},{3,7},{4,0},{5,1},{6,2},{7,3},{8,12},{9,13},{10,... | collective-permute-start | bytes 233480 | tf_op jit(solution)/shard_map/ppermute | solution.py:265
  34.5 2.5 %collective-permute-start.20 = (bf16[8,4864]{1,0:T(8,128)(2,1)S(1)}, bf16[8,4864]{1,0:T(8,128)(2,1)S(1)}, u32[]{:S(2)}, u32[]{:S(2)}) collective-permute-start(bf16[8,4864]{1,0:T(8,128)(2,1)S(1)} %add_convert_fusion.3), channel_id=1, source_target_pairs={{0,8},{1,9},{2,10},{3,11},{4,12},{5,13},{6,14},{7,15},{8,0},{9,1},... | collective-permute-start | bytes 233480 | tf_op jit(solution)/shard_map/ppermute | solution.py:265
  37.0 1.4 %collective-permute-start.26 = (bf16[8,4864]{1,0:T(8,128)(2,1)S(1)}, bf16[8,4864]{1,0:T(8,128)(2,1)S(1)}, u32[]{:S(2)}, u32[]{:S(2)}) collective-permute-start(bf16[8,4864]{1,0:T(8,128)(2,1)S(1)} %add_convert_fusion.2), channel_id=1, source_target_pairs={{0,2},{1,3},{2,0},{3,1},{4,6},{5,7},{6,4},{7,5},{8,10},{9,11},{10,... | collective-permute-start | bytes 233480 | tf_op jit(solution)/shard_map/ppermute | solution.py:265
  38.5 0.3 collective-permute-done.25.refs_3_
  38.8 1.9 %collective-permute-done.20.refs_0_ = bf16[8,4864]{1,0:T(8,128)(2,1)S(1)} collective-permute-done((bf16[8,4864]{1,0:T(8,128)(2,1)S(1)}, bf16[8,4864]{1,0:T(8,128)(2,1)S(1)}, u32[]{:S(2)}, u32[]{:S(2)}) %collective-permute-start.20) | collective-permute-done | bytes 77856 | tf_op jit(solution)/shard_map/ppermute | solution.py:265
  40.7 0.8 %collective-permute-done.26.refs_4_ = bf16[8,4864]{1,0:T(8,128)(2,1)S(1)} collective-permute-done((bf16[8,4864]{1,0:T(8,128)(2,1)S(1)}, bf16[8,4864]{1,0:T(8,128)(2,1)S(1)}, u32[]{:S(2)}, u32[]{:S(2)}) %collective-permute-start.26) | collective-permute-done | bytes 77856 | tf_op jit(solution)/shard_map/ppermute | solution.py:265
  41.4 1.3 %shard_map.67 = bf16[8,6400]{1,0:T(8,128)(2,1)} custom-call(s32[1,8]{1,0:T(1,128)S(1)} %bitcast.8, bf16[8,6400]{1,0:T(8,128)(2,1)S(1)} %copy-done, bf16[8,4864]{1,0:T(8,128)(2,1)S(1)} %collective-permute-done.20.refs_0_, f32[8,4864]{1,0:T(8,128)S(1)} %convert_add_fusion.refs_1_, bf16[8,4864]{1,0:T(8,128)(2,1)S(1)} %collective-permute-done.23.refs_2_, ...), custom_call_target="tpu_custom_call" | custom-call | tf_op jit(solution)/shard_map/pallas_call | solution.py:121
  (38 shorter events, 1.6 us)
Async XLA Ops:
  1.2 7.9 %collective-permute-start.3 = (bf16[8,4864]{1,0:T(8,128)(2,1)S(1)}, bf16[8,4864]{1,0:T(8,128)(2,1)S(1)}, u32[]{:S(2)}, u32[]{:S(2)}) collective-permute-start(bf16[8,4864]{1,0:T(8,128)(2,1)S(1)} %get-tuple-element.42), channel_id=1, source_target_pairs={{0,8},{1,9},{2,10},{3,11},{4,12},{5,13},{6,14},{7,15},{8,0},{9,1},... | collective-permute-start | bytes 233480 | tf_op jit(solution)/shard_map/ppermute | solution.py:265
  5.3 6.6 %collective-permute-start.2 = (bf16[8,4864]{1,0:T(8,128)(2,1)S(1)}, bf16[8,4864]{1,0:T(8,128)(2,1)S(1)}, u32[]{:S(2)}, u32[]{:S(2)}) collective-permute-start(bf16[8,4864]{1,0:T(8,128)(2,1)S(1)} %get-tuple-element.39.refs_3_), channel_id=1, source_target_pairs={{0,2},{1,3},{2,0},{3,1},{4,6},{5,7},{6,4},{7,5},{8,10},{9,11},{10,... | collective-permute-start | bytes 233480 | tf_op jit(solution)/shard_map/ppermute | solution.py:265
  6.8 6.2 %collective-permute-start.1 = (bf16[8,4864]{1,0:T(8,128)(2,1)S(1)}, bf16[8,4864]{1,0:T(8,128)(2,1)S(1)}, u32[]{:S(2)}, u32[]{:S(2)}) collective-permute-start(bf16[8,4864]{1,0:T(8,128)(2,1)S(1)} %get-tuple-element.39.refs_3_), channel_id=1, source_target_pairs={{0,4},{1,5},{2,6},{3,7},{4,0},{5,1},{6,2},{7,3},{8,12},{9,13},{10,... | collective-permute-start | bytes 233480 | tf_op jit(solution)/shard_map/ppermute | solution.py:265
  8.3 5.4 %collective-permute-start = (bf16[8,4864]{1,0:T(8,128)(2,1)S(1)}, bf16[8,4864]{1,0:T(8,128)(2,1)S(1)}, u32[]{:S(2)}, u32[]{:S(2)}) collective-permute-start(bf16[8,4864]{1,0:T(8,128)(2,1)S(1)} %get-tuple-element.39.refs_3_), channel_id=1, source_target_pairs={{0,6},{1,7},{2,4},{3,5},{4,2},{5,3},{6,0},{7,1},{8,14},{9,15},{10,... | collective-permute-start | bytes 233480 | tf_op jit(solution)/shard_map/ppermute | solution.py:265
  9.1 7.9 %collective-permute-start.6 = (bf16[8,4864]{1,0:T(8,128)(2,1)S(1)}, bf16[8,4864]{1,0:T(8,128)(2,1)S(1)}, u32[]{:S(2)}, u32[]{:S(2)}) collective-permute-start(bf16[8,4864]{1,0:T(8,128)(2,1)S(1)} %collective-permute-done.3.refs_2_), channel_id=1, source_target_pairs={{0,2},{1,3},{2,0},{3,1},{4,6},{5,7},{6,4},{7,5},{8,10},{9,11},{10,... | collective-permute-start | bytes 233480 | tf_op jit(solution)/shard_map/ppermute | solution.py:265
  10.7 6.3 %collective-permute-start.5 = (bf16[8,4864]{1,0:T(8,128)(2,1)S(1)}, bf16[8,4864]{1,0:T(8,128)(2,1)S(1)}, u32[]{:S(2)}, u32[]{:S(2)}) collective-permute-start(bf16[8,4864]{1,0:T(8,128)(2,1)S(1)} %collective-permute-done.3.refs_2_), channel_id=1, source_target_pairs={{0,4},{1,5},{2,6},{3,7},{4,0},{5,1},{6,2},{7,3},{8,12},{9,13},{10,... | collective-permute-start | bytes 233480 | tf_op jit(solution)/shard_map/ppermute | solution.py:265
  11.8 5.3 %collective-permute-start.4 = (bf16[8,4864]{1,0:T(8,128)(2,1)S(1)}, bf16[8,4864]{1,0:T(8,128)(2,1)S(1)}, u32[]{:S(2)}, u32[]{:S(2)}) collective-permute-start(bf16[8,4864]{1,0:T(8,128)(2,1)S(1)} %collective-permute-done.3.refs_2_), channel_id=1, source_target_pairs={{0,6},{1,7},{2,4},{3,5},{4,2},{5,3},{6,0},{7,1},{8,14},{9,15},{10,... | collective-permute-start | bytes 233480 | tf_op jit(solution)/shard_map/ppermute | solution.py:265
  16.9 24.5 %copy-start = (bf16[8,6400]{1,0:T(8,128)(2,1)S(1)}, bf16[8,6400]{1,0:T(8,128)(2,1)}, u32[]{:S(2)}) copy-start(bf16[8,6400]{1,0:T(8,128)(2,1)} %hidden_far.3) | copy-start | bytes 307204
  16.9 24.5 %copy-start.1 = (s32[8,1]{0,1:T(1,128)S(1)}, s32[8,1]{0,1:T(1,128)}, u32[]{:S(2)}) copy-start(s32[8,1]{0,1:T(1,128)} %param.9) | copy-start | bytes 100
  17.1 2.3 %collective-permute-start.7 = (bf16[4,8,4864]{2,1,0:T(8,128)(2,1)S(1)}, bf16[4,8,4864]{2,1,0:T(8,128)(2,1)S(1)}, u32[]{:S(2)}, u32[]{:S(2)}) collective-permute-start(bf16[4,8,4864]{2,1,0:T(8,128)(2,1)S(1)} %get-tuple-element.43.refs_0_), channel_id=1, source_target_pairs={{0,1},{1,0},{2,3},{3,2},{4,5},{5,4},{6,7},{7,6},{8,9},{9,8},{10,11... | collective-permute-start | bytes 933896 | tf_op jit(solution)/shard_map/ppermute | solution.py:265
  17.1 1.7 %collective-permute-start.8 = (bf16[8,4864]{1,0:T(8,128)(2,1)S(1)}, bf16[8,4864]{1,0:T(8,128)(2,1)S(1)}, u32[]{:S(2)}, u32[]{:S(2)}) collective-permute-start(bf16[8,4864]{1,0:T(8,128)(2,1)S(1)} %collective-permute-done.3.refs_2_), channel_id=1, source_target_pairs={{0,1},{1,0},{2,3},{3,2},{4,5},{5,4},{6,7},{7,6},{8,9},{9,8},{10,11... | collective-permute-start | bytes 233480 | tf_op jit(solution)/shard_map/ppermute | solution.py:265
  17.7 1.3 %collective-permute-start.9 = (bf16[8,4864]{1,0:T(8,128)(2,1)S(1)}, bf16[8,4864]{1,0:T(8,128)(2,1)S(1)}, u32[]{:S(2)}, u32[]{:S(2)}) collective-permute-start(bf16[8,4864]{1,0:T(8,128)(2,1)S(1)} %collective-permute-done.4.refs_3_), channel_id=1, source_target_pairs={{0,1},{1,0},{2,3},{3,2},{4,5},{5,4},{6,7},{7,6},{8,9},{9,8},{10,11... | collective-permute-start | bytes 233480 | tf_op jit(solution)/shard_map/ppermute | solution.py:265
  17.7 1.4 %collective-permute-start.10 = (bf16[8,4864]{1,0:T(8,128)(2,1)S(1)}, bf16[8,4864]{1,0:T(8,128)(2,1)S(1)}, u32[]{:S(2)}, u32[]{:S(2)}) collective-permute-start(bf16[8,4864]{1,0:T(8,128)(2,1)S(1)} %collective-permute-done.5.refs_4_), channel_id=1, source_target_pairs={{0,1},{1,0},{2,3},{3,2},{4,5},{5,4},{6,7},{7,6},{8,9},{9,8},{10,11... | collective-permute-start | bytes 233480 | tf_op jit(solution)/shard_map/ppermute | solution.py:265
  18.2 1.3 %collective-permute-start.11 = (bf16[8,4864]{1,0:T(8,128)(2,1)S(1)}, bf16[8,4864]{1,0:T(8,128)(2,1)S(1)}, u32[]{:S(2)}, u32[]{:S(2)}) collective-permute-start(bf16[8,4864]{1,0:T(8,128)(2,1)S(1)} %collective-permute-done.6.refs_5_), channel_id=1, source_target_pairs={{0,1},{1,0},{2,3},{3,2},{4,5},{5,4},{6,7},{7,6},{8,9},{9,8},{10,11... | collective-permute-start | bytes 233480 | tf_op jit(solution)/shard_map/ppermute | solution.py:265
  24.3 1.3 %collective-permute-start.13 = (bf16[8,4864]{1,0:T(8,128)(2,1)S(1)}, bf16[8,4864]{1,0:T(8,128)(2,1)S(1)}, u32[]{:S(2)}, u32[]{:S(2)}) collective-permute-start(bf16[8,4864]{1,0:T(8,128)(2,1)S(1)} %get-tuple-element.53), channel_id=1, source_target_pairs={{0,1},{1,0},{2,3},{3,2},{4,5},{5,4},{6,7},{7,6},{8,9},{9,8},{10,11... | collective-permute-start | bytes 233480 | tf_op jit(solution)/shard_map/ppermute | solution.py:265
  24.5 6.3 %collective-permute-start.12 = (bf16[8,4864]{1,0:T(8,128)(2,1)S(1)}, bf16[8,4864]{1,0:T(8,128)(2,1)S(1)}, u32[]{:S(2)}, u32[]{:S(2)}) collective-permute-start(bf16[8,4864]{1,0:T(8,128)(2,1)S(1)} %get-tuple-element.51), channel_id=1, source_target_pairs={{0,1},{1,0},{2,3},{3,2},{4,5},{5,4},{6,7},{7,6},{8,9},{9,8},{10,11... | collective-permute-start | bytes 233480 | tf_op jit(solution)/shard_map/ppermute | solution.py:265
  24.8 2.0 %collective-permute-start.15 = (bf16[8,4864]{1,0:T(8,128)(2,1)S(1)}, bf16[8,4864]{1,0:T(8,128)(2,1)S(1)}, u32[]{:S(2)}, u32[]{:S(2)}) collective-permute-start(bf16[8,4864]{1,0:T(8,128)(2,1)S(1)} %get-tuple-element.60), channel_id=1, source_target_pairs={{0,1},{1,0},{2,3},{3,2},{4,5},{5,4},{6,7},{7,6},{8,9},{9,8},{10,11... | collective-permute-start | bytes 233480 | tf_op jit(solution)/shard_map/ppermute | solution.py:265
  25.0 2.4 %collective-permute-start.17 = (bf16[8,4864]{1,0:T(8,128)(2,1)S(1)}, bf16[8,4864]{1,0:T(8,128)(2,1)S(1)}, u32[]{:S(2)}, u32[]{:S(2)}) collective-permute-start(bf16[8,4864]{1,0:T(8,128)(2,1)S(1)} %get-tuple-element.62), channel_id=1, source_target_pairs={{0,1},{1,0},{2,3},{3,2},{4,5},{5,4},{6,7},{7,6},{8,9},{9,8},{10,11... | collective-permute-start | bytes 233480 | tf_op jit(solution)/shard_map/ppermute | solution.py:265
  25.6 5.4 %collective-permute-start.14 = (bf16[8,4864]{1,0:T(8,128)(2,1)S(1)}, bf16[8,4864]{1,0:T(8,128)(2,1)S(1)}, u32[]{:S(2)}, u32[]{:S(2)}) collective-permute-start(bf16[8,4864]{1,0:T(8,128)(2,1)S(1)} %add_convert_fusion.6), channel_id=1, source_target_pairs={{0,6},{1,7},{2,4},{3,5},{4,2},{5,3},{6,0},{7,1},{8,14},{9,15},{10,... | collective-permute-start | bytes 233480 | tf_op jit(solution)/shard_map/ppermute | solution.py:265
  26.9 7.6 %collective-permute-start.19 = (bf16[8,4864]{1,0:T(8,128)(2,1)S(1)}, bf16[8,4864]{1,0:T(8,128)(2,1)S(1)}, u32[]{:S(2)}, u32[]{:S(2)}) collective-permute-start(bf16[8,4864]{1,0:T(8,128)(2,1)S(1)} %get-tuple-element.64), channel_id=1, source_target_pairs={{0,1},{1,0},{2,3},{3,2},{4,5},{5,4},{6,7},{7,6},{8,9},{9,8},{10,11... | collective-permute-start | bytes 233480 | tf_op jit(solution)/shard_map/ppermute | solution.py:265
  26.9 1.4 %collective-permute-start.22 = (bf16[8,4864]{1,0:T(8,128)(2,1)S(1)}, bf16[8,4864]{1,0:T(8,128)(2,1)S(1)}, u32[]{:S(2)}, u32[]{:S(2)}) collective-permute-start(bf16[8,4864]{1,0:T(8,128)(2,1)S(1)} %get-tuple-element.69), channel_id=1, source_target_pairs={{0,1},{1,0},{2,3},{3,2},{4,5},{5,4},{6,7},{7,6},{8,9},{9,8},{10,11... | collective-permute-start | bytes 233480 | tf_op jit(solution)/shard_map/ppermute | solution.py:265
  27.4 2.4 %collective-permute-start.24 = (bf16[8,4864]{1,0:T(8,128)(2,1)S(1)}, bf16[8,4864]{1,0:T(8,128)(2,1)S(1)}, u32[]{:S(2)}, u32[]{:S(2)}) collective-permute-start(bf16[8,4864]{1,0:T(8,128)(2,1)S(1)} %get-tuple-element.71), channel_id=1, source_target_pairs={{0,1},{1,0},{2,3},{3,2},{4,5},{5,4},{6,7},{7,6},{8,9},{9,8},{10,11... | collective-permute-start | bytes 233480 | tf_op jit(solution)/shard_map/ppermute | solution.py:265
  28.3 4.6 %collective-permute-start.16 = (bf16[8,4864]{1,0:T(8,128)(2,1)S(1)}, bf16[8,4864]{1,0:T(8,128)(2,1)S(1)}, u32[]{:S(2)}, u32[]{:S(2)}) collective-permute-start(bf16[8,4864]{1,0:T(8,128)(2,1)S(1)} %add_convert_fusion.5), channel_id=1, source_target_pairs={{0,4},{1,5},{2,6},{3,7},{4,0},{5,1},{6,2},{7,3},{8,12},{9,13},{10,... | collective-permute-start | bytes 233480 | tf_op jit(solution)/shard_map/ppermute | solution.py:265
  29.9 4.6 %collective-permute-start.18 = (bf16[8,4864]{1,0:T(8,128)(2,1)S(1)}, bf16[8,4864]{1,0:T(8,128)(2,1)S(1)}, u32[]{:S(2)}, u32[]{:S(2)}) collective-permute-start(bf16[8,4864]{1,0:T(8,128)(2,1)S(1)} %add_convert_fusion.4), channel_id=1, source_target_pairs={{0,2},{1,3},{2,0},{3,1},{4,6},{5,7},{6,4},{7,5},{8,10},{9,11},{10,... | collective-permute-start | bytes 233480 | tf_op jit(solution)/shard_map/ppermute | solution.py:265
  30.8 7.7 %collective-permute-start.21 = (bf16[8,4864]{1,0:T(8,128)(2,1)S(1)}, bf16[8,4864]{1,0:T(8,128)(2,1)S(1)}, u32[]{:S(2)}, u32[]{:S(2)}) collective-permute-start(bf16[8,4864]{1,0:T(8,128)(2,1)S(1)} %get-tuple-element.67), channel_id=1, source_target_pairs={{0,1},{1,0},{2,3},{3,2},{4,5},{5,4},{6,7},{7,6},{8,9},{9,8},{10,11... | collective-permute-start | bytes 233480 | tf_op jit(solution)/shard_map/ppermute | solution.py:265
  31.0 7.5 %collective-permute-start.23 = (bf16[8,4864]{1,0:T(8,128)(2,1)S(1)}, bf16[8,4864]{1,0:T(8,128)(2,1)S(1)}, u32[]{:S(2)}, u32[]{:S(2)}) collective-permute-start(bf16[8,4864]{1,0:T(8,128)(2,1)S(1)} %add_convert_fusion.1), channel_id=1, source_target_pairs={{0,6},{1,7},{2,4},{3,5},{4,2},{5,3},{6,0},{7,1},{8,14},{9,15},{10,... | collective-permute-start | bytes 233480 | tf_op jit(solution)/shard_map/ppermute | solution.py:265
  32.9 5.8 %collective-permute-start.25 = (bf16[8,4864]{1,0:T(8,128)(2,1)S(1)}, bf16[8,4864]{1,0:T(8,128)(2,1)S(1)}, u32[]{:S(2)}, u32[]{:S(2)}) collective-permute-start(bf16[8,4864]{1,0:T(8,128)(2,1)S(1)} %add_convert_fusion), channel_id=1, source_target_pairs={{0,4},{1,5},{2,6},{3,7},{4,0},{5,1},{6,2},{7,3},{8,12},{9,13},{10,... | collective-permute-start | bytes 233480 | tf_op jit(solution)/shard_map/ppermute | solution.py:265
  34.5 6.1 %collective-permute-start.20 = (bf16[8,4864]{1,0:T(8,128)(2,1)S(1)}, bf16[8,4864]{1,0:T(8,128)(2,1)S(1)}, u32[]{:S(2)}, u32[]{:S(2)}) collective-permute-start(bf16[8,4864]{1,0:T(8,128)(2,1)S(1)} %add_convert_fusion.3), channel_id=1, source_target_pairs={{0,8},{1,9},{2,10},{3,11},{4,12},{5,13},{6,14},{7,15},{8,0},{9,1},... | collective-permute-start | bytes 233480 | tf_op jit(solution)/shard_map/ppermute | solution.py:265
  37.0 4.4 %collective-permute-start.26 = (bf16[8,4864]{1,0:T(8,128)(2,1)S(1)}, bf16[8,4864]{1,0:T(8,128)(2,1)S(1)}, u32[]{:S(2)}, u32[]{:S(2)}) collective-permute-start(bf16[8,4864]{1,0:T(8,128)(2,1)S(1)} %add_convert_fusion.2), channel_id=1, source_target_pairs={{0,2},{1,3},{2,0},{3,1},{4,6},{5,7},{6,4},{7,5},{8,10},{9,11},{10,... | collective-permute-start | bytes 233480 | tf_op jit(solution)/shard_map/ppermute | solution.py:265
